TPU v7x, 32 devices: a whole 2x2x4 slice. The times are simulated.
32 devices in a mesh: batch: 8 (over z, core), expert: 4 (over y, x).
Axes of the slice: x: 2, y: 2, z: 4, core: 2. Of those that a mesh axis runs over, the one named last changes fastest.
Arguments:
- tokens: bfloat16 [8, 1024, 1536], P('batch', 'expert'), may hold values from -6 to 6
- cotangent: bfloat16 [8, 1024, 1536], P('batch', 'expert'), may hold values from -6 to 6
- attn_gain: bfloat16 [1536], P(('batch', 'expert')), may hold values from 0.5 to 1.5
- query_weight: bfloat16 [1536, 1536], P(('batch', 'expert')), may hold values from -0.15625 to 0.15625
- key_weight: bfloat16 [1536, 512], P(('batch', 'expert')), may hold values from -0.15625 to 0.15625
- value_weight: bfloat16 [1536, 512], P(('batch', 'expert')), may hold values from -0.15625 to 0.15625
- out_weight: bfloat16 [1536, 1536], P(('batch', 'expert')), may hold values from -1 to 1
- ffn_gain: bfloat16 [1536], P(('batch', 'expert')), may hold values from 0.5 to 1.5
- router_weight: bfloat16 [1536, 20], P(('batch', 'expert')), may hold values from -0.078125 to 0.078125
- gate_weight: bfloat16 [20, 1536, 512], P('expert', 'batch'), may hold values from -0.15625 to 0.15625
- up_weight: bfloat16 [20, 1536, 512], P('expert', 'batch'), may hold values from -0.15625 to 0.15625
- down_weight: bfloat16 [20, 512, 1536], P('expert', 'batch'), may hold values from -1 to 1
- routes: int32 [8, 1024, 8], P('batch', 'expert'), may hold values from 0 to 19, all different within a row
- ranking: int32 [8, 1024], P('batch', 'expert'), may hold values from 0 to 1023, each once within a row
Outputs:
- layer_out: bfloat16 [8, 1024, 1536], P('batch', 'expert')
- input_grad: float32 [8, 1024, 1536], P('batch', 'expert')
- attn_gain_grad: float32 [1536], P(('batch', 'expert'))
- query_grad: float32 [1536, 1536], P(('batch', 'expert'))
- key_grad: float32 [1536, 512], P(('batch', 'expert'))
- value_grad: float32 [1536, 512], P(('batch', 'expert'))
- out_proj_grad: float32 [1536, 1536], P(('batch', 'expert'))
- ffn_gain_grad: float32 [1536], P(('batch', 'expert'))
- router_grad: float32 [1536, 20], P(('batch', 'expert'))
- gate_proj_grad: float32 [20, 1536, 512], P('expert', 'batch')
- up_proj_grad: float32 [20, 1536, 512], P('expert', 'batch')
- down_proj_grad: float32 [20, 512, 1536], P('expert', 'batch')
Inputs may be any that keep to these rules, and one draw needn't show every extreme that they name: `routes`: each token names 8 different experts, and every expert is named by some token. `ranking`: within each group a permutation of the rows.
All inputs are finite; a program needn't handle non-finite values.
Results may differ from a plain program's by a relative error of at most 0.02.
Values may be sent and summed in bfloat16 or wider, within the bound.
No kernel may reach another device: no remote copies, remote signals or barrier semaphores. Data moves between devices by JAX's collectives and lax.ppermute only.
A program may use at most 256 MiB of HBM per device.

v0:
```python
from functools import partial

import jax
import jax.numpy as jnp
from jax import lax
from jax.experimental import pallas as pl
from jax.experimental.pallas import tpu as pltpu
from jax.sharding import PartitionSpec as P

HEADS = 24
KV_HEADS = 8
HEAD_DIM = 64
PROMPT = 512
CLEN = 256


EPS = 1e-06
THETA = 10000.0


def product(left, right):
    return jnp.dot(left, right, preferred_element_type=jnp.float32)


def place_of(row_ids):
    return jnp.where(row_ids < PROMPT, row_ids, PROMPT + (row_ids - PROMPT) % CLEN)


def visible(query_ids, key_ids):
    causal = key_ids[None, :] <= query_ids[:, None]
    same_run = (key_ids[None, :] - PROMPT) // CLEN == (query_ids[:, None] - PROMPT) // CLEN
    return causal & ((key_ids[None, :] < PROMPT) | same_run)


def dot_plain(left, right):
    return lax.dot_general(left, right, (((1,), (0,)), ((), ())), preferred_element_type=jnp.float32)


def dot_right(left, right):
    return lax.dot_general(left, right, (((1,), (1,)), ((), ())), preferred_element_type=jnp.float32)


def dot_left(left, right):
    return lax.dot_general(left, right, (((0,), (0,)), ((), ())), preferred_element_type=jnp.float32)


ANYWHERE = pl.BlockSpec(memory_space=pl.ANY)
INSIDE = pl.BlockSpec(memory_space=pltpu.VMEM)
SCALARS = pl.BlockSpec(memory_space=pltpu.SMEM)
VMEM_BYTES = 62 * 1024 * 1024


def cost(flops, *arrays):
    return pl.CostEstimate(flops=1, bytes_accessed=1, transcendentals=0)


def weight_copies(spots, pieces, target, sems):
    copies = []
    for p, piece in enumerate(pieces):
        blocks, rows = piece.shape[0], piece.shape[1]
        for k in range(blocks):
            place = pl.multiple_of(spots[p, k] * rows, rows)
            copies.append(
                pltpu.make_async_copy(
                    piece.at[k], target.at[pl.ds(place, rows)], sems.at[p * blocks + k]
                )
            )
    return copies


def block_copies(blocks, target, sems, first, columns=None):
    copies = []
    start = 0
    for i, block in enumerate(blocks):
        rows = block.shape[0]
        source = block if columns is None else block.at[:, columns]
        copies.append(
            pltpu.make_async_copy(source, target.at[pl.ds(start, rows)], sems.at[first + i])
        )
        start += rows
    return copies


def swap_halves(values):
    half = HEAD_DIM // 2
    lane = lax.broadcasted_iota(jnp.int32, values.shape, 1)
    return jnp.where(
        lane % HEAD_DIM < half,
        pltpu.roll(values, 2 * HEAD_DIM - half, 1),
        pltpu.roll(values, half, 1),
    )


def mean_square_scale(values):
    return lax.rsqrt(jnp.mean(values * values, axis=-1, keepdims=True) + EPS)


def enter_kernel(count, gain_at, spots, tokens, cosine, sine, *refs):
    pieces = refs[:count]
    normed, query, keyval, small, weight, sems = refs[count:]
    low = jnp.bfloat16
    copies = weight_copies(spots, pieces, weight, sems)
    for copy in copies:
        copy.start()
    inputs = tokens[...].astype(jnp.float32)
    scaled = inputs * mean_square_scale(inputs)
    for copy in copies:
        copy.wait()
    query_width = query.shape[1]
    kv_width = keyval.shape[1] // 2
    qkv_width = query_width + 2 * kv_width
    turned = weight[:, qkv_width:].astype(jnp.float32).T
    small[...] = turned
    rows = (scaled * turned[gain_at : gain_at + 1]).astype(low)
    normed[...] = rows
    pair = 2 * HEAD_DIM
    scale = HEAD_DIM**-0.5
    for start in range(0, query_width + kv_width, 512):
        product_part = dot_plain(rows, weight[:, start : start + 512])
        for offset in range(0, 512, pair):
            part = product_part[:, offset : offset + pair]
            part = part * cosine[...] + swap_halves(part) * sine[...]
            at = start + offset
            if at < query_width:
                query[:, at : at + pair] = (part * scale).astype(low)
            else:
                keyval[:, at - query_width : at - query_width + pair] = part.astype(low)
    keyval[:, kv_width:] = dot_plain(
        rows, weight[:, query_width + kv_width : qkv_width]
    ).astype(low)


def enter(tokens, cosine, sine, pieces, spots, gain_at, query_width, kv_width):
    rows, width = tokens.shape
    columns = pieces[0].shape[2]
    low = jnp.bfloat16
    return pl.pallas_call(
        partial(enter_kernel, len(pieces), gain_at),
        in_specs=[SCALARS, INSIDE, INSIDE, INSIDE] + [ANYWHERE] * len(pieces),
        out_specs=[INSIDE] * 4,
        out_shape=[
            jax.ShapeDtypeStruct((rows, width), low),
            jax.ShapeDtypeStruct((rows, query_width), low),
            jax.ShapeDtypeStruct((rows, 2 * kv_width), low),
            jax.ShapeDtypeStruct((columns - query_width - 2 * kv_width, width), jnp.float32),
        ],
        scratch_shapes=[
            pltpu.VMEM((width, columns), low),
            pltpu.SemaphoreType.DMA((len(pieces) * pieces[0].shape[0],)),
        ],
        compiler_params=pltpu.CompilerParams(vmem_limit_bytes=VMEM_BYTES),
        cost_estimate=cost(2 * rows * width * columns, *pieces),
        name="enter",
    )(spots, tokens, cosine, sine, *pieces)


def both_places(values):
    wide = values.astype(jnp.float32)
    low_lane = lax.broadcasted_iota(jnp.int32, values.shape, 1) < HEAD_DIM
    moved = pltpu.roll(wide, HEAD_DIM, 1)
    kind = values.dtype
    return [
        [jnp.where(low_lane, wide, 0.0).astype(kind), jnp.where(low_lane, 0.0, moved).astype(kind)],
        [jnp.where(low_lane, moved, 0.0).astype(kind), jnp.where(low_lane, 0.0, wide).astype(kind)],
    ]


def attend_kernel(
    count, query, keyval, bias, tokens, small, member, kept, gain_at, spots, *refs
):
    pieces = refs[:count]
    attended, log_totals, residual, sent, gate_rows, weight, sems = refs[count:]
    low = jnp.bfloat16
    rows = query.shape[0]
    width = tokens.shape[1]
    kv_width = keyval.shape[1] // 2
    pair_lanes = 2 * HEAD_DIM
    repeat = HEADS // KV_HEADS
    copies = weight_copies(spots, pieces, weight, sems)
    for copy in copies:
        copy.start()
    log_totals[...] = jnp.zeros_like(log_totals)
    lane = lax.broadcasted_iota(jnp.int32, log_totals.shape, 1)

    @pl.loop(0, KV_HEADS // 2)
    def _(pair):
        at = pl.ds(pl.multiple_of(pair * pair_lanes, pair_lanes), pair_lanes)
        keys = both_places(keyval[:, at])
        at = pl.ds(pl.multiple_of(kv_width + pair * pair_lanes, pair_lanes), pair_lanes)
        values = both_places(keyval[:, at])
        for i in range(repeat):
            at = pl.ds(pl.multiple_of((pair * repeat + i) * pair_lanes, pair_lanes), pair_lanes)
            queries = query[:, at]
            total = jnp.zeros((rows, pair_lanes), jnp.float32)
            for a in range(2):
                head = 2 * i + a
                scores = dot_right(queries, keys[head // repeat][a]) + bias[...]
                peak = jnp.max(scores, axis=-1, keepdims=True)
                lifted = jnp.exp(scores - peak)
                row_total = jnp.sum(lifted, axis=-1, keepdims=True)
                weights_low = (lifted * (1.0 / row_total)).astype(low)
                total += dot_plain(weights_low, values[head // repeat][a])
                log_totals[...] = jnp.where(
                    lane == pair * (2 * repeat) + head, peak + jnp.log(row_total), log_totals[...]
                )
            attended[:, at] = total.astype(low)

    for copy in copies:
        copy.wait()
    hidden = tokens[...].astype(jnp.float32) + dot_plain(attended[...], weight[...])
    residual[...] = hidden
    gain = small[gain_at : gain_at + 1, :]
    normed = (hidden * mean_square_scale(hidden) * gain).astype(low)
    logits = dot_right(normed, small[...].astype(low))
    chosen = member[...] > 0.0
    logits = jnp.where(chosen, logits, -1e30)
    lifted = jnp.where(chosen, jnp.exp(logits - jnp.max(logits, axis=-1, keepdims=True)), 0.0)
    gates = lifted / jnp.sum(lifted, axis=-1, keepdims=True)
    gate_rows[...] = gates
    sent[:, :width] = normed
    sent[:, width:] = (gates * kept[...]).astype(low)


def attend(query, keyval, bias, tokens, small, member, kept, gain_at, pieces, spots):
    rows, width = tokens.shape
    query_width = query.shape[1]
    lanes = small.shape[0]
    low = jnp.bfloat16

    def kernel(*refs):
        attend_kernel(len(pieces), *refs[:7], gain_at, *refs[7:])

    return pl.pallas_call(
        kernel,
        in_specs=[INSIDE] * 7 + [SCALARS] + [ANYWHERE] * len(pieces),
        out_specs=[INSIDE] * 5,
        out_shape=[
            jax.ShapeDtypeStruct((rows, query_width), low),
            jax.ShapeDtypeStruct((rows, 128), jnp.float32),
            jax.ShapeDtypeStruct((rows, width), jnp.float32),
            jax.ShapeDtypeStruct((rows, width + lanes), low),
            jax.ShapeDtypeStruct((rows, lanes), jnp.float32),
        ],
        scratch_shapes=[
            pltpu.VMEM((query_width, width), low),
            pltpu.SemaphoreType.DMA((len(pieces) * pieces[0].shape[0],)),
        ],
        compiler_params=pltpu.CompilerParams(vmem_limit_bytes=VMEM_BYTES),
        cost_estimate=cost(2 * rows * width * width + 8 * rows * query_width * bias.shape[1], *pieces),
        name="attend",
    )(query, keyval, bias, tokens, small, member, kept, spots, *pieces)


def grad_shapes(cut, rows, columns):
    low = jnp.bfloat16
    if cut:
        block = rows // 32
        return (
            [jax.ShapeDtypeStruct((4, 4, block, columns), low)] * 2,
            pltpu.VMEM((4, 2, 4, block, columns), low),
        )
    return (
        [jax.ShapeDtypeStruct((1, 1, 1, rows, columns), low)],
        pltpu.VMEM((1, 1, 1, rows, columns), low),
    )


def grad_copies(cut, place, source, outs, sems):
    if not cut:
        return [pltpu.make_async_copy(source, outs[0], sems.at[0])]
    core, member = place[0], place[1]
    other, own = outs
    copies = []
    for r in range(4):
        copies.append(
            pltpu.make_async_copy(
                source.at[:, 1 - core, member ^ r], other.at[r], sems.at[2 * r]
            )
        )
        copies.append(
            pltpu.make_async_copy(source.at[:, core, member ^ r], own.at[r], sems.at[2 * r + 1])
        )
    return copies


def turn_kernel(
    count,
    cut,
    gain_at,
    place,
    spots,
    normed_grad,
    residual,
    grad_out,
    small,
    gate_rows,
    member,
    kept,
    normed,
    attended,
    *refs,
):
    pieces = refs[:count]
    refs = refs[count:]
    outs = refs[: (2 if cut else 1)]
    resid_grad, head_grad, weight, weight_grad, sems, out_sems = refs[len(outs) :]
    low = jnp.bfloat16
    rows, width = residual.shape
    lanes = gate_rows.shape[1]
    copies = weight_copies(spots, pieces, weight, sems)
    for copy in copies:
        copy.start()
    lane = lax.broadcasted_iota(jnp.int32, (rows, lanes), 1)
    gates = gate_rows[...]
    gate_grads = normed_grad[:, width:] * kept[...]
    chosen_grad = gates * (gate_grads - jnp.sum(gates * gate_grads, axis=-1, keepdims=True))
    logit_grad = (chosen_grad * member[...]).astype(low)
    hidden = residual[...]
    scale = mean_square_scale(hidden)
    row_grad = normed_grad[:, :width] + dot_plain(logit_grad, small[...].astype(low))
    gain = small[gain_at : gain_at + 1, :]
    scaled = row_grad * gain
    total_grad = (
        grad_out[...].astype(jnp.float32)
        + scale * scaled
        - hidden * (scale * scale * scale) * jnp.mean(scaled * hidden, axis=-1, keepdims=True)
    )
    resid_grad[...] = total_grad
    attn_grad = total_grad.astype(low)
    shape = weight_grad.shape[:-1]
    gain_grad = (row_grad * hidden * scale).astype(low)
    picks = jnp.where(lane == gain_at, 1.0, 0.0).astype(low)
    weight_grad[..., width:] = (
        (dot_left(normed[...][:, :width], logit_grad) + dot_left(gain_grad, picks))
        .astype(low)
        .reshape(shape + (lanes,))
    )
    for start in range(0, width, 512):
        weight_grad[..., start : start + 512] = (
            dot_left(attended[...], attn_grad[:, start : start + 512])
            .astype(low)
            .reshape(shape + (512,))
        )
    out_copies = grad_copies(cut, place, weight_grad, outs, out_sems)
    for copy in out_copies:
        copy.start()
    for copy in copies:
        copy.wait()
    head_grad[...] = dot_right(attn_grad, weight[...]).astype(low)
    for copy in out_copies:
        copy.wait()


def turn(place, spots, operands, pieces, cut, gain_at):
    residual, gate_rows, attended = operands[1], operands[4], operands[8]
    rows, width = residual.shape
    query_width = attended.shape[1]
    low = jnp.bfloat16
    grads, held = grad_shapes(cut, query_width, width + gate_rows.shape[1])
    return pl.pallas_call(
        partial(turn_kernel, len(pieces), cut, gain_at),
        in_specs=[SCALARS, SCALARS] + [INSIDE] * len(operands) + [ANYWHERE] * len(pieces),
        out_specs=[ANYWHERE] * len(grads) + [INSIDE] * 2,
        out_shape=grads
        + [
            jax.ShapeDtypeStruct((rows, width), jnp.float32),
            jax.ShapeDtypeStruct((rows, query_width), low),
        ],
        scratch_shapes=[
            pltpu.VMEM((query_width, width), low),
            held,
            pltpu.SemaphoreType.DMA((len(pieces) * pieces[0].shape[0],)),
            pltpu.SemaphoreType.DMA((8,)),
        ],
        compiler_params=pltpu.CompilerParams(vmem_limit_bytes=VMEM_BYTES),
        cost_estimate=cost(0),
        name="turn",
    )(place, spots, *operands, *pieces)


def attend_back_kernel(
    head_grad, query, keyval, bias, log_totals, cosine, sine, query_grad, keyval_grad, totals
):
    low = jnp.bfloat16
    rows = query.shape[0]
    kv_width = keyval.shape[1] // 2
    pair_lanes = 2 * HEAD_DIM
    repeat = HEADS // KV_HEADS
    totals[...] = log_totals[...].T

    @pl.loop(0, KV_HEADS // 2)
    def _(pair):
        key_at = pl.ds(pl.multiple_of(pair * pair_lanes, pair_lanes), pair_lanes)
        value_at = pl.ds(pl.multiple_of(kv_width + pair * pair_lanes, pair_lanes), pair_lanes)
        keys = both_places(keyval[:, key_at])
        values = both_places(keyval[:, value_at])
        key_grads = [[None, None], [None, None]]
        value_grads = [[None, None], [None, None]]
        for i in range(repeat):
            at = pl.ds(pl.multiple_of((pair * repeat + i) * pair_lanes, pair_lanes), pair_lanes)
            queries = query[:, at]
            grads = head_grad[:, at]
            query_part = jnp.zeros((rows, pair_lanes), jnp.float32)
            for a in range(2):
                head = 2 * i + a
                g = head // repeat
                total = totals[pl.ds(pair * (2 * repeat) + head, 1), :]
                weights = jnp.exp(dot_right(keys[g][a], queries) + bias[...] - total)
                weight_grads = dot_right(values[g][a], grads)
                delta = jnp.sum(weights * weight_grads, axis=0, keepdims=True)
                score_grads = (weights * (weight_grads - delta)).astype(low)
                value_part = dot_plain(weights.astype(low), grads)
                key_part = dot_plain(score_grads, queries)
                query_part += dot_left(score_grads, keys[g][a])
                if key_grads[g][a] is None:
                    key_grads[g][a], value_grads[g][a] = key_part, value_part
                else:
                    key_grads[g][a] += key_part
                    value_grads[g][a] += value_part
            query_part = query_part * (HEAD_DIM**-0.5)
            query_part = query_part * cosine[...] - swap_halves(query_part) * sine[...]
            query_grad[:, at] = query_part.astype(low)
        low_lane = lax.broadcasted_iota(jnp.int32, (keyval.shape[0], pair_lanes), 1) < HEAD_DIM
        for at, found in ((key_at, key_grads), (value_at, value_grads)):
            keyval_grad[:, at] = jnp.where(
                low_lane,
                found[0][0] + pltpu.roll(found[0][1], HEAD_DIM, 1),
                pltpu.roll(found[1][0], HEAD_DIM, 1) + found[1][1],
            ).astype(low)


def attend_back(head_grad, query, keyval, bias, log_totals, cosine, sine):
    rows, query_width = query.shape
    low = jnp.bfloat16
    return pl.pallas_call(
        attend_back_kernel,
        in_specs=[INSIDE] * 7,
        out_specs=[INSIDE] * 2,
        out_shape=[
            jax.ShapeDtypeStruct((rows, query_width), low),
            jax.ShapeDtypeStruct(keyval.shape, low),
        ],
        scratch_shapes=[pltpu.VMEM((128, rows), jnp.float32)],
        compiler_params=pltpu.CompilerParams(vmem_limit_bytes=VMEM_BYTES),
        cost_estimate=cost(0),
        name="attend_back",
    )(head_grad, query, keyval, bias, log_totals, cosine, sine)


def leave_kernel(
    count,
    cut,
    gain_at,
    place,
    spots,
    keyval_sum,
    query_grad,
    normed,
    tokens,
    resid_grad,
    small,
    cosine,
    sine,
    *refs,
):
    pieces = refs[:count]
    refs = refs[count:]
    outs = refs[: (2 if cut else 1)]
    input_grad, weight, weight_grad, joined, sems, out_sems = refs[len(outs) :]
    low = jnp.bfloat16
    rows, width = tokens.shape
    query_width = query_grad.shape[1]
    kv_width = keyval_sum.shape[1] // 2
    qkv_width = query_width + 2 * kv_width
    pair = 2 * HEAD_DIM
    copies = weight_copies(spots, pieces, weight, sems)
    for copy in copies:
        copy.start()
    joined[:, :query_width] = query_grad[...]
    for start in range(0, kv_width, pair):
        part = keyval_sum[:, start : start + pair]
        part = part * cosine[...] - swap_halves(part) * sine[...]
        joined[:, query_width + start : query_width + start + pair] = part.astype(low)
    joined[:, query_width + kv_width :] = keyval_sum[:, kv_width:].astype(low)
    shape = weight_grad.shape[:-1]
    for start in range(0, qkv_width, 512):
        weight_grad[..., start : start + 512] = (
            dot_left(normed[...], joined[:, start : start + 512]).astype(low).reshape(shape + (512,))
        )
    for copy in copies:
        copy.wait()
    row_grad = dot_right(joined[...], weight[:, :qkv_width])
    inputs = tokens[...].astype(jnp.float32)
    scale = mean_square_scale(inputs)
    lanes = weight_grad.shape[-1] - qkv_width
    lane = lax.broadcasted_iota(jnp.int32, (rows, lanes), 1)
    picks = jnp.where(lane == gain_at, 1.0, 0.0).astype(low)
    weight_grad[..., qkv_width:] = (
        dot_left((row_grad * inputs * scale).astype(low), picks).astype(low).reshape(shape + (lanes,))
    )
    out_copies = grad_copies(cut, place, weight_grad, outs, out_sems)
    for copy in out_copies:
        copy.start()
    scaled = row_grad * small[gain_at : gain_at + 1, :]
    input_grad[...] = (
        resid_grad[...]
        + scale * scaled
        - inputs * (scale * scale * scale) * jnp.mean(scaled * inputs, axis=-1, keepdims=True)
    )
    for copy in out_copies:
        copy.wait()


def leave(place, spots, operands, pieces, cut, gain_at):
    tokens, query_grad, keyval_sum = operands[3], operands[1], operands[0]
    rows, width = tokens.shape
    columns = pieces[0].shape[2]
    low = jnp.bfloat16
    grads, held = grad_shapes(cut, width, columns)
    return pl.pallas_call(
        partial(leave_kernel, len(pieces), cut, gain_at),
        in_specs=[SCALARS, SCALARS] + [INSIDE] * len(operands) + [ANYWHERE] * len(pieces),
        out_specs=[ANYWHERE] * len(grads) + [INSIDE],
        out_shape=grads + [jax.ShapeDtypeStruct((rows, width), jnp.float32)],
        scratch_shapes=[
            pltpu.VMEM((width, columns), low),
            held,
            pltpu.VMEM((rows, query_grad.shape[1] + keyval_sum.shape[1]), low),
            pltpu.SemaphoreType.DMA((len(pieces) * pieces[0].shape[0],)),
            pltpu.SemaphoreType.DMA((8,)),
        ],
        compiler_params=pltpu.CompilerParams(vmem_limit_bytes=VMEM_BYTES),
        cost_estimate=cost(0),
        name="leave",
    )(place, spots, *operands, *pieces)


def expert_kernel(cut, carried, last, row_blocks, grad_blocks, row_tile, place, first, packed, *refs):
    blocks_in = refs[:row_blocks]
    grads_in = refs[row_blocks : row_blocks + grad_blocks]
    refs = refs[row_blocks + grad_blocks :]
    if carried:
        mix_in, turn_in = refs[:2]
        refs = refs[2:]
    count = packed.shape[2]
    outs = 4 if cut else 1
    packed_grads = refs[:outs]
    mix_out, turn_out = refs[outs : outs + 2]
    refs = refs[outs + 2 :]
    if last:
        mix, turned = refs[:2]
        refs = refs[2:]
    else:
        mix, turned = mix_out, turn_out
    (
        rows,
        grads,
        gates,
        gate_w,
        up_w,
        down_w,
        gate_g,
        up_g,
        down_g,
        weighted,
        gate_side,
        up_side,
        load_sems,
        save_sems,
        carry_sems,
    ) = refs
    hidden_width = gate_w.shape[-1]
    total_rows, width = rows.shape
    lanes = gates.shape[1]
    low = jnp.bfloat16

    def sides(gate, up, down):
        for side, inner in ((0, gate), (1, up)):
            for j in range(3):
                yield side, pl.ds(j * hidden_width, hidden_width), inner, j
        yield 2, pl.ds(0, width), down, None

    def loads(e):
        slot = e % 2
        copies = []
        for i, (side, columns, inner, j) in enumerate(sides(gate_w, up_w, down_w)):
            outer = packed.at[:, side, e, :, columns]
            inner = inner.at[slot] if j is None else inner.at[slot, :, j]
            copies.append(pltpu.make_async_copy(outer, inner, load_sems.at[slot, i]))
        return copies

    def saves(e):
        slot = e % 2
        copies = []
        for i, (side, columns, inner, j) in enumerate(sides(gate_g, up_g, down_g)):
            if not cut:
                outer = packed_grads[0].at[:, side, e, :, columns]
                source = inner.at[slot] if j is None else inner.at[slot, :, j]
                copies.append(pltpu.make_async_copy(source, outer, save_sems.at[slot, i]))
                continue
            own, rest, far, near = packed_grads
            targets = [own, rest.at[0], rest.at[1], rest.at[2]]
            targets += [near.at[1], near.at[0], far.at[0], far.at[1]]
            for n, target in enumerate(targets):
                block = 2 * lax.rem(place[2] + n % 4, 4) + (place[0] ^ (n // 4))
                source = inner.at[slot, block] if j is None else inner.at[slot, block, j]
                outer = target.at[side, e, :, columns]
                copies.append(pltpu.make_async_copy(source, outer, save_sems.at[slot, 8 * i + n]))
        return copies

    carries = (
        block_copies(grads_in, grads, carry_sems, 0, pl.ds(0, width))
        + block_copies(blocks_in, rows, carry_sems, grad_blocks, pl.ds(0, width))
        + block_copies(
            blocks_in, gates, carry_sems, grad_blocks + row_blocks, pl.ds(width, lanes)
        )
    )
    sums = []
    if carried:
        at = grad_blocks + 2 * row_blocks
        sums = [
            pltpu.make_async_copy(mix_in, mix, carry_sems.at[at]),
            pltpu.make_async_copy(turn_in, turned, carry_sems.at[at + 1]),
        ]
    for copy in loads(0) + carries + sums:
        copy.start()
    for e in range(count):
        slot = e % 2
        if e + 1 < count:
            for copy in loads(e + 1):
                copy.start()
        for copy in loads(e):
            copy.wait()
        if e == 0:
            for copy in carries:
                copy.wait()
            if not carried:
                turned[:, width:] = jnp.zeros((total_rows, lanes), jnp.float32)

        @pl.loop(0, total_rows // row_tile)
        def _(tile):
            span = pl.ds(pl.multiple_of(tile * row_tile, row_tile), row_tile)
            gate_full = gate_w[slot].reshape(width, hidden_width)
            up_full = up_w[slot].reshape(width, hidden_width)
            down_full = down_w[slot].reshape(hidden_width, width)
            here = rows[span, :]
            slope = dot_right(grads[span, :], down_full)
            gate_pre = dot_plain(here, gate_full)
            up_pre = dot_plain(here, up_full)
            lane = lax.broadcasted_iota(jnp.int32, (row_tile, lanes), 1)
            chosen = lane == first[0] + e
            gate_column = jnp.sum(
                jnp.where(chosen, gates[span, :].astype(jnp.float32), 0.0), axis=1, keepdims=True
            )
            sigmoid_gate = jax.nn.sigmoid(gate_pre)
            activated = gate_pre * sigmoid_gate
            hidden = (activated * up_pre).astype(low).astype(jnp.float32)
            share = jnp.sum(hidden * slope, axis=1, keepdims=True)
            if e == 0 and sums:

                @pl.when(tile == 0)
                def _():
                    for copy in sums:
                        copy.wait()

            turned[span, width:] = jnp.where(chosen, share, turned[span, width:])
            part_weighted = (hidden * gate_column).astype(low)
            hidden_grad = slope * gate_column
            part_gate = (
                hidden_grad * up_pre * (sigmoid_gate + activated * (1.0 - sigmoid_gate))
            ).astype(low)
            part_up = (hidden_grad * activated).astype(low)
            weighted[span, :] = part_weighted
            gate_side[span, :] = part_gate
            up_side[span, :] = part_up
            mix_part = dot_plain(part_weighted, down_full)
            turn_part = dot_right(part_gate, gate_full) + dot_right(part_up, up_full)
            if e == 0 and not carried:
                mix[span, :] = mix_part
                turned[span, :width] = turn_part
            elif last and e == count - 1:
                mix_out[span, :] = (mix[span, :] + mix_part).astype(low)
                turn_out[span, :width] = (turned[span, :width] + turn_part).astype(low)
                turn_out[span, width:] = turned[span, width:].astype(low)
            else:
                mix[span, :] += mix_part
                turned[span, :width] += turn_part

        if e >= 2:
            for copy in saves(e - 2):
                copy.wait()
        down_g[slot] = dot_left(weighted[...], grads[...]).astype(low).reshape(down_g.shape[1:])
        gate_g[slot] = dot_left(rows[...], gate_side[...]).astype(low).reshape(gate_g.shape[1:])
        up_g[slot] = dot_left(rows[...], up_side[...]).astype(low).reshape(up_g.shape[1:])
        for copy in saves(e):
            copy.start()
    for e in range(max(0, count - 2), count):
        for copy in saves(e):
            copy.wait()


def expert_pass(place, first, rows, grads, packed, carry, cut, last):
    blocks, _, count, part, width = packed.shape
    hidden_width = blocks * part
    total_rows = sum(block.shape[0] for block in rows)
    lanes = rows[0].shape[1] - width
    low = jnp.bfloat16
    wide = jnp.float32
    carried = carry is not None
    flops = 18 * total_rows * count * hidden_width * width
    side = pltpu.VMEM((2, blocks, 3, part, hidden_width), low)
    sides = [side, side, pltpu.VMEM((2, blocks, part, width), low)]
    sums = [(total_rows, width), (total_rows, width + lanes)]
    one = packed.shape[1:]
    grads_out = [one, (3,) + one, (2,) + one, (2,) + one] if cut else [packed.shape]
    outs = len(grads_out)
    found = pl.pallas_call(
        partial(expert_kernel, cut, carried, last, len(rows), len(grads), min(512, total_rows)),
        in_specs=[SCALARS, SCALARS]
        + [ANYWHERE] * (1 + len(rows) + len(grads) + (2 if carried else 0)),
        out_specs=[ANYWHERE] * outs + [INSIDE, INSIDE],
        out_shape=[jax.ShapeDtypeStruct(shape, low) for shape in grads_out]
        + [jax.ShapeDtypeStruct(shape, low if last else wide) for shape in sums],
        scratch_shapes=([pltpu.VMEM(shape, wide) for shape in sums] if last else [])
        + [
            pltpu.VMEM((total_rows, width), low),
            pltpu.VMEM((total_rows, width), low),
            pltpu.VMEM((total_rows, lanes), low),
        ]
        + sides
        + sides
        + [pltpu.VMEM((total_rows, hidden_width), low)] * 3
        + [
            pltpu.SemaphoreType.DMA((2, 7)),
            pltpu.SemaphoreType.DMA((2, 56)),
            pltpu.SemaphoreType.DMA((2 * len(rows) + len(grads) + 2,)),
        ],
        compiler_params=pltpu.CompilerParams(vmem_limit_bytes=VMEM_BYTES),
        cost_estimate=cost(flops, packed, packed, *rows, *grads),
        name="experts",
    )(place, first, packed, *rows, *grads, *(carry or ()))
    return found[:outs], found[outs], found[outs + 1]


def unpack_kernel(counts, *refs):
    found, (gate, up, down) = refs[:-3], refs[-3:]
    hidden_width = gate.shape[2]
    base = 0
    at = 0
    for terms in counts:
        parts = found[at : at + terms]
        at += terms
        count, part = parts[0].shape[1], parts[0].shape[2]
        for e in range(count):
            for side in range(3):
                total = parts[0][side, e].astype(jnp.float32)
                for other in parts[1:]:
                    total += other[side, e].astype(jnp.float32)
                if side == 2:
                    down[base + e] = total
                    continue
                for j in range(3):
                    (gate, up)[side][base + e, j * part : (j + 1) * part, :] = total[
                        :, j * hidden_width : (j + 1) * hidden_width
                    ]
        base += count


def unpack(chunks, gate_shape, down_shape):
    arrays = [term for terms in chunks for term in terms]
    return pl.pallas_call(
        partial(unpack_kernel, [len(terms) for terms in chunks]),
        in_specs=[INSIDE] * len(arrays),
        out_specs=[INSIDE] * 3,
        out_shape=[
            jax.ShapeDtypeStruct(gate_shape, jnp.float32),
            jax.ShapeDtypeStruct(gate_shape, jnp.float32),
            jax.ShapeDtypeStruct(down_shape, jnp.float32),
        ],
        compiler_params=pltpu.CompilerParams(vmem_limit_bytes=VMEM_BYTES),
        cost_estimate=cost(0),
        name="unpack",
    )(*arrays)


def cube():
    return lax.axis_size("batch") == 8 and lax.axis_size("expert") == 4


def pair_moves(size, flip):
    return [(i, i ^ flip) for i in range(size)]


def shift_moves(step):
    return [(2 * z + c, 2 * ((z + step) % 4) + c) for z in range(4) for c in range(2)]


def gather_blocks(rows, at_once=False):
    size = lax.axis_size("expert")
    if size != 4:
        stacked = lax.all_gather(rows, "expert", axis=0)
        own = lax.axis_index("expert")
        return [
            lax.dynamic_index_in_dim(stacked, own ^ r, axis=0, keepdims=False) for r in range(size)
        ]
    across, along = pair_moves(size, 1), pair_moves(size, 2)
    if at_once:
        return [rows] + [lax.ppermute(rows, "expert", pair_moves(size, r)) for r in range(1, 4)]
    half = rows.shape[0] // 2
    first = lax.ppermute(rows, "expert", across)
    second = lax.ppermute(rows, "expert", along)
    top = lax.ppermute(second[:half], "expert", across)
    bottom = lax.ppermute(first[half:], "expert", along)
    return [rows, first, second, top, bottom]


def scatter_start(parts):
    low = jnp.bfloat16
    if lax.axis_size("expert") != 4:
        own = lax.axis_index("expert")
        order = jnp.arange(len(parts), dtype=jnp.int32) ^ own
        stacked = jnp.take(jnp.stack(parts), order, axis=0).astype(low)
        return [lax.psum_scatter(stacked, "expert", scatter_dimension=0).astype(jnp.float32)]
    across, along = pair_moves(4, 1), pair_moves(4, 2)
    half = parts[0].shape[0] // 2
    top = lax.ppermute(parts[3][:half].astype(low), "expert", across)
    bottom = lax.ppermute(parts[3][half:].astype(low), "expert", along)
    first_top = lax.ppermute(parts[1][:half].astype(low), "expert", across)
    second_bottom = lax.ppermute(parts[2][half:].astype(low), "expert", along)
    for_first = add_low(parts[1][half:], bottom)
    for_second = add_low(parts[2][:half], top)
    return [parts[0], first_top, second_bottom, for_first, for_second]


def scatter_finish(state):
    if len(state) == 1:
        return state[0]
    own, first_top, second_bottom, for_first, for_second = state
    half = first_top.shape[0]
    second_top = lax.ppermute(for_second, "expert", pair_moves(4, 2))
    first_bottom = lax.ppermute(for_first, "expert", pair_moves(4, 1))
    return jnp.concatenate(
        [
            total_of([own[:half], first_top, second_top]),
            total_of([own[half:], first_bottom, second_bottom]),
        ],
        axis=0,
    )


def scatter_blocks(parts):
    return scatter_finish(scatter_start(parts))


def after(values, events):
    return lax.optimization_barrier((values, events))[0]


def send_parts(parts):
    if lax.axis_size("expert") != 4:
        return [scatter_blocks(parts)]
    low = jnp.bfloat16
    return [parts[0]] + [
        lax.ppermute(parts[r].astype(low), "expert", pair_moves(4, r)) for r in range(1, 4)
    ]


def total_of(parts):
    total = parts[0].astype(jnp.float32)
    for part in parts[1:]:
        total += part.astype(jnp.float32)
    return total


def shift_dense(rows):
    if not cube():
        return [lax.all_gather(rows, ("batch", "expert"), axis=0, tiled=True)]
    below = lax.ppermute(rows, "batch", shift_moves(1))
    above = lax.ppermute(rows, "batch", shift_moves(3))
    return [rows, below, lax.ppermute(below, "batch", shift_moves(1)), above]


def gather_dense(line, columns, events):
    found = [rows[:, columns] for rows in line]
    if not cube():
        return [found[0][None]], jnp.zeros((1, 1), jnp.int32), (), ()
    place = lax.axis_index("batch")
    level, core = place // 2, place % 2
    member = lax.axis_index("expert")
    mine = gather_blocks(after(jnp.stack(found), events))
    plane, far = mine[1:3], mine[3:]
    mine = mine[:3] + [jnp.concatenate(far, axis=0)]
    other = [lax.ppermute(block, "batch", pair_moves(8, 1)) for block in mine]
    spots = [
        [(((level + 4 - k) % 4) * 2 + (core ^ c)) * 4 + (member ^ r) for k in range(4)]
        for c in range(2)
        for r in range(4)
    ]
    return mine + other, jnp.array(spots, jnp.int32), plane, far


def sum_chunk(packed_grad):
    return lax.psum_scatter(packed_grad, "batch", scatter_dimension=0, tiled=True)


def exchange_cores(values):
    return lax.ppermute(values, "batch", pair_moves(8, 1))


def step_up(values):
    return lax.ppermute(values, "batch", shift_moves(1))


def step_down(values):
    return lax.ppermute(values, "batch", shift_moves(3))


def add_low(*parts):
    total = parts[0].astype(jnp.float32)
    for part in parts[1:]:
        total += part.astype(jnp.float32)
    return total.astype(jnp.bfloat16)


def join_cores(own, received):
    return [add_low(own[r], received[r]) for r in range(4)]


def scatter_line(plane):
    level = lax.axis_index("batch") // 2
    own, up, far, down = (
        lax.dynamic_index_in_dim(plane, (level + r) % 4, axis=0, keepdims=False) for r in range(4)
    )
    forwarded = step_up(add_low(up, step_up(add_low(far))))
    return total_of([own, forwarded, step_down(add_low(down))])


def scatter_whole(found):
    values = found[0].reshape(found[0].shape[3:])
    total = lax.psum_scatter(values, ("batch", "expert"), scatter_dimension=0, tiled=True)
    return total.astype(jnp.float32)


def pack_kernel(chunks, query, key, value, small, out, gate, up, down, dense, *packed):
    start = 0
    for part in (query, key, value, small, out):
        dense[:, start : start + part.shape[1]] = part[...]
        start += part.shape[1]
    part, hidden_width = down.shape[1], gate.shape[2]
    for n, target in enumerate(packed):
        for e in range(chunks[n], chunks[n + 1]):
            for side, source in ((0, gate), (1, up)):
                for j in range(3):
                    target[side, e - chunks[n], :, j * hidden_width : (j + 1) * hidden_width] = (
                        source[e, j * part : (j + 1) * part, :]
                    )
            target[2, e - chunks[n]] = down[e]


def pack(chunks, query, key, value, small, out, gate, up, down):
    low = jnp.bfloat16
    columns = sum(part.shape[1] for part in (query, key, value, small, out))
    return pl.pallas_call(
        partial(pack_kernel, chunks),
        in_specs=[INSIDE] * 8,
        out_specs=[INSIDE] * len(chunks),
        out_shape=[jax.ShapeDtypeStruct((query.shape[0], columns), low)]
        + [
            jax.ShapeDtypeStruct((3, b - a) + down.shape[1:], low)
            for a, b in zip(chunks[:-1], chunks[1:])
        ],
        compiler_params=pltpu.CompilerParams(vmem_limit_bytes=VMEM_BYTES),
        cost_estimate=cost(0),
        name="pack",
    )(query, key, value, small, out, gate, up, down)


def local(
    tokens,
    cotangent,
    attn_gain,
    query_weight,
    key_weight,
    value_weight,
    out_weight,
    ffn_gain,
    router_weight,
    gate_weight,
    up_weight,
    down_weight,
    routes,
    ranking,
):
    low = jnp.bfloat16
    wide = jnp.float32
    query_width = HEADS * HEAD_DIM
    kv_width = KV_HEADS * HEAD_DIM
    qkv_width = query_width + 2 * kv_width
    width = tokens.shape[2]
    experts_total = router_weight.shape[1]
    extra = -(-(experts_total + 2) // 128) * 128
    first_gain, second_gain = experts_total, experts_total + 1
    local_experts = gate_weight.shape[0]
    member_count = lax.axis_size("expert")
    member_id = lax.axis_index("expert")
    local_rows = tokens.shape[1]
    group_rows = local_rows * member_count
    cut = cube()
    line_place = lax.axis_index("batch")
    place = jnp.stack([line_place % 2, member_id, line_place // 2]).astype(jnp.int32)

    route_rows = routes[0]
    rank_rows = ranking[0]
    expert_lanes = jnp.arange(extra, dtype=jnp.int32)
    member = jnp.any(route_rows[:, :, None] == expert_lanes[None, None, :], axis=1)
    marks = jnp.where(
        expert_lanes[None, :] == experts_total,
        (rank_rows // 32)[:, None],
        jnp.where(expert_lanes[None, :] == experts_total + 1, (rank_rows % 32)[:, None], member),
    ).astype(low)
    grad_out = cotangent[0]
    small_width = qkv_width + extra
    chunks = (0, 3, local_experts)
    dense_rows, *packed_own = pack(
        chunks,
        query_weight,
        key_weight,
        value_weight,
        jnp.concatenate(
            [
                router_weight,
                attn_gain[:, None],
                ffn_gain[:, None],
                jnp.zeros((query_weight.shape[0], extra - experts_total - 2), low),
            ],
            axis=1,
        ),
        out_weight,
        gate_weight,
        up_weight,
        down_weight,
    )
    line = shift_dense(dense_rows)
    grad_blocks = gather_blocks(
        after(jnp.concatenate([grad_out, marks], axis=1), dense_rows)
    )
    marks_all = jnp.concatenate([block[:, width:] for block in grad_blocks], axis=0)
    qkv_pieces, qkv_spots, plane, far = gather_dense(line, slice(0, small_width), grad_blocks)
    out_pieces, out_spots, out_plane, _ = gather_dense(line, slice(small_width, None), far)
    packed_all = [
        lax.all_gather(after(packed, events), "batch", axis=0)
        for packed, events in zip(packed_own, ((line, grad_blocks), plane))
    ]

    row_ids = member_id * local_rows + jnp.arange(local_rows, dtype=jnp.int32)
    half_dim = HEAD_DIM // 2
    frequency = THETA ** (-jnp.arange(half_dim, dtype=wide) / half_dim)
    angles = place_of(row_ids).astype(wide)[:, None] * frequency[None, :]
    cosine = jnp.tile(jnp.cos(angles), (1, 4))
    sine_part = jnp.tile(jnp.concatenate([-jnp.sin(angles), jnp.sin(angles)], axis=1), (1, 2))
    normed, query, keyval, small = enter(
        tokens[0], cosine, sine_part, qkv_pieces, qkv_spots, first_gain, query_width, kv_width
    )

    rank_all = (
        marks_all[:, experts_total].astype(wide) * 32 + marks_all[:, experts_total + 1].astype(wide)
    )
    earlier = (rank_all[None, :] < rank_rows.astype(wide)[:, None]).astype(low)
    before = product(earlier, marks_all)
    capacity = 5 * group_rows * route_rows.shape[1] // (4 * experts_total)
    member = member.astype(wide)
    kept = jnp.where(before < capacity, member, 0.0)

    keyval_blocks = gather_blocks(after(keyval, out_plane))
    if member_count == 4:
        ordered = keyval_blocks[:3] + [jnp.concatenate(keyval_blocks[3:], axis=0)]
        away = 1 << 20
        keys = jnp.concatenate(
            [
                lax.select_n(member_id, *ordered),
                lax.select_n(member_id ^ 1, *ordered),
                keyval,
            ],
            axis=0,
        )
        starts = [
            jnp.where(member_id >= 1, 0, away),
            jnp.where(member_id >= 2, local_rows, away),
            member_id * local_rows,
        ]
    else:
        keys = jnp.concatenate(keyval_blocks, axis=0)
        starts = [(member_id ^ r) * local_rows for r in range(member_count)]
    key_ids = jnp.concatenate([s + jnp.arange(local_rows, dtype=jnp.int32) for s in starts])
    bias = jnp.where(visible(row_ids, key_ids), 0.0, -1e30).astype(wide)
    attended, log_totals, residual, sent, gate_rows = attend(
        query, keys, bias, tokens[0], small, member, kept, second_gain, out_pieces, out_spots
    )
    sent_blocks = gather_blocks(sent)

    carry, chunk_grads = None, []
    for packed, a, b in zip(packed_all, chunks[:-1], chunks[1:]):
        first = (member_id * local_experts + a).astype(jnp.int32).reshape(1)
        packed_grads, mixture_all, row_grad = expert_pass(
            place,
            first,
            sent_blocks,
            grad_blocks,
            packed,
            carry,
            cut and b == local_experts,
            b == local_experts,
        )
        carry = (mixture_all, row_grad)
        chunk_grads.append(packed_grads)

    def blocks_of(values):
        return [values[r * local_rows : (r + 1) * local_rows] for r in range(member_count)]

    totals = [sum_chunk(chunk_grads[0][0])]
    if cut:
        own, rest, far, near = chunk_grads[1]
        far, near = exchange_cores(far), exchange_cores(near)
        far_sum, down_sum = add_low(rest[1], far[0]), add_low(rest[2], far[1])
    normed_grad = scatter_blocks(blocks_of(row_grad))
    if cut:
        normed_grad = after(normed_grad, (far_sum, down_sum))
    turned = turn(
        place,
        out_spots,
        (
            normed_grad,
            residual,
            grad_out,
            small,
            gate_rows,
            member,
            kept,
            sent,
            attended,
        ),
        out_pieces,
        cut,
        second_gain,
    )
    out_found = turned[:-2]
    resid_grad, head_grad = turned[-2:]
    mixture_parts = send_parts(blocks_of(after(mixture_all, normed_grad)))
    if cut:
        up_sum = add_low(rest[0], near[0], step_up(far_sum))
    query_grad, key_grads = attend_back(
        head_grad, query, keys, bias.T, log_totals, cosine, sine_part
    )
    if member_count == 4:
        zero = jnp.zeros((), low)
        for_first, for_second, for_own = blocks_of(key_grads)[:3]
        key_parts = []
        for r in range(4):
            part = jnp.where(member_id == r, for_first, zero)
            part += jnp.where(member_id ^ 1 == r, for_second, zero)
            key_parts.append(part + for_own if r == 0 else part)
    else:
        key_parts = blocks_of(key_grads)
    if cut:
        out_found = out_found[1], exchange_cores(out_found[0])
        key_parts = after(key_parts, (mixture_parts[1:], up_sum))
    keyval_sum = scatter_blocks(key_parts)
    if cut:
        out_state = scatter_start(join_cores(*out_found))
    if cut:
        keyval_sum = after(keyval_sum, out_found)
    left = leave(
        place,
        qkv_spots,
        (
            keyval_sum,
            query_grad,
            normed,
            tokens[0],
            resid_grad,
            small,
            cosine,
            sine_part,
        ),
        qkv_pieces,
        cut,
        first_gain,
    )
    qkv_found, input_grad = left[:-1], left[-1]
    result = (residual + total_of(mixture_parts)).astype(low)
    if cut:
        down_term = step_down(after(down_sum, key_parts))
        received = exchange_cores(after(qkv_found[0], (totals[0], out_state[1:], down_term)))
        out_plane = scatter_finish(out_state)
        up_term = step_up(up_sum)
        qkv_parts = join_cores(qkv_found[1], after(received, out_plane))
        qkv_plane = after(scatter_blocks(qkv_parts), up_term)
        out_sum = scatter_line(out_plane)
        qkv_sum = scatter_line(qkv_plane)
        terms = [[totals[0][0]], after([own, near[1], down_term, up_term], qkv_plane)]
    else:
        out_sum = scatter_whole(out_found)
        qkv_sum = scatter_whole(qkv_found)
        terms = [[totals[0][0]]] + [[sum_chunk(found[0])[0]] for found in chunk_grads[1:]]
    gate_total, up_total, down_total = unpack(terms, gate_weight.shape, down_weight.shape)
    return (
        result[None],
        input_grad[None],
        qkv_sum[:, qkv_width + first_gain],
        qkv_sum[:, :query_width],
        qkv_sum[:, query_width : query_width + kv_width],
        qkv_sum[:, query_width + kv_width : qkv_width],
        out_sum[:, :width],
        out_sum[:, width + second_gain],
        out_sum[:, width : width + experts_total],
        gate_total,
        up_total,
        down_total,
    )


def solution(mesh):
    return jax.shard_map(
        local,
        mesh=mesh,
        in_specs=(
            P("batch", "expert", None),
            P("batch", "expert", None),
            P(("batch", "expert")),
            P(("batch", "expert"), None),
            P(("batch", "expert"), None),
            P(("batch", "expert"), None),
            P(("batch", "expert"), None),
            P(("batch", "expert")),
            P(("batch", "expert"), None),
            P("expert", "batch", None),
            P("expert", "batch", None),
            P("expert", "batch", None),
            P("batch", "expert", None),
            P("batch", "expert"),
        ),
        out_specs=(
            P("batch", "expert", None),
            P("batch", "expert", None),
            P(("batch", "expert")),
            P(("batch", "expert"), None),
            P(("batch", "expert"), None),
            P(("batch", "expert"), None),
            P(("batch", "expert"), None),
            P(("batch", "expert")),
            P(("batch", "expert"), None),
            P("expert", "batch", None),
            P("expert", "batch", None),
            P("expert", "batch", None),
        ),
        check_vma=False,
    )
```

profile of v0, /device:TPU:0, one launch (start us, length us, event | category | flops | bytes accessed | tf_op | source)
XLA Modules:
  0.0 563.8 jit_solution(13527985031173571125)
XLA Ops:
  23.6 15.9 %collective-permute-done.4.refs_7_ = bf16[256,1664]{1,0:T(8,128)(2,1)S(1)} collective-permute-done((bf16[256,1664]{1,0:T(8,128)(2,1)S(1)}, bf16[256,1664]{1,0:T(8,128)(2,1)S(1)}, u32[]{:S(2)}, u32[]{:S(2)}) %collective-permute-start.4) | collective-permute-done | bytes 852000 | tf_op jit(solution)/shard_map/ppermute | solution.py:811
  47.3 10.1 %collective-permute-done.2 = bf16[48,4224]{1,0:T(8,128)(2,1)S(1)} collective-permute-done((bf16[48,4224]{1,0:T(8,128)(2,1)}, bf16[48,4224]{1,0:T(8,128)(2,1)S(1)}, u32[]{:S(2)}, u32[]{:S(2)}) %collective-permute-start.2) | collective-permute-done | bytes 405536 | tf_op jit(solution)/shard_map/ppermute | solution.py:879
  57.5 6.9 %collective-permute-done.1 = bf16[48,4224]{1,0:T(8,128)(2,1)S(1)} collective-permute-done((bf16[48,4224]{1,0:T(8,128)(2,1)S(1)}, bf16[48,4224]{1,0:T(8,128)(2,1)S(1)}, u32[]{:S(2)}, u32[]{:S(2)}) %collective-permute-start.1) | collective-permute-done | bytes 405536 | tf_op jit(solution)/shard_map/ppermute | solution.py:880
  66.9 20.6 %collective-permute-done.7.refs_1_ = bf16[4,48,2688]{2,1,0:T(8,128)(2,1)S(1)} collective-permute-done((bf16[4,48,2688]{2,1,0:T(8,128)(2,1)S(1)}, bf16[4,48,2688]{2,1,0:T(8,128)(2,1)S(1)}, u32[]{:S(2)}, u32[]{:S(2)}) %collective-permute-start.7) | collective-permute-done | bytes 1032224 | tf_op jit(solution)/shard_map/ppermute | solution.py:810
  101.7 6.5 %collective-permute-done.9 = bf16[2,48,2688]{2,1,0:T(8,128)(2,1)S(1)} collective-permute-done((bf16[2,48,2688]{2,1,0:T(8,128)(2,1)S(1)}, bf16[2,48,2688]{2,1,0:T(8,128)(2,1)S(1)}, u32[]{:S(2)}, u32[]{:S(2)}) %collective-permute-start.9) | collective-permute-done | bytes 516128 | tf_op jit(solution)/shard_map/ppermute | solution.py:812
  117.6 8.2 %enter.1 = (bf16[256,1536]{1,0:T(8,128)(2,1)}, bf16[256,1536]{1,0:T(8,128)(2,1)}, bf16[256,1024]{1,0:T(8,128)(2,1)}, f32[128,1536]{1,0:T(8,128)}) custom-call(s32[8,4]{1,0:T(8,128)} %concatenate.91.spots.refs_7_, bf16[256,1536]{1,0:T(8,128)(2,1)} %bitcast.180, f32[256,128]{1,0:T(8,128)} %copy.57.cosine, f32[256,128]{1,0:T(8,128)} %copy.58.sine, ...), custom_call_target="tpu_custom_call" | custom-call | flops 1 | bytes 1 | tf_op jit(solution)/shard_map/enter/pallas_call | solution.py:137
  135.0 7.7 %collective-permute-done.18 = bf16[256,1024]{1,0:T(8,128)(2,1)S(1)} collective-permute-done((bf16[256,1024]{1,0:T(8,128)(2,1)}, bf16[256,1024]{1,0:T(8,128)(2,1)S(1)}, u32[]{:S(2)}, u32[]{:S(2)}) %collective-permute-start.18) | collective-permute-done | bytes 524320 | tf_op jit(solution)/shard_map/ppermute | solution.py:811
  144.2 8.0 %collective-permute-done.17 = bf16[256,1024]{1,0:T(8,128)(2,1)S(1)} collective-permute-done((bf16[256,1024]{1,0:T(8,128)(2,1)}, bf16[256,1024]{1,0:T(8,128)(2,1)S(1)}, u32[]{:S(2)}, u32[]{:S(2)}) %collective-permute-start.17) | collective-permute-done | bytes 524320 | tf_op jit(solution)/shard_map/ppermute | solution.py:810
  164.3 17.2 %attend.1 = (bf16[256,1536]{1,0:T(8,128)(2,1)}, f32[256,128]{1,0:T(8,128)}, f32[256,1536]{1,0:T(8,128)}, bf16[256,1664]{1,0:T(8,128)(2,1)}, f32[256,128]{1,0:T(8,128)}) custom-call(bf16[256,1536]{1,0:T(8,128)(2,1)} %get-tuple-element.69.refs_0_.query, bf16[768,1024]{1,0:T(8,128)(2,1)} %pad_maximum_fusion.3.refs_1_.keyval, ...), custom_call_target="tpu_custom_call" | custom-call | flops 1 | bytes 1 | tf_op jit(solution)/shard_map/attend/pallas_call | solution.py:233
  183.3 19.2 %collective-permute-done.28.refs_2_ = bf16[256,1664]{1,0:T(8,128)(2,1)S(1)} collective-permute-done((bf16[256,1664]{1,0:T(8,128)(2,1)}, bf16[256,1664]{1,0:T(8,128)(2,1)S(1)}, u32[]{:S(2)}, u32[]{:S(2)}) %collective-permute-start.28) | collective-permute-done | bytes 852000 | tf_op jit(solution)/shard_map/ppermute | solution.py:811
  204.9 8.4 %collective-permute-done.29.refs_3_ = bf16[128,1664]{1,0:T(8,128)(2,1)} collective-permute-done((bf16[128,1664]{1,0:T(8,128)(2,1)S(1)}, bf16[128,1664]{1,0:T(8,128)(2,1)}, u32[]{:S(2)}, u32[]{:S(2)}) %collective-permute-start.29) | collective-permute-done | bytes 426016 | tf_op jit(solution)/shard_map/ppermute | solution.py:812
  214.6 62.5 %experts.2 = (bf16[8,3,3,64,1536]{4,3,2,1,0:T(8,128)(2,1)}, f32[1024,1536]{1,0:T(8,128)}, f32[1024,1664]{1,0:T(8,128)}) custom-call(s32[3]{0:T(128)} %pad_add_fusion.1.place, s32[1]{0:T(128)} %bitcast.61.first, bf16[8,3,3,64,1536]{4,3,2,1,0:T(8,128)(2,1)} %bitcast.178, bf16[256,1664]{1,0:T(8,128)(2,1)} %get-tuple-element.77.refs_0_.normed, ...), custom_call_target="tpu_custom_call" | custom-call | flops 1 | bytes 1 | tf_op jit(solution)/shard_map/experts/pallas_call | solution.py:717
  277.1 6.2 %all-gather.5.cloned.1.call-done = bf16[24,2,64,1536]{3,2,1,0:T(8,128)(2,1)} async-done(((bf16[3,2,64,1536]{3,2,1,0:T(8,128)(2,1)}), bf16[24,2,64,1536]{3,2,1,0:T(8,128)(2,1)}) %all-gather.5.cloned.1.call-update) | async-done | bytes 9437200 | tf_op jit(solution)/shard_map/all_gather | solution.py:1051
  283.3 45.8 %experts.3 = (bf16[3,2,64,1536]{3,2,1,0:T(8,128)(2,1)}, bf16[3,3,2,64,1536]{4,3,2,1,0:T(8,128)(2,1)}, bf16[2,3,2,64,1536]{4,3,2,1,0:T(8,128)(2,1)}, bf16[2,3,2,6...) custom-call(s32[3]{0:T(128)} %pad_add_fusion.1.place, s32[1]{0:T(128)} %bitcast.59.first, ...), custom_call_target="tpu_custom_call" | custom-call | flops 1 | bytes 1 | tf_op jit(solution)/shard_map/experts/pallas_call | solution.py:717
  335.6 9.1 %collective-permute-done.32 = bf16[128,1664]{1,0:T(8,128)(2,1)S(1)} collective-permute-done((bf16[128,1664]{1,0:T(8,128)(2,1)S(1)}, bf16[128,1664]{1,0:T(8,128)(2,1)S(1)}, u32[]{:S(2)}, u32[]{:S(2)}) %collective-permute-start.32) | collective-permute-done | bytes 426016 | tf_op jit(solution)/shard_map/ppermute | solution.py:826
  375.0 11.4 %turn.1 = (bf16[4,4,48,1664]{3,2,1,0:T(8,128)(2,1)}, bf16[4,4,48,1664]{3,2,1,0:T(8,128)(2,1)}, f32[256,1536]{1,0:T(8,128)}, bf16[256,1536]{1,0:T(8,128)(2,1)}) custom-call(s32[3]{0:T(128)} %pad_add_fusion.1.place, s32[8,4]{1,0:T(8,128)} %concatenate.91.spots.refs_7_, f32[256,1664]{1,0:T(8,128)} %pad_maximum_fusion.2.normed_grad, ...), custom_call_target="tpu_custom_call" | custom-call | flops 1 | bytes 1 | tf_op jit(solution)/shard_map/turn/pallas_call | solution.py:360
  386.4 21.3 %attend_back.1 = (bf16[256,1536]{1,0:T(8,128)(2,1)}, bf16[768,1024]{1,0:T(8,128)(2,1)}) custom-call(bf16[256,1536]{1,0:T(8,128)(2,1)} %get-tuple-element.90.head_grad, bf16[256,1536]{1,0:T(8,128)(2,1)} %get-tuple-element.69.refs_0_.query, bf16[768,1024]{1,0:T(8,128)(2,1)} %pad_maximum_fusion.3.refs_1_.keyval, f32[768,256]{1,0:T(8,128)} %and_select_fusion.bias, ...), custom_call_target="tpu_custom_call" | custom-call | flops 1 | bytes 1 | tf_op jit(solution)/shard_map/attend_back/pallas_call | solution.py:435
  409.3 9.8 %collective-permute-done.42 = bf16[3,2,64,1536]{3,2,1,0:T(8,128)(2,1)} collective-permute-done((bf16[3,2,64,1536]{3,2,1,0:T(8,128)(2,1)}, bf16[3,2,64,1536]{3,2,1,0:T(8,128)(2,1)}, u32[]{:S(2)}, u32[]{:S(2)}) %collective-permute-start.42) | collective-permute-done | bytes 1179680 | tf_op jit(solution)/shard_map/ppermute | solution.py:911
  448.4 15.1 %leave.1 = (bf16[4,4,48,2688]{3,2,1,0:T(8,128)(2,1)}, bf16[4,4,48,2688]{3,2,1,0:T(8,128)(2,1)}, f32[256,1536]{1,0:T(8,128)}) custom-call(s32[3]{0:T(128)} %pad_add_fusion.1.place, s32[8,4]{1,0:T(8,128)} %concatenate.91.spots.refs_7_, f32[256,1024]{1,0:T(8,128)} %pad_maximum_fusion.4.keyval_sum, bf16[256,1536]{1,0:T(8,128)(2,1)} %get-tuple-element.101.query_grad, ...), custom_call_target="tpu_custom_call" | custom-call | flops 1 | bytes 1 | tf_op jit(solution)/shard_map/leave/pallas_call | solution.py:520
  467.3 8.6 %collective-permute-done.54.refs_3_ = bf16[3,2,64,1536]{3,2,1,0:T(8,128)(2,1)} collective-permute-done((bf16[3,2,64,1536]{3,2,1,0:T(8,128)(2,1)}, bf16[3,2,64,1536]{3,2,1,0:T(8,128)(2,1)}, u32[]{:S(2)}, u32[]{:S(2)}) %collective-permute-start.54) | collective-permute-done | bytes 1179680 | tf_op jit(solution)/shard_map/ppermute | solution.py:915
  490.8 13.2 %collective-permute-done.61 = bf16[2,48,2688]{2,1,0:T(8,128)(2,1)S(1)} collective-permute-done((bf16[2,48,2688]{2,1,0:T(8,128)(2,1)S(1)}, bf16[2,48,2688]{2,1,0:T(8,128)(2,1)S(1)}, u32[]{:S(2)}, u32[]{:S(2)}) %collective-permute-start.61) | collective-permute-done | bytes 516128 | tf_op jit(solution)/shard_map/ppermute | solution.py:827
  510.3 8.4 %collective-permute-done.58 = bf16[2,48,2688]{2,1,0:T(8,128)(2,1)S(1)} collective-permute-done((bf16[2,48,2688]{2,1,0:T(8,128)(2,1)S(1)}, bf16[2,48,2688]{2,1,0:T(8,128)(2,1)S(1)}, u32[]{:S(2)}, u32[]{:S(2)}) %collective-permute-start.58) | collective-permute-done | bytes 516128 | tf_op jit(solution)/shard_map/ppermute | solution.py:828
  535.9 5.9 %collective-permute-done.65 = bf16[48,2688]{1,0:T(8,128)(2,1)S(1)} collective-permute-done((bf16[48,2688]{1,0:T(8,128)(2,1)S(1)}, bf16[48,2688]{1,0:T(8,128)(2,1)S(1)}, u32[]{:S(2)}, u32[]{:S(2)}) %collective-permute-start.65) | collective-permute-done | bytes 258080 | tf_op jit(solution)/shard_map/ppermute | solution.py:911
  547.5 5.7 %unpack.1 = (f32[5,192,512]{2,1,0:T(8,128)}, f32[5,192,512]{2,1,0:T(8,128)}, f32[5,64,1536]{2,1,0:T(8,128)}) custom-call(bf16[3,3,64,1536]{3,2,1,0:T(8,128)(2,1)} %bitcast.185, bf16[3,2,64,1536]{3,2,1,0:T(8,128)(2,1)} %get-tuple-element.113.refs_1_, bf16[3,2,64,1536]{3,2,1,0:T(8,128)(2,1)} %slice_bitcast_fusion.refs_2_, ...), custom_call_target="tpu_custom_call" | custom-call | flops 1 | bytes 1 | tf_op jit(solution)/shard_map/unpack/pallas_call | solution.py:771
  (335 shorter events, 197.2 us)
Async XLA Ops:
  7.2 207.4 %all-gather.7.cloned.1.call-start = ((), (), s32[]{:S(2)}) async-start(), calls=%async_computation.3 | async-start | bytes 15925248 | tf_op jit(solution)/shard_map/all_gather | solution.py:1051
  22.0 25.3 %collective-permute-start = (bf16[48,4224]{1,0:T(8,128)(2,1)}, bf16[48,4224]{1,0:T(8,128)(2,1)S(1)}, u32[]{:S(2)}, u32[]{:S(2)}) collective-permute-start(bf16[48,4224]{1,0:T(8,128)(2,1)} %get-tuple-element.66), channel_id=1, source_target_pairs={{0,8},{4,12},{8,16},{12,20},{16,24},{20,28},{24,0},{28,4},{1,9},{5... | collective-permute-start | bytes 1216520 | tf_op jit(solution)/shard_map/ppermute | solution.py:878
  39.5 24.8 %collective-permute-start.5 = (bf16[128,1664]{1,0:T(8,128)(2,1)S(1)}, bf16[128,1664]{1,0:T(8,128)(2,1)S(1)}, u32[]{:S(2)}, u32[]{:S(2)}) collective-permute-start(bf16[128,1664]{1,0:T(8,128)(2,1)S(1)} %slice.431), channel_id=1, source_target_pairs={{0,1},{1,0},{2,3},{3,2},{4,5},{5,4},{6,7},{7,6},{8,9},{9,8},{10,11... | collective-permute-start | bytes 1277960 | tf_op jit(solution)/shard_map/ppermute | solution.py:812
  42.2 22.1 %collective-permute-start.6 = (bf16[128,1664]{1,0:T(8,128)(2,1)S(1)}, bf16[128,1664]{1,0:T(8,128)(2,1)}, u32[]{:S(2)}, u32[]{:S(2)}) collective-permute-start(bf16[128,1664]{1,0:T(8,128)(2,1)S(1)} %slice.432), channel_id=1, source_target_pairs={{0,2},{1,3},{2,0},{3,1},{4,6},{5,7},{6,4},{7,5},{8,10},{9,11},{10,... | collective-permute-start | bytes 1277960 | tf_op jit(solution)/shard_map/ppermute | solution.py:813
  64.4 218.9 %all-gather.5.cloned.1.call-start = ((), (), s32[]{:S(2)}) async-start(), calls=%async_computation.2 | async-start | bytes 10616832 | tf_op jit(solution)/shard_map/all_gather | solution.py:1051
  65.2 22.3 %collective-permute-start.7 = (bf16[4,48,2688]{2,1,0:T(8,128)(2,1)S(1)}, bf16[4,48,2688]{2,1,0:T(8,128)(2,1)S(1)}, u32[]{:S(2)}, u32[]{:S(2)}) collective-permute-start(bf16[4,48,2688]{2,1,0:T(8,128)(2,1)S(1)} %pad_maximum_fusion.5.refs_0_), channel_id=1, source_target_pairs={{0,1},{1,0},{2,3},{3,2},{4,5},{5,4},{6,7},{7,6},{8,9},{9,8},{10,11... | collective-permute-start | bytes 3096584 | tf_op jit(solution)/shard_map/ppermute | solution.py:810
  66.4 22.2 %collective-permute-start.8 = (bf16[4,48,2688]{2,1,0:T(8,128)(2,1)S(1)}, bf16[4,48,2688]{2,1,0:T(8,128)(2,1)S(1)}, u32[]{:S(2)}, u32[]{:S(2)}) collective-permute-start(bf16[4,48,2688]{2,1,0:T(8,128)(2,1)S(1)} %pad_maximum_fusion.5.refs_0_), channel_id=1, source_target_pairs={{0,2},{1,3},{2,0},{3,1},{4,6},{5,7},{6,4},{7,5},{8,10},{9,11},{10,... | collective-permute-start | bytes 3096584 | tf_op jit(solution)/shard_map/ppermute | solution.py:811
  89.6 386.3 %reduce-scatter.2.cloned.1.call-start = ((), (), s32[]{:S(2)}) async-start(), calls=%async_computation.1 | async-start | bytes 15925248 | tf_op jit(solution)/shard_map/reduce_scatter | solution.py:903
  135.0 27.6 %collective-permute-start.23 = (bf16[4,48,1536]{2,1,0:T(8,128)(2,1)}, bf16[4,48,1536]{2,1,0:T(8,128)(2,1)S(1)}, u32[]{:S(2)}, u32[]{:S(2)}) collective-permute-start(bf16[4,48,1536]{2,1,0:T(8,128)(2,1)} %pad_maximum_fusion.7.refs_8_.refs_0_), channel_id=1, source_target_pairs={{0,4},{4,0},{8,12},{12,8},{16,20},{20,16},{24,28},{28,24},{1,5},{5... | collective-permute-start | bytes 1769480 | tf_op jit(solution)/shard_map/ppermute | solution.py:893
  181.9 22.1 %collective-permute-start.27 = (bf16[256,1664]{1,0:T(8,128)(2,1)}, bf16[256,1664]{1,0:T(8,128)(2,1)S(1)}, u32[]{:S(2)}, u32[]{:S(2)}) collective-permute-start(bf16[256,1664]{1,0:T(8,128)(2,1)} %get-tuple-element.77.refs_0_.normed), channel_id=1, source_target_pairs={{0,1},{1,0},{2,3},{3,2},{4,5},{5,4},{6,7},{7,6},{8,9},{9,8},{10,11... | collective-permute-start | bytes 2555912 | tf_op jit(solution)/shard_map/ppermute | solution.py:810
  329.0 31.3 %collective-permute-start.37 = (bf16[2,3,2,64,1536]{4,3,2,1,0:T(8,128)(2,1)}, bf16[2,3,2,64,1536]{4,3,2,1,0:T(8,128)(2,1)}, u32[]{:S(2)}, u32[]{:S(2)}) collective-permute-start(bf16[2,3,2,64,1536]{4,3,2,1,0:T(8,128)(2,1)} %get-tuple-element.85), channel_id=1, source_target_pairs={{0,4},{4,0},{8,12},{12,8},{16,20},{20,16},{24,28},{28,24},{1,5},{5... | collective-permute-start | bytes 7077896 | tf_op jit(solution)/shard_map/ppermute | solution.py:907
  348.5 59.2 %collective-permute-start.41 = (bf16[2,3,2,64,1536]{4,3,2,1,0:T(8,128)(2,1)}, bf16[2,3,2,64,1536]{4,3,2,1,0:T(8,128)(2,1)}, u32[]{:S(2)}, u32[]{:S(2)}) collective-permute-start(bf16[2,3,2,64,1536]{4,3,2,1,0:T(8,128)(2,1)} %get-tuple-element.93), channel_id=1, source_target_pairs={{0,4},{4,0},{8,12},{12,8},{16,20},{20,16},{24,28},{28,24},{1,5},{5... | collective-permute-start | bytes 7077896 | tf_op jit(solution)/shard_map/ppermute | solution.py:907
  364.1 55.0 %collective-permute-start.42 = (bf16[3,2,64,1536]{3,2,1,0:T(8,128)(2,1)}, bf16[3,2,64,1536]{3,2,1,0:T(8,128)(2,1)}, u32[]{:S(2)}, u32[]{:S(2)}) collective-permute-start(bf16[3,2,64,1536]{3,2,1,0:T(8,128)(2,1)} %get-tuple-element.173), channel_id=1, source_target_pairs={{0,8},{4,12},{8,16},{12,20},{16,24},{20,28},{24,0},{28,4},{1,9},{5... | collective-permute-start | bytes 3538952 | tf_op jit(solution)/shard_map/ppermute | solution.py:911
  371.5 51.1 %collective-permute-start.38 = (bf16[256,1536]{1,0:T(8,128)(2,1)}, bf16[256,1536]{1,0:T(8,128)(2,1)}, u32[]{:S(2)}, u32[]{:S(2)}) collective-permute-start(bf16[256,1536]{1,0:T(8,128)(2,1)} %get-tuple-element.184), channel_id=1, source_target_pairs={{0,1},{1,0},{2,3},{3,2},{4,5},{5,4},{6,7},{7,6},{8,9},{9,8},{10,11... | collective-permute-start | bytes 2359304 | tf_op jit(solution)/shard_map/ppermute | solution.py:864
  372.8 49.9 %collective-permute-start.39 = (bf16[256,1536]{1,0:T(8,128)(2,1)S(1)}, bf16[256,1536]{1,0:T(8,128)(2,1)}, u32[]{:S(2)}, u32[]{:S(2)}) collective-permute-start(bf16[256,1536]{1,0:T(8,128)(2,1)S(1)} %get-tuple-element.186), channel_id=1, source_target_pairs={{0,2},{1,3},{2,0},{3,1},{4,6},{5,7},{6,4},{7,5},{8,10},{9,11},{10,... | collective-permute-start | bytes 2359304 | tf_op jit(solution)/shard_map/ppermute | solution.py:864
  374.3 48.4 %collective-permute-start.40 = (bf16[256,1536]{1,0:T(8,128)(2,1)S(1)}, bf16[256,1536]{1,0:T(8,128)(2,1)}, u32[]{:S(2)}, u32[]{:S(2)}) collective-permute-start(bf16[256,1536]{1,0:T(8,128)(2,1)S(1)} %get-tuple-element.185), channel_id=1, source_target_pairs={{0,3},{1,2},{2,1},{3,0},{4,7},{5,6},{6,5},{7,4},{8,11},{9,10},{10,... | collective-permute-start | bytes 2359304 | tf_op jit(solution)/shard_map/ppermute | solution.py:864
  407.7 33.6 %collective-permute-start.49 = (bf16[4,4,48,1664]{3,2,1,0:T(8,128)(2,1)}, bf16[4,4,48,1664]{3,2,1,0:T(8,128)(2,1)S(1)}, u32[]{:S(2)}, u32[]{:S(2)}) collective-permute-start(bf16[4,4,48,1664]{3,2,1,0:T(8,128)(2,1)} %get-tuple-element.99), channel_id=1, source_target_pairs={{0,4},{4,0},{8,12},{12,8},{16,20},{20,16},{24,28},{28,24},{1,5},{5... | collective-permute-start | bytes 7667720 | tf_op jit(solution)/shard_map/ppermute | solution.py:907
  436.5 39.3 %collective-permute-start.54 = (bf16[3,2,64,1536]{3,2,1,0:T(8,128)(2,1)}, bf16[3,2,64,1536]{3,2,1,0:T(8,128)(2,1)}, u32[]{:S(2)}, u32[]{:S(2)}) collective-permute-start(bf16[3,2,64,1536]{3,2,1,0:T(8,128)(2,1)} %get-tuple-element.108), channel_id=1, source_target_pairs={{0,24},{4,28},{8,0},{12,4},{16,8},{20,12},{24,16},{28,20},{1,25},{... | collective-permute-start | bytes 3538952 | tf_op jit(solution)/shard_map/ppermute | solution.py:915
  443.3 22.2 %collective-permute-start.52 = (bf16[2,48,1664]{2,1,0:T(8,128)(2,1)}, bf16[2,48,1664]{2,1,0:T(8,128)(2,1)}, u32[]{:S(2)}, u32[]{:S(2)}) collective-permute-start(bf16[2,48,1664]{2,1,0:T(8,128)(2,1)} %get-tuple-element.204), channel_id=1, source_target_pairs={{0,2},{1,3},{2,0},{3,1},{4,6},{5,7},{6,4},{7,5},{8,10},{9,11},{10,... | collective-permute-start | bytes 958472 | tf_op jit(solution)/shard_map/ppermute | solution.py:827
  445.8 30.0 %collective-permute-start.50 = (bf16[2,48,1664]{2,1,0:T(8,128)(2,1)}, bf16[2,48,1664]{2,1,0:T(8,128)(2,1)}, u32[]{:S(2)}, u32[]{:S(2)}) collective-permute-start(bf16[2,48,1664]{2,1,0:T(8,128)(2,1)} %slice_bitcast_fusion.16), channel_id=1, source_target_pairs={{0,1},{1,0},{2,3},{3,2},{4,5},{5,4},{6,7},{7,6},{8,9},{9,8},{10,11... | collective-permute-start | bytes 958472 | tf_op jit(solution)/shard_map/ppermute | solution.py:828
  447.0 28.8 %collective-permute-start.51 = (bf16[2,48,1664]{2,1,0:T(8,128)(2,1)}, bf16[2,48,1664]{2,1,0:T(8,128)(2,1)}, u32[]{:S(2)}, u32[]{:S(2)}) collective-permute-start(bf16[2,48,1664]{2,1,0:T(8,128)(2,1)} %slice_bitcast_fusion.15), channel_id=1, source_target_pairs={{0,2},{1,3},{2,0},{3,1},{4,6},{5,7},{6,4},{7,5},{8,10},{9,11},{10,... | collective-permute-start | bytes 958472 | tf_op jit(solution)/shard_map/ppermute | solution.py:829
  481.8 48.1 %collective-permute-start.64 = (bf16[3,2,64,1536]{3,2,1,0:T(8,128)(2,1)S(1)}, bf16[3,2,64,1536]{3,2,1,0:T(8,128)(2,1)S(1)}, u32[]{:S(2)}, u32[]{:S(2)}) collective-permute-start(bf16[3,2,64,1536]{3,2,1,0:T(8,128)(2,1)S(1)} %copy-done.32), channel_id=1, source_target_pairs={{0,8},{4,12},{8,16},{12,20},{16,24},{20,28},{24,0},{28,4},{1,9},{5... | collective-permute-start | bytes 3538952 | tf_op jit(solution)/shard_map/ppermute | solution.py:911
  483.3 24.0 %collective-permute-start.56 = (bf16[2,48,1664]{2,1,0:T(8,128)(2,1)S(1)}, bf16[2,48,1664]{2,1,0:T(8,128)(2,1)S(1)}, u32[]{:S(2)}, u32[]{:S(2)}) collective-permute-start(bf16[2,48,1664]{2,1,0:T(8,128)(2,1)S(1)} %copy-done.38), channel_id=1, source_target_pairs={{0,2},{1,3},{2,0},{3,1},{4,6},{5,7},{6,4},{7,5},{8,10},{9,11},{10,... | collective-permute-start | bytes 958472 | tf_op jit(solution)/shard_map/ppermute | solution.py:840
  484.8 23.1 %collective-permute-start.57 = (bf16[2,48,1664]{2,1,0:T(8,128)(2,1)S(1)}, bf16[2,48,1664]{2,1,0:T(8,128)(2,1)S(1)}, u32[]{:S(2)}, u32[]{:S(2)}) collective-permute-start(bf16[2,48,1664]{2,1,0:T(8,128)(2,1)S(1)} %copy-done.37), channel_id=1, source_target_pairs={{0,1},{1,0},{2,3},{3,2},{4,5},{5,4},{6,7},{7,6},{8,9},{9,8},{10,11... | collective-permute-start | bytes 958472 | tf_op jit(solution)/shard_map/ppermute | solution.py:841
  (92 other events, 1313.2 us)
Sparse Core Ops, SparseCore 0:
  64.5 127.5 all-gather.6
  194.3 88.9 all-gather.4
  285.6 185.6 reduce-scatter.1
where the time goes:
time: 572 us; the launch traced here: 564 us
  waiting for transfers between devices  211 us (37%)
  Pallas kernels  191 us (33%)
  starting transfers between devices  69.5 us (12%)
  other arithmetic  39.8 us (7%)
  local copies, waits for them, and re-layouts  36.8 us (6%)
  between operations  15.3 us (3%)
    pallas_call x2, Pallas kernels, expert_pass(): pl.pallas_call(partial(expert_kernel, cut, carried, last, len(rows), len(...  108 us
    ppermute x5, waiting for transfers between devices, gather_blocks(): second = lax.ppermute(rows, 'expert', along)  45.6 us
    ppermute x5, waiting for transfers between devices, gather_blocks(): first = lax.ppermute(rows, 'expert', across)  28.6 us
    pallas_call x1, Pallas kernels, attend_back(): pl.pallas_call(attend_back_kernel, in_specs=[INSIDE] * 7, out_specs=[INSI...  21.3 us
    ppermute x6, waiting for transfers between devices, step_up(): return lax.ppermute(values, 'batch', shift_moves(1))  19.3 us
    ppermute x5, waiting for transfers between devices, gather_blocks(): top = lax.ppermute(second[:half], 'expert', across)  17.9 us
    ppermute x4, waiting for transfers between devices, scatter_start(): bottom = lax.ppermute(parts[3][half:].astype(low), 'expert', along)  17.4 us
    pallas_call x1, Pallas kernels, attend(): pl.pallas_call(kernel, in_specs=[INSIDE] * 7 + [SCALARS] + [ANYWHERE] * l...  17.2 us
  transfers between devices with their start and end apart: 74, of which 35 were waited for; matrix products, arithmetic and copies ran while one was open for 11% of the time, Pallas kernels for 33%

commit v1 on v0

--- a/solution.py
+++ b/solution.py
@@ -165,20 +165,12 @@
     ]
 
 
-def attend_kernel(
-    count, query, keyval, bias, tokens, small, member, kept, gain_at, spots, *refs
-):
-    pieces = refs[:count]
-    attended, log_totals, residual, sent, gate_rows, weight, sems = refs[count:]
+def attend_kernel(query, keyval, bias, attended, log_totals):
     low = jnp.bfloat16
     rows = query.shape[0]
-    width = tokens.shape[1]
     kv_width = keyval.shape[1] // 2
     pair_lanes = 2 * HEAD_DIM
     repeat = HEADS // KV_HEADS
-    copies = weight_copies(spots, pieces, weight, sems)
-    for copy in copies:
-        copy.start()
     log_totals[...] = jnp.zeros_like(log_totals)
     lane = lax.broadcasted_iota(jnp.int32, log_totals.shape, 1)
 
@@ -205,6 +197,31 @@
                 )
             attended[:, at] = total.astype(low)
 
+
+def attend(query, keyval, bias):
+    rows, query_width = query.shape
+    return pl.pallas_call(
+        attend_kernel,
+        in_specs=[INSIDE] * 3,
+        out_specs=[INSIDE] * 2,
+        out_shape=[
+            jax.ShapeDtypeStruct((rows, query_width), jnp.bfloat16),
+            jax.ShapeDtypeStruct((rows, 128), jnp.float32),
+        ],
+        compiler_params=pltpu.CompilerParams(vmem_limit_bytes=VMEM_BYTES),
+        cost_estimate=cost(8 * rows * query_width * bias.shape[1], query, keyval, bias),
+        name="attend",
+    )(query, keyval, bias)
+
+
+def project_kernel(count, gain_at, spots, attended, tokens, small, member, kept, *refs):
+    pieces = refs[:count]
+    residual, sent, gate_rows, weight, sems = refs[count:]
+    low = jnp.bfloat16
+    width = tokens.shape[1]
+    copies = weight_copies(spots, pieces, weight, sems)
+    for copy in copies:
+        copy.start()
     for copy in copies:
         copy.wait()
     hidden = tokens[...].astype(jnp.float32) + dot_plain(attended[...], weight[...])
@@ -221,34 +238,27 @@
     sent[:, width:] = (gates * kept[...]).astype(low)
 
 
-def attend(query, keyval, bias, tokens, small, member, kept, gain_at, pieces, spots):
+def project(attended, tokens, small, member, kept, gain_at, pieces, spots):
     rows, width = tokens.shape
-    query_width = query.shape[1]
     lanes = small.shape[0]
     low = jnp.bfloat16
-
-    def kernel(*refs):
-        attend_kernel(len(pieces), *refs[:7], gain_at, *refs[7:])
-
     return pl.pallas_call(
-        kernel,
-        in_specs=[INSIDE] * 7 + [SCALARS] + [ANYWHERE] * len(pieces),
-        out_specs=[INSIDE] * 5,
+        partial(project_kernel, len(pieces), gain_at),
+        in_specs=[SCALARS] + [INSIDE] * 5 + [ANYWHERE] * len(pieces),
+        out_specs=[INSIDE] * 3,
         out_shape=[
-            jax.ShapeDtypeStruct((rows, query_width), low),
-            jax.ShapeDtypeStruct((rows, 128), jnp.float32),
             jax.ShapeDtypeStruct((rows, width), jnp.float32),
             jax.ShapeDtypeStruct((rows, width + lanes), low),
             jax.ShapeDtypeStruct((rows, lanes), jnp.float32),
         ],
         scratch_shapes=[
-            pltpu.VMEM((query_width, width), low),
+            pltpu.VMEM((attended.shape[1], width), low),
             pltpu.SemaphoreType.DMA((len(pieces) * pieces[0].shape[0],)),
         ],
         compiler_params=pltpu.CompilerParams(vmem_limit_bytes=VMEM_BYTES),
-        cost_estimate=cost(2 * rows * width * width + 8 * rows * query_width * bias.shape[1], *pieces),
-        name="attend",
-    )(query, keyval, bias, tokens, small, member, kept, spots, *pieces)
+        cost_estimate=cost(2 * rows * width * width, *pieces),
+        name="project",
+    )(spots, attended, tokens, small, member, kept, *pieces)
 
 
 def grad_shapes(cut, rows, columns):
@@ -795,7 +805,7 @@
     return [(2 * z + c, 2 * ((z + step) % 4) + c) for z in range(4) for c in range(2)]
 
 
-def gather_blocks(rows, at_once=False):
+def gather_start(rows):
     size = lax.axis_size("expert")
     if size != 4:
         stacked = lax.all_gather(rows, "expert", axis=0)
@@ -803,15 +813,21 @@
         return [
             lax.dynamic_index_in_dim(stacked, own ^ r, axis=0, keepdims=False) for r in range(size)
         ]
-    across, along = pair_moves(size, 1), pair_moves(size, 2)
-    if at_once:
-        return [rows] + [lax.ppermute(rows, "expert", pair_moves(size, r)) for r in range(1, 4)]
-    half = rows.shape[0] // 2
-    first = lax.ppermute(rows, "expert", across)
-    second = lax.ppermute(rows, "expert", along)
-    top = lax.ppermute(second[:half], "expert", across)
-    bottom = lax.ppermute(first[half:], "expert", along)
-    return [rows, first, second, top, bottom]
+    return [rows] + [lax.ppermute(rows, "expert", pair_moves(4, r)) for r in (1, 2)]
+
+
+def gather_finish(state, events=()):
+    if lax.axis_size("expert") != 4:
+        return state
+    first, second = after(state[1:], events)
+    half = first.shape[0] // 2
+    top = lax.ppermute(second[:half], "expert", pair_moves(4, 1))
+    bottom = lax.ppermute(first[half:], "expert", pair_moves(4, 2))
+    return state + [top, bottom]
+
+
+def gather_blocks(rows):
+    return gather_finish(gather_start(rows))
 
 
 def scatter_start(parts):
@@ -872,31 +888,36 @@
     return total
 
 
-def shift_dense(rows):
+def shift_dense(rows, events):
     if not cube():
         return [lax.all_gather(rows, ("batch", "expert"), axis=0, tiled=True)]
-    below = lax.ppermute(rows, "batch", shift_moves(1))
-    above = lax.ppermute(rows, "batch", shift_moves(3))
-    return [rows, below, lax.ppermute(below, "batch", shift_moves(1)), above]
-
-
-def gather_dense(line, columns, events):
+    below, above = step_up(rows), step_down(rows)
+    return [rows, below, step_up(after(below, (above, events))), above]
+
+
+def dense_start(line, columns, events):
     found = [rows[:, columns] for rows in line]
     if not cube():
-        return [found[0][None]], jnp.zeros((1, 1), jnp.int32), (), ()
+        return [found[0][None]]
+    return gather_start(after(jnp.stack(found), events))
+
+
+def dense_finish(state, events=()):
+    if not cube():
+        return state, jnp.zeros((1, 1), jnp.int32), ()
     place = lax.axis_index("batch")
     level, core = place // 2, place % 2
     member = lax.axis_index("expert")
-    mine = gather_blocks(after(jnp.stack(found), events))
-    plane, far = mine[1:3], mine[3:]
+    mine = gather_finish(state, events)
+    far = mine[3:]
     mine = mine[:3] + [jnp.concatenate(far, axis=0)]
-    other = [lax.ppermute(block, "batch", pair_moves(8, 1)) for block in mine]
+    other = [exchange_cores(block) for block in mine]
     spots = [
         [(((level + 4 - k) % 4) * 2 + (core ^ c)) * 4 + (member ^ r) for k in range(4)]
         for c in range(2)
         for r in range(4)
     ]
-    return mine + other, jnp.array(spots, jnp.int32), plane, far
+    return mine + other, jnp.array(spots, jnp.int32), far
 
 
 def sum_chunk(packed_grad):
@@ -926,13 +947,17 @@
     return [add_low(own[r], received[r]) for r in range(4)]
 
 
-def scatter_line(plane):
+def line_start(plane):
     level = lax.axis_index("batch") // 2
     own, up, far, down = (
         lax.dynamic_index_in_dim(plane, (level + r) % 4, axis=0, keepdims=False) for r in range(4)
     )
-    forwarded = step_up(add_low(up, step_up(add_low(far))))
-    return total_of([own, forwarded, step_down(add_low(down))])
+    return own, step_down(add_low(down)), add_low(up, step_up(add_low(far)))
+
+
+def line_finish(state, events=()):
+    own, down, up = state
+    return total_of([own, down, step_up(after(up, events))])
 
 
 def scatter_whole(found):
@@ -1040,24 +1065,38 @@
         up_weight,
         down_weight,
     )
-    line = shift_dense(dense_rows)
-    grad_blocks = gather_blocks(
-        after(jnp.concatenate([grad_out, marks], axis=1), dense_rows)
-    )
-    marks_all = jnp.concatenate([block[:, width:] for block in grad_blocks], axis=0)
-    qkv_pieces, qkv_spots, plane, far = gather_dense(line, slice(0, small_width), grad_blocks)
-    out_pieces, out_spots, out_plane, _ = gather_dense(line, slice(small_width, None), far)
-    packed_all = [
-        lax.all_gather(after(packed, events), "batch", axis=0)
-        for packed, events in zip(packed_own, ((line, grad_blocks), plane))
-    ]
-
     row_ids = member_id * local_rows + jnp.arange(local_rows, dtype=jnp.int32)
     half_dim = HEAD_DIM // 2
     frequency = THETA ** (-jnp.arange(half_dim, dtype=wide) / half_dim)
     angles = place_of(row_ids).astype(wide)[:, None] * frequency[None, :]
     cosine = jnp.tile(jnp.cos(angles), (1, 4))
     sine_part = jnp.tile(jnp.concatenate([-jnp.sin(angles), jnp.sin(angles)], axis=1), (1, 2))
+    if member_count == 4:
+        away = 1 << 20
+        starts = [
+            jnp.where(member_id >= 1, 0, away),
+            jnp.where(member_id >= 2, local_rows, away),
+            member_id * local_rows,
+        ]
+    else:
+        starts = [(member_id ^ r) * local_rows for r in range(member_count)]
+    key_ids = jnp.concatenate([s + jnp.arange(local_rows, dtype=jnp.int32) for s in starts])
+    bias = jnp.where(visible(row_ids, key_ids), 0.0, -1e30).astype(wide)
+    bias_turned = bias.T
+    tables = (cosine, sine_part, bias, bias_turned)
+
+    line = shift_dense(dense_rows, tables)
+    grad_blocks = gather_blocks(after(jnp.concatenate([grad_out, marks], axis=1), dense_rows))
+    marks_all = jnp.concatenate([block[:, width:] for block in grad_blocks], axis=0)
+    qkv_state = dense_start(line, slice(0, small_width), grad_blocks)
+    plane = qkv_state[1:]
+    qkv_pieces, qkv_spots, far = dense_finish(qkv_state)
+    out_state = dense_start(line, slice(small_width, None), far)
+    packed_all = [
+        lax.all_gather(after(packed, events), "batch", axis=0)
+        for packed, events in zip(packed_own, ((line, grad_blocks), plane))
+    ]
+
     normed, query, keyval, small = enter(
         tokens[0], cosine, sine_part, qkv_pieces, qkv_spots, first_gain, query_width, kv_width
     )
@@ -1071,10 +1110,9 @@
     member = member.astype(wide)
     kept = jnp.where(before < capacity, member, 0.0)
 
-    keyval_blocks = gather_blocks(after(keyval, out_plane))
+    keyval_blocks = gather_blocks(after(keyval, out_state[1:]))
     if member_count == 4:
         ordered = keyval_blocks[:3] + [jnp.concatenate(keyval_blocks[3:], axis=0)]
-        away = 1 << 20
         keys = jnp.concatenate(
             [
                 lax.select_n(member_id, *ordered),
@@ -1083,18 +1121,12 @@
             ],
             axis=0,
         )
-        starts = [
-            jnp.where(member_id >= 1, 0, away),
-            jnp.where(member_id >= 2, local_rows, away),
-            member_id * local_rows,
-        ]
     else:
         keys = jnp.concatenate(keyval_blocks, axis=0)
-        starts = [(member_id ^ r) * local_rows for r in range(member_count)]
-    key_ids = jnp.concatenate([s + jnp.arange(local_rows, dtype=jnp.int32) for s in starts])
-    bias = jnp.where(visible(row_ids, key_ids), 0.0, -1e30).astype(wide)
-    attended, log_totals, residual, sent, gate_rows = attend(
-        query, keys, bias, tokens[0], small, member, kept, second_gain, out_pieces, out_spots
+    attended, log_totals = attend(query, keys, bias)
+    out_pieces, out_spots, _ = dense_finish(out_state, keyval_blocks[3:])
+    residual, sent, gate_rows = project(
+        attended, tokens[0], small, member, kept, second_gain, out_pieces, out_spots
     )
     sent_blocks = gather_blocks(sent)
 
@@ -1122,9 +1154,10 @@
         own, rest, far, near = chunk_grads[1]
         far, near = exchange_cores(far), exchange_cores(near)
         far_sum, down_sum = add_low(rest[1], far[0]), add_low(rest[2], far[1])
-    normed_grad = scatter_blocks(blocks_of(row_grad))
+    turn_state = scatter_start(blocks_of(row_grad))
     if cut:
-        normed_grad = after(normed_grad, (far_sum, down_sum))
+        turn_state = after(turn_state, (far_sum, down_sum))
+    normed_grad = scatter_finish(turn_state)
     turned = turn(
         place,
         out_spots,
@@ -1149,7 +1182,7 @@
     if cut:
         up_sum = add_low(rest[0], near[0], step_up(far_sum))
     query_grad, key_grads = attend_back(
-        head_grad, query, keys, bias.T, log_totals, cosine, sine_part
+        head_grad, query, keys, bias_turned, log_totals, cosine, sine_part
     )
     if member_count == 4:
         zero = jnp.zeros((), low)
@@ -1195,14 +1228,17 @@
         up_term = step_up(up_sum)
         qkv_parts = join_cores(qkv_found[1], after(received, out_plane))
         qkv_plane = after(scatter_blocks(qkv_parts), up_term)
-        out_sum = scatter_line(out_plane)
-        qkv_sum = scatter_line(qkv_plane)
+        out_sum = line_finish(line_start(out_plane))
+        qkv_state = line_start(qkv_plane)
         terms = [[totals[0][0]], after([own, near[1], down_term, up_term], qkv_plane)]
+        expert_totals = unpack(terms, gate_weight.shape, down_weight.shape)
+        qkv_sum = line_finish(qkv_state, expert_totals)
     else:
         out_sum = scatter_whole(out_found)
         qkv_sum = scatter_whole(qkv_found)
         terms = [[totals[0][0]]] + [[sum_chunk(found[0])[0]] for found in chunk_grads[1:]]
-    gate_total, up_total, down_total = unpack(terms, gate_weight.shape, down_weight.shape)
+        expert_totals = unpack(terms, gate_weight.shape, down_weight.shape)
+    gate_total, up_total, down_total = expert_totals
     return (
         result[None],
         input_grad[None],

time: 572 us -> 565 us (0.988)
  waiting for transfers between devices: 211 us -> 199 us
    ppermute x31 -> x20, waiting for transfers between devices: 117 us -> 92.9 us  [the longest x10 69.9 us: gather_start(): lax.ppermute(rows, 'expert', pair_moves(4, r))]
    ppermute x3, waiting for transfers between devices: 0.01 us -> 12 us  [send_parts(): lax.ppermute(parts[r].astype(low), 'expert', pair_moves(4, r))]
    ppermute x4, waiting for transfers between devices: 17.4 us -> 26.8 us  [scatter_start(): bottom = lax.ppermute(parts[3][half:].astype(low), 'expert', along)]
    ppermute x4, waiting for transfers between devices: 10.5 us -> 1.62 us  [scatter_start(): top = lax.ppermute(parts[3][:half].astype(low), 'expert', across)]
    ppermute x31 -> x20, starting transfers between devices: 28.1 us -> 20.1 us  [the longest x10 10.8 us: gather_start(): lax.ppermute(rows, 'expert', pair_moves(4, r))]
    ppermute x4, waiting for transfers between devices: 4.58 us -> 10.5 us  [scatter_finish(): second_top = lax.ppermute(for_second, 'expert', pair_moves(4, 2))]
    pallas_call x1 -> x2, Pallas kernels: 17.2 us -> 21.4 us  [the longest x1 13.8 us: attend(): pl.pallas_call(attend_kernel, in_specs=[INSIDE] * 3, out_specs=[INSIDE] *...]
    ppermute x6 -> x8, waiting for transfers between devices: 19.3 us -> 18.2 us  [step_up(): return lax.ppermute(values, 'batch', shift_moves(1))]
  transfers between devices with their start and end apart: 74 -> 74, of which waited for: 35 -> 39; matrix products, arithmetic and copies ran while one was open for 11% -> 12% of each run, Pallas kernels for 33% -> 34%
where the time goes in v1:
time: 565 us; the launch traced here: 557 us
  waiting for transfers between devices  199 us (35%)
  Pallas kernels  195 us (35%)
  starting transfers between devices  67.2 us (12%)
  local copies, waits for them, and re-layouts  41.1 us (7%)
  other arithmetic  39 us (7%)
  between operations  15 us (3%)
    pallas_call x2, Pallas kernels, expert_pass(): pl.pallas_call(partial(expert_kernel, cut, carried, last, len(rows), len(...  108 us
    ppermute x10, waiting for transfers between devices, gather_start(): lax.ppermute(rows, 'expert', pair_moves(4, r))  69.9 us
    ppermute x4, waiting for transfers between devices, scatter_start(): bottom = lax.ppermute(parts[3][half:].astype(low), 'expert', along)  26.8 us
    pallas_call x1, Pallas kernels, attend_back(): pl.pallas_call(attend_back_kernel, in_specs=[INSIDE] * 7, out_specs=[INSI...  21.3 us
    ppermute x5, waiting for transfers between devices, gather_finish(): top = lax.ppermute(second[:half], 'expert', pair_moves(4, 1))  18.6 us
    ppermute x8, waiting for transfers between devices, step_up(): return lax.ppermute(values, 'batch', shift_moves(1))  18.2 us
    convert_element_type x14, other arithmetic, add_low(): return total.astype(jnp.bfloat16)  17.7 us
    ppermute x4, waiting for transfers between devices, scatter_start(): first_top = lax.ppermute(parts[1][:half].astype(low), 'expert', across)  17 us
  transfers between devices with their start and end apart: 74, of which 39 were waited for; matrix products, arithmetic and copies ran while one was open for 12% of the time, Pallas kernels for 34%

profile of v1, /device:TPU:0, one launch (start us, length us, event | category | flops | bytes accessed | tf_op | source)
XLA Modules:
  0.0 557.3 jit_solution(1188577030498135720)
XLA Ops:
  26.7 14.3 %collective-permute-done.3.refs_6_ = bf16[256,1664]{1,0:T(8,128)(2,1)S(1)} collective-permute-done((bf16[256,1664]{1,0:T(8,128)(2,1)S(1)}, bf16[256,1664]{1,0:T(8,128)(2,1)S(1)}, u32[]{:S(2)}, u32[]{:S(2)}) %collective-permute-start.3) | collective-permute-done | bytes 852000 | tf_op jit(solution)/shard_map/ppermute | solution.py:816
  45.2 10.9 %collective-permute-done.2 = bf16[48,4224]{1,0:T(8,128)(2,1)S(1)} collective-permute-done((bf16[48,4224]{1,0:T(8,128)(2,1)}, bf16[48,4224]{1,0:T(8,128)(2,1)S(1)}, u32[]{:S(2)}, u32[]{:S(2)}) %collective-permute-start.2) | collective-permute-done | bytes 405536 | tf_op jit(solution)/shard_map/ppermute | solution.py:932
  63.0 19.4 %collective-permute-done.7.refs_1_ = bf16[4,48,2688]{2,1,0:T(8,128)(2,1)S(1)} collective-permute-done((bf16[4,48,2688]{2,1,0:T(8,128)(2,1)S(1)}, bf16[4,48,2688]{2,1,0:T(8,128)(2,1)S(1)}, u32[]{:S(2)}, u32[]{:S(2)}) %collective-permute-start.7) | collective-permute-done | bytes 1032224 | tf_op jit(solution)/shard_map/ppermute | solution.py:816
  105.5 8.2 %enter.1 = (bf16[256,1536]{1,0:T(8,128)(2,1)}, bf16[256,1536]{1,0:T(8,128)(2,1)}, bf16[256,1024]{1,0:T(8,128)(2,1)}, f32[128,1536]{1,0:T(8,128)}) custom-call(s32[8,4]{1,0:T(8,128)} %concatenate.91.spots, bf16[256,1536]{1,0:T(8,128)(2,1)} %bitcast.180, f32[256,128]{1,0:T(8,128)} %copy.57.cosine, f32[256,128]{1,0:T(8,128)} %copy.58.sine, ...), custom_call_target="tpu_custom_call" | custom-call | flops 1 | bytes 1 | tf_op jit(solution)/shard_map/enter/pallas_call | solution.py:137
  121.3 9.6 %collective-permute-done.17 = bf16[256,1024]{1,0:T(8,128)(2,1)S(1)} collective-permute-done((bf16[256,1024]{1,0:T(8,128)(2,1)}, bf16[256,1024]{1,0:T(8,128)(2,1)S(1)}, u32[]{:S(2)}, u32[]{:S(2)}) %collective-permute-start.17) | collective-permute-done | bytes 524320 | tf_op jit(solution)/shard_map/ppermute | solution.py:816
  150.1 13.8 %attend.1 = (bf16[256,1536]{1,0:T(8,128)(2,1)}, f32[256,128]{1,0:T(8,128)}) custom-call(bf16[256,1536]{1,0:T(8,128)(2,1)} %get-tuple-element.90.query, bf16[768,1024]{1,0:T(8,128)(2,1)} %pad_maximum_fusion.3.keyval, f32[256,768]{1,0:T(8,128)} %and_select_fusion.1.bias), custom_call_target="tpu_custom_call" | custom-call | flops 1 | bytes 1 | tf_op jit(solution)/shard_map/attend/pallas_call | solution.py:203
  164.7 7.6 %project.1 = (f32[256,1536]{1,0:T(8,128)}, bf16[256,1664]{1,0:T(8,128)(2,1)}, f32[256,128]{1,0:T(8,128)}) custom-call(s32[8,4]{1,0:T(8,128)} %concatenate.91.spots, bf16[256,1536]{1,0:T(8,128)(2,1)} %get-tuple-element.96.attended, bf16[256,1536]{1,0:T(8,128)(2,1)} %bitcast.181, f32[128,1536]{1,0:T(8,128)} %get-tuple-element.97.small, ...), custom_call_target="tpu_custom_call" | custom-call | flops 1 | bytes 1 | tf_op jit(solution)/shard_map/project/pallas_call | solution.py:245
  174.5 19.0 %collective-permute-done.27.refs_1_ = bf16[256,1664]{1,0:T(8,128)(2,1)S(1)} collective-permute-done((bf16[256,1664]{1,0:T(8,128)(2,1)}, bf16[256,1664]{1,0:T(8,128)(2,1)S(1)}, u32[]{:S(2)}, u32[]{:S(2)}) %collective-permute-start.27) | collective-permute-done | bytes 852000 | tf_op jit(solution)/shard_map/ppermute | solution.py:816
  197.0 8.3 %collective-permute-done.29.refs_3_ = bf16[128,1664]{1,0:T(8,128)(2,1)} collective-permute-done((bf16[128,1664]{1,0:T(8,128)(2,1)S(1)}, bf16[128,1664]{1,0:T(8,128)(2,1)}, u32[]{:S(2)}, u32[]{:S(2)}) %collective-permute-start.29) | collective-permute-done | bytes 426016 | tf_op jit(solution)/shard_map/ppermute | solution.py:824
  205.8 62.6 %experts.2 = (bf16[8,3,3,64,1536]{4,3,2,1,0:T(8,128)(2,1)}, f32[1024,1536]{1,0:T(8,128)}, f32[1024,1664]{1,0:T(8,128)}) custom-call(s32[3]{0:T(128)} %pad_add_fusion.1.place, s32[1]{0:T(128)} %bitcast.61.first, bf16[8,3,3,64,1536]{4,3,2,1,0:T(8,128)(2,1)} %bitcast.178, bf16[256,1664]{1,0:T(8,128)(2,1)} %get-tuple-element.103.refs_0_.normed, ...), custom_call_target="tpu_custom_call" | custom-call | flops 1 | bytes 1 | tf_op jit(solution)/shard_map/experts/pallas_call | solution.py:727
  268.4 6.7 %all-gather.5.cloned.1.call-done = bf16[24,2,64,1536]{3,2,1,0:T(8,128)(2,1)} async-done(((bf16[3,2,64,1536]{3,2,1,0:T(8,128)(2,1)}), bf16[24,2,64,1536]{3,2,1,0:T(8,128)(2,1)}) %all-gather.5.cloned.1.call-update) | async-done | bytes 9437200 | tf_op jit(solution)/shard_map/all_gather | solution.py:1096
  275.1 45.5 %experts.3 = (bf16[3,2,64,1536]{3,2,1,0:T(8,128)(2,1)}, bf16[3,3,2,64,1536]{4,3,2,1,0:T(8,128)(2,1)}, bf16[2,3,2,64,1536]{4,3,2,1,0:T(8,128)(2,1)}, bf16[2,3,2,6...) custom-call(s32[3]{0:T(128)} %pad_add_fusion.1.place, s32[1]{0:T(128)} %bitcast.59.first, ...), custom_call_target="tpu_custom_call" | custom-call | flops 1 | bytes 1 | tf_op jit(solution)/shard_map/experts/pallas_call | solution.py:727
  326.9 8.5 %collective-permute-done.33 = bf16[128,1664]{1,0:T(8,128)(2,1)S(1)} collective-permute-done((bf16[128,1664]{1,0:T(8,128)(2,1)S(1)}, bf16[128,1664]{1,0:T(8,128)(2,1)S(1)}, u32[]{:S(2)}, u32[]{:S(2)}) %collective-permute-start.33) | collective-permute-done | bytes 426016 | tf_op jit(solution)/shard_map/ppermute | solution.py:843
  339.7 5.3 collective-permute-done.31
  347.0 9.2 %collective-permute-done.36 = bf16[128,1664]{1,0:T(8,128)(2,1)} collective-permute-done((bf16[128,1664]{1,0:T(8,128)(2,1)}, bf16[128,1664]{1,0:T(8,128)(2,1)}, u32[]{:S(2)}, u32[]{:S(2)}) %collective-permute-start.36) | collective-permute-done | bytes 426016 | tf_op jit(solution)/shard_map/ppermute | solution.py:856
  359.0 11.5 %turn.1 = (bf16[4,4,48,1664]{3,2,1,0:T(8,128)(2,1)}, bf16[4,4,48,1664]{3,2,1,0:T(8,128)(2,1)}, f32[256,1536]{1,0:T(8,128)}, bf16[256,1536]{1,0:T(8,128)(2,1)}) custom-call(s32[3]{0:T(128)} %pad_add_fusion.1.place, s32[8,4]{1,0:T(8,128)} %concatenate.91.spots, f32[256,1664]{1,0:T(8,128)} %pad_maximum_fusion.2.normed_grad, ...), custom_call_target="tpu_custom_call" | custom-call | flops 1 | bytes 1 | tf_op jit(solution)/shard_map/turn/pallas_call | solution.py:370
  376.5 21.3 %attend_back.1 = (bf16[256,1536]{1,0:T(8,128)(2,1)}, bf16[768,1024]{1,0:T(8,128)(2,1)}) custom-call(bf16[256,1536]{1,0:T(8,128)(2,1)} %get-tuple-element.121.head_grad, bf16[256,1536]{1,0:T(8,128)(2,1)} %get-tuple-element.90.query, bf16[768,1024]{1,0:T(8,128)(2,1)} %pad_maximum_fusion.3.keyval, f32[768,256]{1,0:T(8,128)} %and_select_fusion.bias, ...), custom_call_target="tpu_custom_call" | custom-call | flops 1 | bytes 1 | tf_op jit(solution)/shard_map/attend_back/pallas_call | solution.py:445
  406.0 12.0 %collective-permute-done.40 = bf16[256,1536]{1,0:T(8,128)(2,1)S(1)} collective-permute-done((bf16[256,1536]{1,0:T(8,128)(2,1)S(1)}, bf16[256,1536]{1,0:T(8,128)(2,1)S(1)}, u32[]{:S(2)}, u32[]{:S(2)}) %collective-permute-start.40) | collective-permute-done | bytes 786464 | tf_op jit(solution)/shard_map/ppermute | solution.py:880
  422.3 5.0 collective-permute-done.46
  447.0 15.3 %leave.1 = (bf16[4,4,48,2688]{3,2,1,0:T(8,128)(2,1)}, bf16[4,4,48,2688]{3,2,1,0:T(8,128)(2,1)}, f32[256,1536]{1,0:T(8,128)}) custom-call(s32[3]{0:T(128)} %pad_add_fusion.1.place, s32[8,4]{1,0:T(8,128)} %concatenate.91.spots, f32[256,1024]{1,0:T(8,128)} %pad_maximum_fusion.4.keyval_sum, bf16[256,1536]{1,0:T(8,128)(2,1)} %get-tuple-element.132.query_grad, ...), custom_call_target="tpu_custom_call" | custom-call | flops 1 | bytes 1 | tf_op jit(solution)/shard_map/leave/pallas_call | solution.py:530
  482.1 13.3 %collective-permute-done.61 = bf16[2,48,2688]{2,1,0:T(8,128)(2,1)S(1)} collective-permute-done((bf16[2,48,2688]{2,1,0:T(8,128)(2,1)S(1)}, bf16[2,48,2688]{2,1,0:T(8,128)(2,1)S(1)}, u32[]{:S(2)}, u32[]{:S(2)}) %collective-permute-start.61) | collective-permute-done | bytes 516128 | tf_op jit(solution)/shard_map/ppermute | solution.py:843
  502.5 7.7 %collective-permute-done.58 = bf16[2,48,2688]{2,1,0:T(8,128)(2,1)S(1)} collective-permute-done((bf16[2,48,2688]{2,1,0:T(8,128)(2,1)S(1)}, bf16[2,48,2688]{2,1,0:T(8,128)(2,1)S(1)}, u32[]{:S(2)}, u32[]{:S(2)}) %collective-permute-start.58) | collective-permute-done | bytes 516128 | tf_op jit(solution)/shard_map/ppermute | solution.py:844
  514.0 5.6 %collective-permute-done.62 = bf16[2,48,2688]{2,1,0:T(8,128)(2,1)S(1)} collective-permute-done((bf16[2,48,2688]{2,1,0:T(8,128)(2,1)S(1)}, bf16[2,48,2688]{2,1,0:T(8,128)(2,1)S(1)}, u32[]{:S(2)}, u32[]{:S(2)}) %collective-permute-start.62) | collective-permute-done | bytes 516128 | tf_op jit(solution)/shard_map/ppermute | solution.py:857
  530.0 5.7 %unpack.1 = (f32[5,192,512]{2,1,0:T(8,128)}, f32[5,192,512]{2,1,0:T(8,128)}, f32[5,64,1536]{2,1,0:T(8,128)}) custom-call(bf16[3,3,64,1536]{3,2,1,0:T(8,128)(2,1)} %bitcast.185, bf16[3,2,64,1536]{3,2,1,0:T(8,128)(2,1)} %get-tuple-element.144.refs_1_, bf16[3,2,64,1536]{3,2,1,0:T(8,128)(2,1)} %slice_bitcast_fusion.refs_2_, ...), custom_call_target="tpu_custom_call" | custom-call | flops 1 | bytes 1 | tf_op jit(solution)/shard_map/unpack/pallas_call | solution.py:781
  (311 shorter events, 196.2 us)
Async XLA Ops:
  7.2 198.6 %all-gather.7.cloned.1.call-start = ((), (), s32[]{:S(2)}) async-start(), calls=%async_computation.3 | async-start | bytes 15925248 | tf_op jit(solution)/shard_map/all_gather | solution.py:1096
  14.2 30.3 %collective-permute-start = (bf16[48,4224]{1,0:T(8,128)(2,1)}, bf16[48,4224]{1,0:T(8,128)(2,1)}, u32[]{:S(2)}, u32[]{:S(2)}) collective-permute-start(bf16[48,4224]{1,0:T(8,128)(2,1)} %get-tuple-element.82), channel_id=1, source_target_pairs={{0,8},{4,12},{8,16},{12,20},{16,24},{20,28},{24,0},{28,4},{1,9},{5... | collective-permute-start | bytes 1216520 | tf_op jit(solution)/shard_map/ppermute | solution.py:932
  17.2 27.3 %collective-permute-start.1 = (bf16[48,4224]{1,0:T(8,128)(2,1)}, bf16[48,4224]{1,0:T(8,128)(2,1)}, u32[]{:S(2)}, u32[]{:S(2)}) collective-permute-start(bf16[48,4224]{1,0:T(8,128)(2,1)} %get-tuple-element.82), channel_id=1, source_target_pairs={{0,24},{4,28},{8,0},{12,4},{16,8},{20,12},{24,16},{28,20},{1,25},{... | collective-permute-start | bytes 1216520 | tf_op jit(solution)/shard_map/ppermute | solution.py:936
  56.9 218.2 %all-gather.5.cloned.1.call-start = ((), (), s32[]{:S(2)}) async-start(), calls=%async_computation.2 | async-start | bytes 10616832 | tf_op jit(solution)/shard_map/all_gather | solution.py:1096
  61.1 21.4 %collective-permute-start.7 = (bf16[4,48,2688]{2,1,0:T(8,128)(2,1)S(1)}, bf16[4,48,2688]{2,1,0:T(8,128)(2,1)S(1)}, u32[]{:S(2)}, u32[]{:S(2)}) collective-permute-start(bf16[4,48,2688]{2,1,0:T(8,128)(2,1)S(1)} %pad_maximum_fusion.5.refs_0_), channel_id=1, source_target_pairs={{0,1},{1,0},{2,3},{3,2},{4,5},{5,4},{6,7},{7,6},{8,9},{9,8},{10,11... | collective-permute-start | bytes 3096584 | tf_op jit(solution)/shard_map/ppermute | solution.py:816
  62.5 21.2 %collective-permute-start.8 = (bf16[4,48,2688]{2,1,0:T(8,128)(2,1)S(1)}, bf16[4,48,2688]{2,1,0:T(8,128)(2,1)}, u32[]{:S(2)}, u32[]{:S(2)}) collective-permute-start(bf16[4,48,2688]{2,1,0:T(8,128)(2,1)S(1)} %pad_maximum_fusion.5.refs_0_), channel_id=1, source_target_pairs={{0,2},{1,3},{2,0},{3,1},{4,6},{5,7},{6,4},{7,5},{8,10},{9,11},{10,... | collective-permute-start | bytes 3096584 | tf_op jit(solution)/shard_map/ppermute | solution.py:816
  83.8 383.9 %reduce-scatter.2.cloned.1.call-start = ((), (), s32[]{:S(2)}) async-start(), calls=%async_computation.1 | async-start | bytes 15925248 | tf_op jit(solution)/shard_map/reduce_scatter | solution.py:924
  172.4 21.1 %collective-permute-start.27 = (bf16[256,1664]{1,0:T(8,128)(2,1)}, bf16[256,1664]{1,0:T(8,128)(2,1)S(1)}, u32[]{:S(2)}, u32[]{:S(2)}) collective-permute-start(bf16[256,1664]{1,0:T(8,128)(2,1)} %get-tuple-element.103.refs_0_.normed), channel_id=1, source_target_pairs={{0,1},{1,0},{2,3},{3,2},{4,5},{5,4},{6,7},{7,6},{8,9},{9,8},{10,11... | collective-permute-start | bytes 2555912 | tf_op jit(solution)/shard_map/ppermute | solution.py:816
  335.3 62.4 %collective-permute-start.41 = (bf16[2,3,2,64,1536]{4,3,2,1,0:T(8,128)(2,1)}, bf16[2,3,2,64,1536]{4,3,2,1,0:T(8,128)(2,1)}, u32[]{:S(2)}, u32[]{:S(2)}) collective-permute-start(bf16[2,3,2,64,1536]{4,3,2,1,0:T(8,128)(2,1)} %get-tuple-element.124), channel_id=1, source_target_pairs={{0,4},{4,0},{8,12},{12,8},{16,20},{20,16},{24,28},{28,24},{1,5},{5... | collective-permute-start | bytes 7077896 | tf_op jit(solution)/shard_map/ppermute | solution.py:928
  347.0 55.4 %collective-permute-start.42 = (bf16[3,2,64,1536]{3,2,1,0:T(8,128)(2,1)S(1)}, bf16[3,2,64,1536]{3,2,1,0:T(8,128)(2,1)}, u32[]{:S(2)}, u32[]{:S(2)}) collective-permute-start(bf16[3,2,64,1536]{3,2,1,0:T(8,128)(2,1)S(1)} %get-tuple-element.205), channel_id=1, source_target_pairs={{0,8},{4,12},{8,16},{12,20},{16,24},{20,28},{24,0},{28,4},{1,9},{5... | collective-permute-start | bytes 3538952 | tf_op jit(solution)/shard_map/ppermute | solution.py:932
  370.5 67.9 %collective-permute-start.49 = (bf16[4,4,48,1664]{3,2,1,0:T(8,128)(2,1)}, bf16[4,4,48,1664]{3,2,1,0:T(8,128)(2,1)}, u32[]{:S(2)}, u32[]{:S(2)}) collective-permute-start(bf16[4,4,48,1664]{3,2,1,0:T(8,128)(2,1)} %get-tuple-element.130), channel_id=1, source_target_pairs={{0,4},{4,0},{8,12},{12,8},{16,20},{20,16},{24,28},{28,24},{1,5},{5... | collective-permute-start | bytes 7667720 | tf_op jit(solution)/shard_map/ppermute | solution.py:928
  373.5 32.5 %collective-permute-start.38 = (bf16[256,1536]{1,0:T(8,128)(2,1)}, bf16[256,1536]{1,0:T(8,128)(2,1)}, u32[]{:S(2)}, u32[]{:S(2)}) collective-permute-start(bf16[256,1536]{1,0:T(8,128)(2,1)} %get-tuple-element.216), channel_id=1, source_target_pairs={{0,1},{1,0},{2,3},{3,2},{4,5},{5,4},{6,7},{7,6},{8,9},{9,8},{10,11... | collective-permute-start | bytes 2359304 | tf_op jit(solution)/shard_map/ppermute | solution.py:880
  375.1 30.9 %collective-permute-start.39 = (bf16[256,1536]{1,0:T(8,128)(2,1)}, bf16[256,1536]{1,0:T(8,128)(2,1)}, u32[]{:S(2)}, u32[]{:S(2)}) collective-permute-start(bf16[256,1536]{1,0:T(8,128)(2,1)} %get-tuple-element.218), channel_id=1, source_target_pairs={{0,2},{1,3},{2,0},{3,1},{4,6},{5,7},{6,4},{7,5},{8,10},{9,11},{10,... | collective-permute-start | bytes 2359304 | tf_op jit(solution)/shard_map/ppermute | solution.py:880
  433.6 34.1 %collective-permute-start.54 = (bf16[3,2,64,1536]{3,2,1,0:T(8,128)(2,1)}, bf16[3,2,64,1536]{3,2,1,0:T(8,128)(2,1)}, u32[]{:S(2)}, u32[]{:S(2)}) collective-permute-start(bf16[3,2,64,1536]{3,2,1,0:T(8,128)(2,1)} %get-tuple-element.139), channel_id=1, source_target_pairs={{0,24},{4,28},{8,0},{12,4},{16,8},{20,12},{24,16},{28,20},{1,25},{... | collective-permute-start | bytes 3538952 | tf_op jit(solution)/shard_map/ppermute | solution.py:936
  441.5 20.9 %collective-permute-start.53 = (bf16[2,48,1664]{2,1,0:T(8,128)(2,1)}, bf16[2,48,1664]{2,1,0:T(8,128)(2,1)}, u32[]{:S(2)}, u32[]{:S(2)}) collective-permute-start(bf16[2,48,1664]{2,1,0:T(8,128)(2,1)} %get-tuple-element.237), channel_id=1, source_target_pairs={{0,1},{1,0},{2,3},{3,2},{4,5},{5,4},{6,7},{7,6},{8,9},{9,8},{10,11... | collective-permute-start | bytes 958472 | tf_op jit(solution)/shard_map/ppermute | solution.py:842
  442.1 22.3 %collective-permute-start.52 = (bf16[2,48,1664]{2,1,0:T(8,128)(2,1)S(1)}, bf16[2,48,1664]{2,1,0:T(8,128)(2,1)}, u32[]{:S(2)}, u32[]{:S(2)}) collective-permute-start(bf16[2,48,1664]{2,1,0:T(8,128)(2,1)S(1)} %get-tuple-element.238), channel_id=1, source_target_pairs={{0,2},{1,3},{2,0},{3,1},{4,6},{5,7},{6,4},{7,5},{8,10},{9,11},{10,... | collective-permute-start | bytes 958472 | tf_op jit(solution)/shard_map/ppermute | solution.py:843
  444.3 23.4 %collective-permute-start.50 = (bf16[2,48,1664]{2,1,0:T(8,128)(2,1)}, bf16[2,48,1664]{2,1,0:T(8,128)(2,1)}, u32[]{:S(2)}, u32[]{:S(2)}) collective-permute-start(bf16[2,48,1664]{2,1,0:T(8,128)(2,1)} %slice_bitcast_fusion.16), channel_id=1, source_target_pairs={{0,1},{1,0},{2,3},{3,2},{4,5},{5,4},{6,7},{7,6},{8,9},{9,8},{10,11... | collective-permute-start | bytes 958472 | tf_op jit(solution)/shard_map/ppermute | solution.py:844
  446.4 21.2 %collective-permute-start.51 = (bf16[2,48,1664]{2,1,0:T(8,128)(2,1)}, bf16[2,48,1664]{2,1,0:T(8,128)(2,1)}, u32[]{:S(2)}, u32[]{:S(2)}) collective-permute-start(bf16[2,48,1664]{2,1,0:T(8,128)(2,1)} %slice_bitcast_fusion.15), channel_id=1, source_target_pairs={{0,2},{1,3},{2,0},{3,1},{4,6},{5,7},{6,4},{7,5},{8,10},{9,11},{10,... | collective-permute-start | bytes 958472 | tf_op jit(solution)/shard_map/ppermute | solution.py:845
  470.2 51.3 %collective-permute-start.64 = (bf16[3,2,64,1536]{3,2,1,0:T(8,128)(2,1)}, bf16[3,2,64,1536]{3,2,1,0:T(8,128)(2,1)S(1)}, u32[]{:S(2)}, u32[]{:S(2)}) collective-permute-start(bf16[3,2,64,1536]{3,2,1,0:T(8,128)(2,1)} %fusion), channel_id=1, source_target_pairs={{0,8},{4,12},{8,16},{12,20},{16,24},{20,28},{24,0},{28,4},{1,9},{5... | collective-permute-start | bytes 3538952 | tf_op jit(solution)/shard_map/ppermute | solution.py:932
  474.7 24.1 %collective-permute-start.56 = (bf16[2,48,1664]{2,1,0:T(8,128)(2,1)S(1)}, bf16[2,48,1664]{2,1,0:T(8,128)(2,1)S(1)}, u32[]{:S(2)}, u32[]{:S(2)}) collective-permute-start(bf16[2,48,1664]{2,1,0:T(8,128)(2,1)S(1)} %copy-done.25), channel_id=1, source_target_pairs={{0,2},{1,3},{2,0},{3,1},{4,6},{5,7},{6,4},{7,5},{8,10},{9,11},{10,... | collective-permute-start | bytes 958472 | tf_op jit(solution)/shard_map/ppermute | solution.py:856
  476.2 23.2 %collective-permute-start.57 = (bf16[2,48,1664]{2,1,0:T(8,128)(2,1)S(1)}, bf16[2,48,1664]{2,1,0:T(8,128)(2,1)S(1)}, u32[]{:S(2)}, u32[]{:S(2)}) collective-permute-start(bf16[2,48,1664]{2,1,0:T(8,128)(2,1)S(1)} %fusion.14), channel_id=1, source_target_pairs={{0,1},{1,0},{2,3},{3,2},{4,5},{5,4},{6,7},{7,6},{8,9},{9,8},{10,11... | collective-permute-start | bytes 958472 | tf_op jit(solution)/shard_map/ppermute | solution.py:857
  498.8 20.9 %collective-permute-start.62 = (bf16[2,48,2688]{2,1,0:T(8,128)(2,1)S(1)}, bf16[2,48,2688]{2,1,0:T(8,128)(2,1)S(1)}, u32[]{:S(2)}, u32[]{:S(2)}) collective-permute-start(bf16[2,48,2688]{2,1,0:T(8,128)(2,1)S(1)} %fusion.6), channel_id=1, source_target_pairs={{0,1},{1,0},{2,3},{3,2},{4,5},{5,4},{6,7},{7,6},{8,9},{9,8},{10,11... | collective-permute-start | bytes 1548296 | tf_op jit(solution)/shard_map/ppermute | solution.py:857
  499.4 21.7 %collective-permute-start.60 = (bf16[2,48,2688]{2,1,0:T(8,128)(2,1)S(1)}, bf16[2,48,2688]{2,1,0:T(8,128)(2,1)S(1)}, u32[]{:S(2)}, u32[]{:S(2)}) collective-permute-start(bf16[2,48,2688]{2,1,0:T(8,128)(2,1)S(1)} %fusion.8), channel_id=1, source_target_pairs={{0,2},{1,3},{2,0},{3,1},{4,6},{5,7},{6,4},{7,5},{8,10},{9,11},{10,... | collective-permute-start | bytes 1548296 | tf_op jit(solution)/shard_map/ppermute | solution.py:856
  511.8 25.1 %collective-permute-start.68 = (bf16[48,1664]{1,0:T(8,128)(2,1)}, bf16[48,1664]{1,0:T(8,128)(2,1)S(1)}, u32[]{:S(2)}, u32[]{:S(2)}) collective-permute-start(bf16[48,1664]{1,0:T(8,128)(2,1)} %get-tuple-element.227), channel_id=1, source_target_pairs={{0,24},{4,28},{8,0},{12,4},{16,8},{20,12},{24,16},{28,20},{1,25},{... | collective-permute-start | bytes 479240 | tf_op jit(solution)/shard_map/ppermute | solution.py:936
  (80 other events, 1043.3 us)
Sparse Core Ops, SparseCore 0:
  57.0 126.8 all-gather.6
  186.1 88.9 all-gather.4
  277.4 176.5 reduce-scatter.1

commit v2 on v1

--- a/solution.py
+++ b/solution.py
@@ -752,8 +752,9 @@
     return found[:outs], found[outs], found[outs + 1]
 
 
-def unpack_kernel(counts, *refs):
+def unpack_kernel(counts, places, *refs):
     found, (gate, up, down) = refs[:-3], refs[-3:]
+    found = [array if place is None else array.at[place] for array, place in zip(found, places)]
     hidden_width = gate.shape[2]
     base = 0
     at = 0
@@ -777,9 +778,10 @@
 
 
 def unpack(chunks, gate_shape, down_shape):
-    arrays = [term for terms in chunks for term in terms]
+    arrays = [array for terms in chunks for array, _ in terms]
+    places = [place for terms in chunks for _, place in terms]
     return pl.pallas_call(
-        partial(unpack_kernel, [len(terms) for terms in chunks]),
+        partial(unpack_kernel, [len(terms) for terms in chunks], places),
         in_specs=[INSIDE] * len(arrays),
         out_specs=[INSIDE] * 3,
         out_shape=[
@@ -902,7 +904,7 @@
     return gather_start(after(jnp.stack(found), events))
 
 
-def dense_finish(state, events=()):
+def dense_finish(state, events=(), late=()):
     if not cube():
         return state, jnp.zeros((1, 1), jnp.int32), ()
     place = lax.axis_index("batch")
@@ -910,7 +912,7 @@
     member = lax.axis_index("expert")
     mine = gather_finish(state, events)
     far = mine[3:]
-    mine = mine[:3] + [jnp.concatenate(far, axis=0)]
+    mine = mine[:3] + [after(jnp.concatenate(far, axis=0), late)]
     other = [exchange_cores(block) for block in mine]
     spots = [
         [(((level + 4 - k) % 4) * 2 + (core ^ c)) * 4 + (member ^ r) for k in range(4)]
@@ -1086,9 +1088,10 @@
     tables = (cosine, sine_part, bias, bias_turned)
 
     line = shift_dense(dense_rows, tables)
-    grad_blocks = gather_blocks(after(jnp.concatenate([grad_out, marks], axis=1), dense_rows))
+    grad_state = gather_start(jnp.concatenate([grad_out, marks], axis=1))
+    grad_blocks = gather_finish(grad_state, line[1::2])
     marks_all = jnp.concatenate([block[:, width:] for block in grad_blocks], axis=0)
-    qkv_state = dense_start(line, slice(0, small_width), grad_blocks)
+    qkv_state = dense_start(line, slice(0, small_width), ())
     plane = qkv_state[1:]
     qkv_pieces, qkv_spots, far = dense_finish(qkv_state)
     out_state = dense_start(line, slice(small_width, None), far)
@@ -1124,7 +1127,7 @@
     else:
         keys = jnp.concatenate(keyval_blocks, axis=0)
     attended, log_totals = attend(query, keys, bias)
-    out_pieces, out_spots, _ = dense_finish(out_state, keyval_blocks[3:])
+    out_pieces, out_spots, _ = dense_finish(out_state, keyval_blocks[3:], attended)
     residual, sent, gate_rows = project(
         attended, tokens[0], small, member, kept, second_gain, out_pieces, out_spots
     )
@@ -1180,7 +1183,8 @@
     resid_grad, head_grad = turned[-2:]
     mixture_parts = send_parts(blocks_of(after(mixture_all, normed_grad)))
     if cut:
-        up_sum = add_low(rest[0], near[0], step_up(far_sum))
+        head_grad = after(head_grad, mixture_parts[1:3])
+        up_part = step_up(far_sum)
     query_grad, key_grads = attend_back(
         head_grad, query, keys, bias_turned, log_totals, cosine, sine_part
     )
@@ -1196,12 +1200,14 @@
         key_parts = blocks_of(key_grads)
     if cut:
         out_found = out_found[1], exchange_cores(out_found[0])
-        key_parts = after(key_parts, (mixture_parts[1:], up_sum))
+        key_parts = after(key_parts, (mixture_parts[3], up_part))
     keyval_sum = scatter_blocks(key_parts)
     if cut:
         out_state = scatter_start(join_cores(*out_found))
     if cut:
-        keyval_sum = after(keyval_sum, out_found)
+        up_sum = add_low(rest[0], near[0], up_part)
+        down_term = step_down(after(down_sum, key_parts))
+        keyval_sum = after(keyval_sum, (out_found, up_sum, down_term))
     left = leave(
         place,
         qkv_spots,
@@ -1222,21 +1228,22 @@
     qkv_found, input_grad = left[:-1], left[-1]
     result = (residual + total_of(mixture_parts)).astype(low)
     if cut:
-        down_term = step_down(after(down_sum, key_parts))
-        received = exchange_cores(after(qkv_found[0], (totals[0], out_state[1:], down_term)))
+        received = exchange_cores(after(qkv_found[0], (totals[0], out_state[1:])))
         out_plane = scatter_finish(out_state)
         up_term = step_up(up_sum)
         qkv_parts = join_cores(qkv_found[1], after(received, out_plane))
         qkv_plane = after(scatter_blocks(qkv_parts), up_term)
         out_sum = line_finish(line_start(out_plane))
         qkv_state = line_start(qkv_plane)
-        terms = [[totals[0][0]], after([own, near[1], down_term, up_term], qkv_plane)]
+        near, down_term, up_term = after((near, down_term, up_term), qkv_plane)
+        terms = [[(totals[0], 0)], [(own, None), (near, 1), (down_term, None), (up_term, None)]]
         expert_totals = unpack(terms, gate_weight.shape, down_weight.shape)
         qkv_sum = line_finish(qkv_state, expert_totals)
     else:
         out_sum = scatter_whole(out_found)
         qkv_sum = scatter_whole(qkv_found)
-        terms = [[totals[0][0]]] + [[sum_chunk(found[0])[0]] for found in chunk_grads[1:]]
+        totals += [sum_chunk(found[0]) for found in chunk_grads[1:]]
+        terms = [[(total, 0)] for total in totals]
         expert_totals = unpack(terms, gate_weight.shape, down_weight.shape)
     gate_total, up_total, down_total = expert_totals
     return (

time: 565 us -> 581 us (1.028)
  waiting for transfers between devices: 199 us -> 211 us
    ppermute x4, waiting for transfers between devices: 4.58 us -> 29.1 us  [step_down(): return lax.ppermute(values, 'batch', shift_moves(3))]
    ppermute x10, waiting for transfers between devices: 69.9 us -> 58.4 us  [gather_start(): lax.ppermute(rows, 'expert', pair_moves(4, r))]
    ppermute x3, waiting for transfers between devices: 12 us -> 20.9 us  [send_parts(): lax.ppermute(parts[r].astype(low), 'expert', pair_moves(4, r))]
  transfers between devices with their start and end apart: 74 -> 74, of which waited for: 39 -> 38; matrix products, arithmetic and copies ran while one was open for 12% -> 12% of each run, Pallas kernels for 34% -> 33%
where the time goes in v2:
time: 581 us; the launch traced here: 573 us
  waiting for transfers between devices  211 us (36%)
  Pallas kernels  196 us (34%)
  starting transfers between devices  70.9 us (12%)
  other arithmetic  40.3 us (7%)
  local copies, waits for them, and re-layouts  39.3 us (7%)
  between operations  15 us (3%)
    pallas_call x2, Pallas kernels, expert_pass(): pl.pallas_call(partial(expert_kernel, cut, carried, last, len(rows), len(...  108 us
    ppermute x10, waiting for transfers between devices, gather_start(): lax.ppermute(rows, 'expert', pair_moves(4, r))  58.4 us
    ppermute x4, waiting for transfers between devices, step_down(): return lax.ppermute(values, 'batch', shift_moves(3))  29.1 us
    ppermute x4, waiting for transfers between devices, scatter_start(): bottom = lax.ppermute(parts[3][half:].astype(low), 'expert', along)  25.8 us
    pallas_call x1, Pallas kernels, attend_back(): pl.pallas_call(attend_back_kernel, in_specs=[INSIDE] * 7, out_specs=[INSI...  21.3 us
    ppermute x3, waiting for transfers between devices, send_parts(): lax.ppermute(parts[r].astype(low), 'expert', pair_moves(4, r))  20.9 us
    ppermute x8, waiting for transfers between devices, step_up(): return lax.ppermute(values, 'batch', shift_moves(1))  19.1 us
    convert_element_type x14, other arithmetic, add_low(): return total.astype(jnp.bfloat16)  17.1 us
  transfers between devices with their start and end apart: 74, of which 38 were waited for; matrix products, arithmetic and copies ran while one was open for 12% of the time, Pallas kernels for 33%

profile of v2, /device:TPU:0, one launch (start us, length us, event | category | flops | bytes accessed | tf_op | source)
XLA Modules:
  0.0 573.3 jit_solution(17096125822437360662)
XLA Ops:
  29.7 7.4 %collective-permute-done.1 = bf16[48,4224]{1,0:T(8,128)(2,1)} collective-permute-done((bf16[48,4224]{1,0:T(8,128)(2,1)}, bf16[48,4224]{1,0:T(8,128)(2,1)}, u32[]{:S(2)}, u32[]{:S(2)}) %collective-permute-start.1) | collective-permute-done | bytes 405536 | tf_op jit(solution)/shard_map/ppermute | solution.py:938
  45.4 10.9 %collective-permute-done.2 = bf16[48,4224]{1,0:T(8,128)(2,1)S(1)} collective-permute-done((bf16[48,4224]{1,0:T(8,128)(2,1)}, bf16[48,4224]{1,0:T(8,128)(2,1)S(1)}, u32[]{:S(2)}, u32[]{:S(2)}) %collective-permute-start.2) | collective-permute-done | bytes 405536 | tf_op jit(solution)/shard_map/ppermute | solution.py:934
  63.2 19.6 %collective-permute-done.3.refs_1_ = bf16[4,48,2688]{2,1,0:T(8,128)(2,1)} collective-permute-done((bf16[4,48,2688]{2,1,0:T(8,128)(2,1)S(1)}, bf16[4,48,2688]{2,1,0:T(8,128)(2,1)}, u32[]{:S(2)}, u32[]{:S(2)}) %collective-permute-start.3) | collective-permute-done | bytes 1032224 | tf_op jit(solution)/shard_map/ppermute | solution.py:818
  106.2 8.2 %enter.1 = (bf16[256,1536]{1,0:T(8,128)(2,1)}, bf16[256,1536]{1,0:T(8,128)(2,1)}, bf16[256,1024]{1,0:T(8,128)(2,1)}, f32[128,1536]{1,0:T(8,128)}) custom-call(s32[8,4]{1,0:T(8,128)} %concatenate.91.spots, bf16[256,1536]{1,0:T(8,128)(2,1)} %bitcast.177, f32[256,128]{1,0:T(8,128)} %copy.56.cosine, f32[256,128]{1,0:T(8,128)} %copy.57.sine, ...), custom_call_target="tpu_custom_call" | custom-call | flops 1 | bytes 1 | tf_op jit(solution)/shard_map/enter/pallas_call | solution.py:137
  119.8 10.5 %collective-permute-done.13 = bf16[256,1024]{1,0:T(8,128)(2,1)S(1)} collective-permute-done((bf16[256,1024]{1,0:T(8,128)(2,1)}, bf16[256,1024]{1,0:T(8,128)(2,1)S(1)}, u32[]{:S(2)}, u32[]{:S(2)}) %collective-permute-start.13) | collective-permute-done | bytes 524320 | tf_op jit(solution)/shard_map/ppermute | solution.py:818
  145.0 13.8 %attend.1 = (bf16[256,1536]{1,0:T(8,128)(2,1)}, f32[256,128]{1,0:T(8,128)}) custom-call(bf16[256,1536]{1,0:T(8,128)(2,1)} %get-tuple-element.85.query, bf16[768,1024]{1,0:T(8,128)(2,1)} %pad_maximum_fusion.3.keyval, f32[256,768]{1,0:T(8,128)} %and_select_fusion.1.bias), custom_call_target="tpu_custom_call" | custom-call | flops 1 | bytes 1 | tf_op jit(solution)/shard_map/attend/pallas_call | solution.py:203
  164.1 7.7 %project.1 = (f32[256,1536]{1,0:T(8,128)}, bf16[256,1664]{1,0:T(8,128)(2,1)}, f32[256,128]{1,0:T(8,128)}) custom-call(s32[8,4]{1,0:T(8,128)} %concatenate.91.spots, bf16[256,1536]{1,0:T(8,128)(2,1)} %get-tuple-element.91.attended, bf16[256,1536]{1,0:T(8,128)(2,1)} %bitcast.178, f32[128,1536]{1,0:T(8,128)} %get-tuple-element.92.small, ...), custom_call_target="tpu_custom_call" | custom-call | flops 1 | bytes 1 | tf_op jit(solution)/shard_map/project/pallas_call | solution.py:245
  174.6 18.7 %collective-permute-done.27.refs_1_ = bf16[256,1664]{1,0:T(8,128)(2,1)S(1)} collective-permute-done((bf16[256,1664]{1,0:T(8,128)(2,1)}, bf16[256,1664]{1,0:T(8,128)(2,1)S(1)}, u32[]{:S(2)}, u32[]{:S(2)}) %collective-permute-start.27) | collective-permute-done | bytes 852000 | tf_op jit(solution)/shard_map/ppermute | solution.py:818
  197.1 8.3 %collective-permute-done.29.refs_3_ = bf16[128,1664]{1,0:T(8,128)(2,1)} collective-permute-done((bf16[128,1664]{1,0:T(8,128)(2,1)S(1)}, bf16[128,1664]{1,0:T(8,128)(2,1)}, u32[]{:S(2)}, u32[]{:S(2)}) %collective-permute-start.29) | collective-permute-done | bytes 426016 | tf_op jit(solution)/shard_map/ppermute | solution.py:826
  206.1 62.4 %experts.2 = (bf16[8,3,3,64,1536]{4,3,2,1,0:T(8,128)(2,1)}, f32[1024,1536]{1,0:T(8,128)}, f32[1024,1664]{1,0:T(8,128)}) custom-call(s32[3]{0:T(128)} %pad_add_fusion.1.place, s32[1]{0:T(128)} %bitcast.61.first, bf16[8,3,3,64,1536]{4,3,2,1,0:T(8,128)(2,1)} %bitcast.175, bf16[256,1664]{1,0:T(8,128)(2,1)} %get-tuple-element.101.refs_0_.normed, ...), custom_call_target="tpu_custom_call" | custom-call | flops 1 | bytes 1 | tf_op jit(solution)/shard_map/experts/pallas_call | solution.py:727
  268.5 6.7 %all-gather.5.cloned.1.call-done = bf16[24,2,64,1536]{3,2,1,0:T(8,128)(2,1)} async-done(((bf16[3,2,64,1536]{3,2,1,0:T(8,128)(2,1)}), bf16[24,2,64,1536]{3,2,1,0:T(8,128)(2,1)}) %all-gather.5.cloned.1.call-update) | async-done | bytes 9437200 | tf_op jit(solution)/shard_map/all_gather | solution.py:1099
  275.2 45.6 %experts.3 = (bf16[3,2,64,1536]{3,2,1,0:T(8,128)(2,1)}, bf16[3,3,2,64,1536]{4,3,2,1,0:T(8,128)(2,1)}, bf16[2,3,2,64,1536]{4,3,2,1,0:T(8,128)(2,1)}, bf16[2,3,2,6...) custom-call(s32[3]{0:T(128)} %pad_add_fusion.1.place, s32[1]{0:T(128)} %bitcast.59.first, ...), custom_call_target="tpu_custom_call" | custom-call | flops 1 | bytes 1 | tf_op jit(solution)/shard_map/experts/pallas_call | solution.py:727
  327.1 8.5 %collective-permute-done.33 = bf16[128,1664]{1,0:T(8,128)(2,1)S(1)} collective-permute-done((bf16[128,1664]{1,0:T(8,128)(2,1)S(1)}, bf16[128,1664]{1,0:T(8,128)(2,1)S(1)}, u32[]{:S(2)}, u32[]{:S(2)}) %collective-permute-start.33) | collective-permute-done | bytes 426016 | tf_op jit(solution)/shard_map/ppermute | solution.py:845
  339.3 6.0 %collective-permute-done.31 = bf16[128,1664]{1,0:T(8,128)(2,1)S(1)} collective-permute-done((bf16[128,1664]{1,0:T(8,128)(2,1)S(1)}, bf16[128,1664]{1,0:T(8,128)(2,1)S(1)}, u32[]{:S(2)}, u32[]{:S(2)}) %collective-permute-start.31) | collective-permute-done | bytes 426016 | tf_op jit(solution)/shard_map/ppermute | solution.py:846
  347.3 8.9 %collective-permute-done.36 = bf16[128,1664]{1,0:T(8,128)(2,1)S(1)} collective-permute-done((bf16[128,1664]{1,0:T(8,128)(2,1)S(1)}, bf16[128,1664]{1,0:T(8,128)(2,1)S(1)}, u32[]{:S(2)}, u32[]{:S(2)}) %collective-permute-start.36) | collective-permute-done | bytes 426016 | tf_op jit(solution)/shard_map/ppermute | solution.py:858
  364.1 11.4 %turn.1 = (bf16[4,4,48,1664]{3,2,1,0:T(8,128)(2,1)}, bf16[4,4,48,1664]{3,2,1,0:T(8,128)(2,1)}, f32[256,1536]{1,0:T(8,128)}, bf16[256,1536]{1,0:T(8,128)(2,1)}) custom-call(s32[3]{0:T(128)} %pad_add_fusion.1.place, s32[8,4]{1,0:T(8,128)} %concatenate.91.spots, f32[256,1664]{1,0:T(8,128)} %pad_maximum_fusion.2.normed_grad, ...), custom_call_target="tpu_custom_call" | custom-call | flops 1 | bytes 1 | tf_op jit(solution)/shard_map/turn/pallas_call | solution.py:370
  375.6 5.9 %collective-permute-done.38 = bf16[256,1536]{1,0:T(8,128)(2,1)} collective-permute-done((bf16[256,1536]{1,0:T(8,128)(2,1)}, bf16[256,1536]{1,0:T(8,128)(2,1)}, u32[]{:S(2)}, u32[]{:S(2)}) %collective-permute-start.38) | collective-permute-done | bytes 786464 | tf_op jit(solution)/shard_map/ppermute | solution.py:882
  381.4 15.1 %collective-permute-done.39 = bf16[256,1536]{1,0:T(8,128)(2,1)} collective-permute-done((bf16[256,1536]{1,0:T(8,128)(2,1)}, bf16[256,1536]{1,0:T(8,128)(2,1)}, u32[]{:S(2)}, u32[]{:S(2)}) %collective-permute-start.39) | collective-permute-done | bytes 786464 | tf_op jit(solution)/shard_map/ppermute | solution.py:882
  396.5 21.3 %attend_back.1 = (bf16[256,1536]{1,0:T(8,128)(2,1)}, bf16[768,1024]{1,0:T(8,128)(2,1)}) custom-call(bf16[256,1536]{1,0:T(8,128)(2,1)} %get-tuple-element.120.head_grad, bf16[256,1536]{1,0:T(8,128)(2,1)} %get-tuple-element.85.query, bf16[768,1024]{1,0:T(8,128)(2,1)} %pad_maximum_fusion.3.keyval, f32[768,256]{1,0:T(8,128)} %and_select_fusion.bias, ...), custom_call_target="tpu_custom_call" | custom-call | flops 1 | bytes 1 | tf_op jit(solution)/shard_map/attend_back/pallas_call | solution.py:445
  447.8 20.0 %collective-permute-done.50.refs_3_ = bf16[3,2,64,1536]{3,2,1,0:T(8,128)(2,1)} collective-permute-done((bf16[3,2,64,1536]{3,2,1,0:T(8,128)(2,1)}, bf16[3,2,64,1536]{3,2,1,0:T(8,128)(2,1)}, u32[]{:S(2)}, u32[]{:S(2)}) %collective-permute-start.50) | collective-permute-done | bytes 1179680 | tf_op jit(solution)/shard_map/ppermute | solution.py:938
  467.8 15.2 %leave.1 = (bf16[4,4,48,2688]{3,2,1,0:T(8,128)(2,1)}, bf16[4,4,48,2688]{3,2,1,0:T(8,128)(2,1)}, f32[256,1536]{1,0:T(8,128)}) custom-call(s32[3]{0:T(128)} %pad_add_fusion.1.place, s32[8,4]{1,0:T(8,128)} %concatenate.91.spots, f32[256,1024]{1,0:T(8,128)} %pad_maximum_fusion.4.keyval_sum, bf16[256,1536]{1,0:T(8,128)(2,1)} %get-tuple-element.132.query_grad, ...), custom_call_target="tpu_custom_call" | custom-call | flops 1 | bytes 1 | tf_op jit(solution)/shard_map/leave/pallas_call | solution.py:530
  500.0 11.8 %collective-permute-done.61 = bf16[2,48,2688]{2,1,0:T(8,128)(2,1)S(1)} collective-permute-done((bf16[2,48,2688]{2,1,0:T(8,128)(2,1)S(1)}, bf16[2,48,2688]{2,1,0:T(8,128)(2,1)S(1)}, u32[]{:S(2)}, u32[]{:S(2)}) %collective-permute-start.61) | collective-permute-done | bytes 516128 | tf_op jit(solution)/shard_map/ppermute | solution.py:845
  518.7 7.7 %collective-permute-done.58 = bf16[2,48,2688]{2,1,0:T(8,128)(2,1)S(1)} collective-permute-done((bf16[2,48,2688]{2,1,0:T(8,128)(2,1)S(1)}, bf16[2,48,2688]{2,1,0:T(8,128)(2,1)S(1)}, u32[]{:S(2)}, u32[]{:S(2)}) %collective-permute-start.58) | collective-permute-done | bytes 516128 | tf_op jit(solution)/shard_map/ppermute | solution.py:846
  546.2 6.0 %unpack.1 = (f32[5,192,512]{2,1,0:T(8,128)}, f32[5,192,512]{2,1,0:T(8,128)}, f32[5,64,1536]{2,1,0:T(8,128)}) custom-call(bf16[1,3,3,64,1536]{4,3,2,1,0:T(8,128)(2,1)} %reduce-scatter.2.cloned.1.call-done.refs_0_, bf16[3,2,64,1536]{3,2,1,0:T(8,128)(2,1)} %get-tuple-element.142.refs_1_, bf16[2,3,2,64,1536]{4,3,2,1,0:T(8,128)(2,1)} %collective-permute-done.49.refs_2_, ...), custom_call_target="tpu_custom_call" | custom-call | flops 1 | bytes 1 | tf_op jit(solution)/shard_map/unpack/pallas_call | solution.py:783
  (318 shorter events, 200.7 us)
Async XLA Ops:
  7.2 198.8 %all-gather.7.cloned.1.call-start = ((), (), s32[]{:S(2)}) async-start(), calls=%async_computation.3 | async-start | bytes 15925248 | tf_op jit(solution)/shard_map/all_gather | solution.py:1099
  57.1 218.2 %all-gather.5.cloned.1.call-start = ((), (), s32[]{:S(2)}) async-start(), calls=%async_computation.2 | async-start | bytes 10616832 | tf_op jit(solution)/shard_map/all_gather | solution.py:1099
  61.2 21.5 %collective-permute-start.3 = (bf16[4,48,2688]{2,1,0:T(8,128)(2,1)S(1)}, bf16[4,48,2688]{2,1,0:T(8,128)(2,1)}, u32[]{:S(2)}, u32[]{:S(2)}) collective-permute-start(bf16[4,48,2688]{2,1,0:T(8,128)(2,1)S(1)} %pad_maximum_fusion.5.refs_0_), channel_id=1, source_target_pairs={{0,1},{1,0},{2,3},{3,2},{4,5},{5,4},{6,7},{7,6},{8,9},{9,8},{10,11... | collective-permute-start | bytes 3096584 | tf_op jit(solution)/shard_map/ppermute | solution.py:818
  83.9 402.2 %reduce-scatter.2.cloned.1.call-start = ((), (), s32[]{:S(2)}) async-start(), calls=%async_computation.1 | async-start | bytes 15925248 | tf_op jit(solution)/shard_map/reduce_scatter | solution.py:926
  134.3 28.7 %collective-permute-start.23 = (bf16[4,48,1536]{2,1,0:T(8,128)(2,1)}, bf16[4,48,1536]{2,1,0:T(8,128)(2,1)S(1)}, u32[]{:S(2)}, u32[]{:S(2)}) collective-permute-start(bf16[4,48,1536]{2,1,0:T(8,128)(2,1)} %pad_maximum_fusion.8.refs_0_), channel_id=1, source_target_pairs={{0,4},{4,0},{8,12},{12,8},{16,20},{20,16},{24,28},{28,24},{1,5},{5... | collective-permute-start | bytes 1769480 | tf_op jit(solution)/shard_map/ppermute | solution.py:930
  134.4 28.6 %collective-permute-start.24 = (bf16[4,48,1536]{2,1,0:T(8,128)(2,1)}, bf16[4,48,1536]{2,1,0:T(8,128)(2,1)}, u32[]{:S(2)}, u32[]{:S(2)}) collective-permute-start(bf16[4,48,1536]{2,1,0:T(8,128)(2,1)} %collective-permute-done.11.refs_1_), channel_id=1, source_target_pairs={{0,4},{4,0},{8,12},{12,8},{16,20},{20,16},{24,28},{28,24},{1,5},{5... | collective-permute-start | bytes 1769480 | tf_op jit(solution)/shard_map/ppermute | solution.py:930
  134.9 28.1 %collective-permute-start.25 = (bf16[4,48,1536]{2,1,0:T(8,128)(2,1)S(1)}, bf16[4,48,1536]{2,1,0:T(8,128)(2,1)}, u32[]{:S(2)}, u32[]{:S(2)}) collective-permute-start(bf16[4,48,1536]{2,1,0:T(8,128)(2,1)S(1)} %collective-permute-done.12.refs_2_), channel_id=1, source_target_pairs={{0,4},{4,0},{8,12},{12,8},{16,20},{20,16},{24,28},{28,24},{1,5},{5... | collective-permute-start | bytes 1769480 | tf_op jit(solution)/shard_map/ppermute | solution.py:930
  171.8 21.5 %collective-permute-start.27 = (bf16[256,1664]{1,0:T(8,128)(2,1)}, bf16[256,1664]{1,0:T(8,128)(2,1)S(1)}, u32[]{:S(2)}, u32[]{:S(2)}) collective-permute-start(bf16[256,1664]{1,0:T(8,128)(2,1)} %get-tuple-element.101.refs_0_.normed), channel_id=1, source_target_pairs={{0,1},{1,0},{2,3},{3,2},{4,5},{5,4},{6,7},{7,6},{8,9},{9,8},{10,11... | collective-permute-start | bytes 2555912 | tf_op jit(solution)/shard_map/ppermute | solution.py:818
  173.0 21.2 %collective-permute-start.28 = (bf16[256,1664]{1,0:T(8,128)(2,1)}, bf16[256,1664]{1,0:T(8,128)(2,1)S(1)}, u32[]{:S(2)}, u32[]{:S(2)}) collective-permute-start(bf16[256,1664]{1,0:T(8,128)(2,1)} %get-tuple-element.101.refs_0_.normed), channel_id=1, source_target_pairs={{0,2},{1,3},{2,0},{3,1},{4,6},{5,7},{6,4},{7,5},{8,10},{9,11},{10,... | collective-permute-start | bytes 2555912 | tf_op jit(solution)/shard_map/ppermute | solution.py:818
  347.3 83.5 %collective-permute-start.49 = (bf16[2,3,2,64,1536]{4,3,2,1,0:T(8,128)(2,1)}, bf16[2,3,2,64,1536]{4,3,2,1,0:T(8,128)(2,1)}, u32[]{:S(2)}, u32[]{:S(2)}) collective-permute-start(bf16[2,3,2,64,1536]{4,3,2,1,0:T(8,128)(2,1)} %get-tuple-element.129), channel_id=1, source_target_pairs={{0,4},{4,0},{8,12},{12,8},{16,20},{20,16},{24,28},{28,24},{1,5},{5... | collective-permute-start | bytes 7077896 | tf_op jit(solution)/shard_map/ppermute | solution.py:930
  362.1 57.3 %collective-permute-start.41 = (bf16[3,2,64,1536]{3,2,1,0:T(8,128)(2,1)S(1)}, bf16[3,2,64,1536]{3,2,1,0:T(8,128)(2,1)}, u32[]{:S(2)}, u32[]{:S(2)}) collective-permute-start(bf16[3,2,64,1536]{3,2,1,0:T(8,128)(2,1)S(1)} %get-tuple-element.203), channel_id=1, source_target_pairs={{0,8},{4,12},{8,16},{12,20},{16,24},{20,28},{24,0},{28,4},{1,9},{5... | collective-permute-start | bytes 3538952 | tf_op jit(solution)/shard_map/ppermute | solution.py:934
  362.1 34.4 %collective-permute-start.39 = (bf16[256,1536]{1,0:T(8,128)(2,1)}, bf16[256,1536]{1,0:T(8,128)(2,1)}, u32[]{:S(2)}, u32[]{:S(2)}) collective-permute-start(bf16[256,1536]{1,0:T(8,128)(2,1)} %get-tuple-element.216), channel_id=1, source_target_pairs={{0,2},{1,3},{2,0},{3,1},{4,6},{5,7},{6,4},{7,5},{8,10},{9,11},{10,... | collective-permute-start | bytes 2359304 | tf_op jit(solution)/shard_map/ppermute | solution.py:882
  363.5 55.9 %collective-permute-start.40 = (bf16[256,1536]{1,0:T(8,128)(2,1)S(1)}, bf16[256,1536]{1,0:T(8,128)(2,1)}, u32[]{:S(2)}, u32[]{:S(2)}) collective-permute-start(bf16[256,1536]{1,0:T(8,128)(2,1)S(1)} %get-tuple-element.215), channel_id=1, source_target_pairs={{0,3},{1,2},{2,1},{3,0},{4,7},{5,6},{6,5},{7,4},{8,11},{9,10},{10,... | collective-permute-start | bytes 2359304 | tf_op jit(solution)/shard_map/ppermute | solution.py:882
  381.4 57.7 %collective-permute-start.48 = (bf16[4,4,48,1664]{3,2,1,0:T(8,128)(2,1)}, bf16[4,4,48,1664]{3,2,1,0:T(8,128)(2,1)}, u32[]{:S(2)}, u32[]{:S(2)}) collective-permute-start(bf16[4,4,48,1664]{3,2,1,0:T(8,128)(2,1)} %get-tuple-element.128), channel_id=1, source_target_pairs={{0,4},{4,0},{8,12},{12,8},{16,20},{20,16},{24,28},{28,24},{1,5},{5... | collective-permute-start | bytes 7667720 | tf_op jit(solution)/shard_map/ppermute | solution.py:930
  434.6 33.2 %collective-permute-start.50 = (bf16[3,2,64,1536]{3,2,1,0:T(8,128)(2,1)}, bf16[3,2,64,1536]{3,2,1,0:T(8,128)(2,1)}, u32[]{:S(2)}, u32[]{:S(2)}) collective-permute-start(bf16[3,2,64,1536]{3,2,1,0:T(8,128)(2,1)} %get-tuple-element.130), channel_id=1, source_target_pairs={{0,24},{4,28},{8,0},{12,4},{16,8},{20,12},{24,16},{28,20},{1,25},{... | collective-permute-start | bytes 3538952 | tf_op jit(solution)/shard_map/ppermute | solution.py:938
  442.3 40.8 %collective-permute-start.54 = (bf16[2,48,1664]{2,1,0:T(8,128)(2,1)}, bf16[2,48,1664]{2,1,0:T(8,128)(2,1)}, u32[]{:S(2)}, u32[]{:S(2)}) collective-permute-start(bf16[2,48,1664]{2,1,0:T(8,128)(2,1)} %get-tuple-element.235), channel_id=1, source_target_pairs={{0,1},{1,0},{2,3},{3,2},{4,5},{5,4},{6,7},{7,6},{8,9},{9,8},{10,11... | collective-permute-start | bytes 958472 | tf_op jit(solution)/shard_map/ppermute | solution.py:844
  443.3 41.8 %collective-permute-start.53 = (bf16[2,48,1664]{2,1,0:T(8,128)(2,1)S(1)}, bf16[2,48,1664]{2,1,0:T(8,128)(2,1)}, u32[]{:S(2)}, u32[]{:S(2)}) collective-permute-start(bf16[2,48,1664]{2,1,0:T(8,128)(2,1)S(1)} %get-tuple-element.236), channel_id=1, source_target_pairs={{0,2},{1,3},{2,0},{3,1},{4,6},{5,7},{6,4},{7,5},{8,10},{9,11},{10,... | collective-permute-start | bytes 958472 | tf_op jit(solution)/shard_map/ppermute | solution.py:845
  445.4 40.7 %collective-permute-start.51 = (bf16[2,48,1664]{2,1,0:T(8,128)(2,1)}, bf16[2,48,1664]{2,1,0:T(8,128)(2,1)}, u32[]{:S(2)}, u32[]{:S(2)}) collective-permute-start(bf16[2,48,1664]{2,1,0:T(8,128)(2,1)} %slice_bitcast_fusion.15), channel_id=1, source_target_pairs={{0,1},{1,0},{2,3},{3,2},{4,5},{5,4},{6,7},{7,6},{8,9},{9,8},{10,11... | collective-permute-start | bytes 958472 | tf_op jit(solution)/shard_map/ppermute | solution.py:846
  447.2 38.9 %collective-permute-start.52 = (bf16[2,48,1664]{2,1,0:T(8,128)(2,1)}, bf16[2,48,1664]{2,1,0:T(8,128)(2,1)}, u32[]{:S(2)}, u32[]{:S(2)}) collective-permute-start(bf16[2,48,1664]{2,1,0:T(8,128)(2,1)} %slice_bitcast_fusion.14), channel_id=1, source_target_pairs={{0,2},{1,3},{2,0},{3,1},{4,6},{5,7},{6,4},{7,5},{8,10},{9,11},{10,... | collective-permute-start | bytes 958472 | tf_op jit(solution)/shard_map/ppermute | solution.py:847
  486.3 51.5 %collective-permute-start.64 = (bf16[3,2,64,1536]{3,2,1,0:T(8,128)(2,1)}, bf16[3,2,64,1536]{3,2,1,0:T(8,128)(2,1)S(1)}, u32[]{:S(2)}, u32[]{:S(2)}) collective-permute-start(bf16[3,2,64,1536]{3,2,1,0:T(8,128)(2,1)} %fusion), channel_id=1, source_target_pairs={{0,8},{4,12},{8,16},{12,20},{16,24},{20,28},{24,0},{28,4},{1,9},{5... | collective-permute-start | bytes 3538952 | tf_op jit(solution)/shard_map/ppermute | solution.py:934
  491.1 24.0 %collective-permute-start.56 = (bf16[2,48,1664]{2,1,0:T(8,128)(2,1)S(1)}, bf16[2,48,1664]{2,1,0:T(8,128)(2,1)S(1)}, u32[]{:S(2)}, u32[]{:S(2)}) collective-permute-start(bf16[2,48,1664]{2,1,0:T(8,128)(2,1)S(1)} %copy-done.32), channel_id=1, source_target_pairs={{0,2},{1,3},{2,0},{3,1},{4,6},{5,7},{6,4},{7,5},{8,10},{9,11},{10,... | collective-permute-start | bytes 958472 | tf_op jit(solution)/shard_map/ppermute | solution.py:858
  492.5 23.1 %collective-permute-start.57 = (bf16[2,48,1664]{2,1,0:T(8,128)(2,1)S(1)}, bf16[2,48,1664]{2,1,0:T(8,128)(2,1)S(1)}, u32[]{:S(2)}, u32[]{:S(2)}) collective-permute-start(bf16[2,48,1664]{2,1,0:T(8,128)(2,1)S(1)} %fusion.14), channel_id=1, source_target_pairs={{0,1},{1,0},{2,3},{3,2},{4,5},{5,4},{6,7},{7,6},{8,9},{9,8},{10,11... | collective-permute-start | bytes 958472 | tf_op jit(solution)/shard_map/ppermute | solution.py:859
  515.7 21.6 %collective-permute-start.60 = (bf16[2,48,2688]{2,1,0:T(8,128)(2,1)S(1)}, bf16[2,48,2688]{2,1,0:T(8,128)(2,1)S(1)}, u32[]{:S(2)}, u32[]{:S(2)}) collective-permute-start(bf16[2,48,2688]{2,1,0:T(8,128)(2,1)S(1)} %fusion.8), channel_id=1, source_target_pairs={{0,2},{1,3},{2,0},{3,1},{4,6},{5,7},{6,4},{7,5},{8,10},{9,11},{10,... | collective-permute-start | bytes 1548296 | tf_op jit(solution)/shard_map/ppermute | solution.py:858
  528.1 25.3 %collective-permute-start.68 = (bf16[48,1664]{1,0:T(8,128)(2,1)}, bf16[48,1664]{1,0:T(8,128)(2,1)S(1)}, u32[]{:S(2)}, u32[]{:S(2)}) collective-permute-start(bf16[48,1664]{1,0:T(8,128)(2,1)} %get-tuple-element.225), channel_id=1, source_target_pairs={{0,24},{4,28},{8,0},{12,4},{16,8},{20,12},{24,16},{28,20},{1,25},{... | collective-permute-start | bytes 479240 | tf_op jit(solution)/shard_map/ppermute | solution.py:938
  (85 other events, 1170.7 us)
Sparse Core Ops, SparseCore 0:
  57.2 126.8 all-gather.6
  186.2 88.9 all-gather.4
  277.6 179.9 reduce-scatter.1

commit v3 on v2

--- a/solution.py
+++ b/solution.py
@@ -874,13 +874,15 @@
     return lax.optimization_barrier((values, events))[0]
 
 
-def send_parts(parts):
+def send_parts(parts, events):
     if lax.axis_size("expert") != 4:
         return [scatter_blocks(parts)]
     low = jnp.bfloat16
-    return [parts[0]] + [
-        lax.ppermute(parts[r].astype(low), "expert", pair_moves(4, r)) for r in range(1, 4)
-    ]
+    first, second = (
+        lax.ppermute(parts[r].astype(low), "expert", pair_moves(4, r)) for r in (1, 2)
+    )
+    far = lax.ppermute(after(parts[3].astype(low), (first, second, events)), "expert", pair_moves(4, 3))
+    return [parts[0], first, second, far]
 
 
 def total_of(parts):
@@ -1181,7 +1183,7 @@
     )
     out_found = turned[:-2]
     resid_grad, head_grad = turned[-2:]
-    mixture_parts = send_parts(blocks_of(after(mixture_all, normed_grad)))
+    mixture_parts = send_parts(blocks_of(after(mixture_all, normed_grad)), resid_grad)
     if cut:
         head_grad = after(head_grad, mixture_parts[1:3])
         up_part = step_up(far_sum)
@@ -1206,8 +1208,7 @@
         out_state = scatter_start(join_cores(*out_found))
     if cut:
         up_sum = add_low(rest[0], near[0], up_part)
-        down_term = step_down(after(down_sum, key_parts))
-        keyval_sum = after(keyval_sum, (out_found, up_sum, down_term))
+        keyval_sum = after(keyval_sum, (out_found, up_sum))
     left = leave(
         place,
         qkv_spots,
@@ -1228,11 +1229,13 @@
     qkv_found, input_grad = left[:-1], left[-1]
     result = (residual + total_of(mixture_parts)).astype(low)
     if cut:
-        received = exchange_cores(after(qkv_found[0], (totals[0], out_state[1:])))
+        down_term = step_down(after(down_sum, key_parts))
+        received = exchange_cores(after(qkv_found[0], (totals[0], out_state[1:], down_term)))
         out_plane = scatter_finish(out_state)
         up_term = step_up(up_sum)
         qkv_parts = join_cores(qkv_found[1], after(received, out_plane))
-        qkv_plane = after(scatter_blocks(qkv_parts), up_term)
+        qkv_state = after(scatter_start(qkv_parts), up_term)
+        qkv_plane = scatter_finish(qkv_state)
         out_sum = line_finish(line_start(out_plane))
         qkv_state = line_start(qkv_plane)
         near, down_term, up_term = after((near, down_term, up_term), qkv_plane)

time: 581 us -> 584 us (level)
  waiting for transfers between devices: 211 us -> 224 us
  starting transfers between devices: 70.9 us -> 63.7 us
    ppermute x8, waiting for transfers between devices: 19.1 us -> 59.4 us  [step_up(): return lax.ppermute(values, 'batch', shift_moves(1))]
    ppermute x4, waiting for transfers between devices: 29.1 us -> 10 us  [step_down(): return lax.ppermute(values, 'batch', shift_moves(3))]
    ppermute x3 -> x2, waiting for transfers between devices: 20.9 us -> 4.73 us  [send_parts(): lax.ppermute(parts[r].astype(low), 'expert', pair_moves(4, r))]
    ppermute x4, waiting for transfers between devices: 1.61 us -> 16.9 us  [scatter_start(): top = lax.ppermute(parts[3][:half].astype(low), 'expert', across)]
    ppermute x4, waiting for transfers between devices: 25.8 us -> 13.8 us  [scatter_start(): bottom = lax.ppermute(parts[3][half:].astype(low), 'expert', along)]
    convert_element_type x14 -> x15, other arithmetic: 17.1 us -> 19.6 us  [add_low(): return total.astype(jnp.bfloat16)]
  transfers between devices with their start and end apart: 74 -> 74, of which waited for: 38 -> 42; matrix products, arithmetic and copies ran while one was open for 12% -> 12% of each run, Pallas kernels for 33% -> 33%
where the time goes in v3:
time: 584 us; the launch traced here: 576 us
  waiting for transfers between devices  224 us (38%)
  Pallas kernels  195 us (33%)
  starting transfers between devices  63.7 us (11%)
  other arithmetic  41.8 us (7%)
  local copies, waits for them, and re-layouts  34.3 us (6%)
  between operations  15.1 us (3%)
    pallas_call x2, Pallas kernels, expert_pass(): pl.pallas_call(partial(expert_kernel, cut, carried, last, len(rows), len(...  108 us
    ppermute x8, waiting for transfers between devices, step_up(): return lax.ppermute(values, 'batch', shift_moves(1))  59.4 us
    ppermute x10, waiting for transfers between devices, gather_start(): lax.ppermute(rows, 'expert', pair_moves(4, r))  59 us
    pallas_call x1, Pallas kernels, attend_back(): pl.pallas_call(attend_back_kernel, in_specs=[INSIDE] * 7, out_specs=[INSI...  21.2 us
    convert_element_type x15, other arithmetic, add_low(): return total.astype(jnp.bfloat16)  19.6 us
    ppermute x4, waiting for transfers between devices, scatter_start(): top = lax.ppermute(parts[3][:half].astype(low), 'expert', across)  16.9 us
    pallas_call x1, Pallas kernels, leave(): pl.pallas_call(partial(leave_kernel, len(pieces), cut, gain_at), in_specs...  15.1 us
    ppermute x5, waiting for transfers between devices, gather_finish(): top = lax.ppermute(second[:half], 'expert', pair_moves(4, 1))  14.5 us
  transfers between devices with their start and end apart: 74, of which 42 were waited for; matrix products, arithmetic and copies ran while one was open for 12% of the time, Pallas kernels for 33%

profile of v3, /device:TPU:0, one launch (start us, length us, event | category | flops | bytes accessed | tf_op | source)
XLA Modules:
  0.0 576.1 jit_solution(5775001914036735231)
XLA Ops:
  29.8 7.3 %collective-permute-done.1 = bf16[48,4224]{1,0:T(8,128)(2,1)} collective-permute-done((bf16[48,4224]{1,0:T(8,128)(2,1)}, bf16[48,4224]{1,0:T(8,128)(2,1)}, u32[]{:S(2)}, u32[]{:S(2)}) %collective-permute-start.1) | collective-permute-done | bytes 405536 | tf_op jit(solution)/shard_map/ppermute | solution.py:940
  44.6 10.9 %collective-permute-done.2 = bf16[48,4224]{1,0:T(8,128)(2,1)S(1)} collective-permute-done((bf16[48,4224]{1,0:T(8,128)(2,1)}, bf16[48,4224]{1,0:T(8,128)(2,1)S(1)}, u32[]{:S(2)}, u32[]{:S(2)}) %collective-permute-start.2) | collective-permute-done | bytes 405536 | tf_op jit(solution)/shard_map/ppermute | solution.py:936
  60.8 19.5 %collective-permute-done.3.refs_1_ = bf16[4,48,2688]{2,1,0:T(8,128)(2,1)} collective-permute-done((bf16[4,48,2688]{2,1,0:T(8,128)(2,1)S(1)}, bf16[4,48,2688]{2,1,0:T(8,128)(2,1)}, u32[]{:S(2)}, u32[]{:S(2)}) %collective-permute-start.3) | collective-permute-done | bytes 1032224 | tf_op jit(solution)/shard_map/ppermute | solution.py:818
  101.3 8.1 %enter.1 = (bf16[256,1536]{1,0:T(8,128)(2,1)}, bf16[256,1536]{1,0:T(8,128)(2,1)}, bf16[256,1024]{1,0:T(8,128)(2,1)}, f32[128,1536]{1,0:T(8,128)}) custom-call(s32[8,4]{1,0:T(8,128)} %concatenate.91.spots, bf16[256,1536]{1,0:T(8,128)(2,1)} %bitcast.173, f32[256,128]{1,0:T(8,128)} %copy.56.cosine, f32[256,128]{1,0:T(8,128)} %copy.57.sine, ...), custom_call_target="tpu_custom_call" | custom-call | flops 1 | bytes 1 | tf_op jit(solution)/shard_map/enter/pallas_call | solution.py:137
  118.2 8.8 %collective-permute-done.13 = bf16[256,1024]{1,0:T(8,128)(2,1)S(1)} collective-permute-done((bf16[256,1024]{1,0:T(8,128)(2,1)}, bf16[256,1024]{1,0:T(8,128)(2,1)S(1)}, u32[]{:S(2)}, u32[]{:S(2)}) %collective-permute-start.13) | collective-permute-done | bytes 524320 | tf_op jit(solution)/shard_map/ppermute | solution.py:818
  141.6 13.7 %attend.1 = (bf16[256,1536]{1,0:T(8,128)(2,1)}, f32[256,128]{1,0:T(8,128)}) custom-call(bf16[256,1536]{1,0:T(8,128)(2,1)} %get-tuple-element.90.query, bf16[768,1024]{1,0:T(8,128)(2,1)} %pad_maximum_fusion.3.keyval, f32[256,768]{1,0:T(8,128)} %and_select_fusion.1.bias), custom_call_target="tpu_custom_call" | custom-call | flops 1 | bytes 1 | tf_op jit(solution)/shard_map/attend/pallas_call | solution.py:203
  160.5 7.7 %project.1 = (f32[256,1536]{1,0:T(8,128)}, bf16[256,1664]{1,0:T(8,128)(2,1)}, f32[256,128]{1,0:T(8,128)}) custom-call(s32[8,4]{1,0:T(8,128)} %concatenate.91.spots, bf16[256,1536]{1,0:T(8,128)(2,1)} %get-tuple-element.96.attended, bf16[256,1536]{1,0:T(8,128)(2,1)} %bitcast.174, f32[128,1536]{1,0:T(8,128)} %get-tuple-element.97.small, ...), custom_call_target="tpu_custom_call" | custom-call | flops 1 | bytes 1 | tf_op jit(solution)/shard_map/project/pallas_call | solution.py:245
  170.8 18.9 %collective-permute-done.27.refs_1_ = bf16[256,1664]{1,0:T(8,128)(2,1)S(1)} collective-permute-done((bf16[256,1664]{1,0:T(8,128)(2,1)}, bf16[256,1664]{1,0:T(8,128)(2,1)S(1)}, u32[]{:S(2)}, u32[]{:S(2)}) %collective-permute-start.27) | collective-permute-done | bytes 852000 | tf_op jit(solution)/shard_map/ppermute | solution.py:818
  193.4 8.4 %collective-permute-done.29.refs_3_ = bf16[128,1664]{1,0:T(8,128)(2,1)} collective-permute-done((bf16[128,1664]{1,0:T(8,128)(2,1)S(1)}, bf16[128,1664]{1,0:T(8,128)(2,1)}, u32[]{:S(2)}, u32[]{:S(2)}) %collective-permute-start.29) | collective-permute-done | bytes 426016 | tf_op jit(solution)/shard_map/ppermute | solution.py:826
  202.6 62.6 %experts.2 = (bf16[8,3,3,64,1536]{4,3,2,1,0:T(8,128)(2,1)}, f32[1024,1536]{1,0:T(8,128)}, f32[1024,1664]{1,0:T(8,128)}) custom-call(s32[3]{0:T(128)} %pad_add_fusion.1.place, s32[1]{0:T(128)} %bitcast.61.first, bf16[8,3,3,64,1536]{4,3,2,1,0:T(8,128)(2,1)} %bitcast.171, bf16[256,1664]{1,0:T(8,128)(2,1)} %get-tuple-element.106.refs_0_.normed, ...), custom_call_target="tpu_custom_call" | custom-call | flops 1 | bytes 1 | tf_op jit(solution)/shard_map/experts/pallas_call | solution.py:727
  265.2 8.5 %all-gather.5.cloned.1.call-done = bf16[24,2,64,1536]{3,2,1,0:T(8,128)(2,1)} async-done(((bf16[3,2,64,1536]{3,2,1,0:T(8,128)(2,1)}), bf16[24,2,64,1536]{3,2,1,0:T(8,128)(2,1)}) %all-gather.5.cloned.1.call-update) | async-done | bytes 9437200 | tf_op jit(solution)/shard_map/all_gather | solution.py:1101
  273.7 45.5 %experts.3 = (bf16[3,2,64,1536]{3,2,1,0:T(8,128)(2,1)}, bf16[3,3,2,64,1536]{4,3,2,1,0:T(8,128)(2,1)}, bf16[2,3,2,64,1536]{4,3,2,1,0:T(8,128)(2,1)}, bf16[2,3,2,6...) custom-call(s32[3]{0:T(128)} %pad_add_fusion.1.place, s32[1]{0:T(128)} %bitcast.59.first, ...), custom_call_target="tpu_custom_call" | custom-call | flops 1 | bytes 1 | tf_op jit(solution)/shard_map/experts/pallas_call | solution.py:727
  325.6 8.5 %collective-permute-done.33 = bf16[128,1664]{1,0:T(8,128)(2,1)S(1)} collective-permute-done((bf16[128,1664]{1,0:T(8,128)(2,1)S(1)}, bf16[128,1664]{1,0:T(8,128)(2,1)S(1)}, u32[]{:S(2)}, u32[]{:S(2)}) %collective-permute-start.33) | collective-permute-done | bytes 426016 | tf_op jit(solution)/shard_map/ppermute | solution.py:845
  337.7 6.0 %collective-permute-done.31 = bf16[128,1664]{1,0:T(8,128)(2,1)S(1)} collective-permute-done((bf16[128,1664]{1,0:T(8,128)(2,1)S(1)}, bf16[128,1664]{1,0:T(8,128)(2,1)S(1)}, u32[]{:S(2)}, u32[]{:S(2)}) %collective-permute-start.31) | collective-permute-done | bytes 426016 | tf_op jit(solution)/shard_map/ppermute | solution.py:846
  345.7 8.8 %collective-permute-done.36 = bf16[128,1664]{1,0:T(8,128)(2,1)S(1)} collective-permute-done((bf16[128,1664]{1,0:T(8,128)(2,1)S(1)}, bf16[128,1664]{1,0:T(8,128)(2,1)S(1)}, u32[]{:S(2)}, u32[]{:S(2)}) %collective-permute-start.36) | collective-permute-done | bytes 426016 | tf_op jit(solution)/shard_map/ppermute | solution.py:858
  361.9 11.4 %turn.1 = (bf16[4,4,48,1664]{3,2,1,0:T(8,128)(2,1)}, bf16[4,4,48,1664]{3,2,1,0:T(8,128)(2,1)}, f32[256,1536]{1,0:T(8,128)}, bf16[256,1536]{1,0:T(8,128)(2,1)}) custom-call(s32[3]{0:T(128)} %pad_add_fusion.1.place, s32[8,4]{1,0:T(8,128)} %concatenate.91.spots, f32[256,1664]{1,0:T(8,128)} %pad_maximum_fusion.2.normed_grad, ...), custom_call_target="tpu_custom_call" | custom-call | flops 1 | bytes 1 | tf_op jit(solution)/shard_map/turn/pallas_call | solution.py:370
  379.4 21.2 %attend_back.1 = (bf16[256,1536]{1,0:T(8,128)(2,1)}, bf16[768,1024]{1,0:T(8,128)(2,1)}) custom-call(bf16[256,1536]{1,0:T(8,128)(2,1)} %get-tuple-element.127.head_grad, bf16[256,1536]{1,0:T(8,128)(2,1)} %get-tuple-element.90.query, bf16[768,1024]{1,0:T(8,128)(2,1)} %pad_maximum_fusion.3.keyval, f32[768,256]{1,0:T(8,128)} %and_select_fusion.bias, ...), custom_call_target="tpu_custom_call" | custom-call | flops 1 | bytes 1 | tf_op jit(solution)/shard_map/attend_back/pallas_call | solution.py:445
  402.2 15.6 %collective-permute-done.41 = bf16[3,2,64,1536]{3,2,1,0:T(8,128)(2,1)} collective-permute-done((bf16[3,2,64,1536]{3,2,1,0:T(8,128)(2,1)S(1)}, bf16[3,2,64,1536]{3,2,1,0:T(8,128)(2,1)}, u32[]{:S(2)}, u32[]{:S(2)}) %collective-permute-start.41) | collective-permute-done | bytes 1179680 | tf_op jit(solution)/shard_map/ppermute | solution.py:936
  420.7 5.3 collective-permute-done.45
  448.9 15.1 %leave.1 = (bf16[4,4,48,2688]{3,2,1,0:T(8,128)(2,1)}, bf16[4,4,48,2688]{3,2,1,0:T(8,128)(2,1)}, f32[256,1536]{1,0:T(8,128)}) custom-call(s32[3]{0:T(128)} %pad_add_fusion.1.place, s32[8,4]{1,0:T(8,128)} %concatenate.91.spots, f32[256,1024]{1,0:T(8,128)} %pad_maximum_fusion.4.keyval_sum, bf16[256,1536]{1,0:T(8,128)(2,1)} %get-tuple-element.138.query_grad, ...), custom_call_target="tpu_custom_call" | custom-call | flops 1 | bytes 1 | tf_op jit(solution)/shard_map/leave/pallas_call | solution.py:530
  471.4 27.0 %collective-permute-done.62.refs_4_ = bf16[3,2,64,1536]{3,2,1,0:T(8,128)(2,1)} collective-permute-done((bf16[3,2,64,1536]{3,2,1,0:T(8,128)(2,1)}, bf16[3,2,64,1536]{3,2,1,0:T(8,128)(2,1)}, u32[]{:S(2)}, u32[]{:S(2)}) %collective-permute-start.62) | collective-permute-done | bytes 1179680 | tf_op jit(solution)/shard_map/ppermute | solution.py:936
  506.4 14.1 %collective-permute-done.61 = bf16[2,48,2688]{2,1,0:T(8,128)(2,1)S(1)} collective-permute-done((bf16[2,48,2688]{2,1,0:T(8,128)(2,1)S(1)}, bf16[2,48,2688]{2,1,0:T(8,128)(2,1)S(1)}, u32[]{:S(2)}, u32[]{:S(2)}) %collective-permute-start.61) | collective-permute-done | bytes 516128 | tf_op jit(solution)/shard_map/ppermute | solution.py:844
  522.2 7.7 %collective-permute-done.58 = bf16[2,48,2688]{2,1,0:T(8,128)(2,1)S(1)} collective-permute-done((bf16[2,48,2688]{2,1,0:T(8,128)(2,1)S(1)}, bf16[2,48,2688]{2,1,0:T(8,128)(2,1)S(1)}, u32[]{:S(2)}, u32[]{:S(2)}) %collective-permute-start.58) | collective-permute-done | bytes 516128 | tf_op jit(solution)/shard_map/ppermute | solution.py:846
  545.4 6.0 %unpack.1 = (f32[5,192,512]{2,1,0:T(8,128)}, f32[5,192,512]{2,1,0:T(8,128)}, f32[5,64,1536]{2,1,0:T(8,128)}) custom-call(bf16[1,3,3,64,1536]{4,3,2,1,0:T(8,128)(2,1)} %reduce-scatter.2.cloned.1.call-done.refs_0_, bf16[3,2,64,1536]{3,2,1,0:T(8,128)(2,1)} %get-tuple-element.152.refs_1_, bf16[2,3,2,64,1536]{4,3,2,1,0:T(8,128)(2,1)} %collective-permute-done.49.refs_2_, ...), custom_call_target="tpu_custom_call" | custom-call | flops 1 | bytes 1 | tf_op jit(solution)/shard_map/unpack/pallas_call | solution.py:783
  (325 shorter events, 194.3 us)
Async XLA Ops:
  7.2 195.4 %all-gather.7.cloned.1.call-start = ((), (), s32[]{:S(2)}) async-start(), calls=%async_computation.3 | async-start | bytes 15925248 | tf_op jit(solution)/shard_map/all_gather | solution.py:1101
  55.5 218.2 %all-gather.5.cloned.1.call-start = ((), (), s32[]{:S(2)}) async-start(), calls=%async_computation.2 | async-start | bytes 10616832 | tf_op jit(solution)/shard_map/all_gather | solution.py:1101
  58.8 21.6 %collective-permute-start.3 = (bf16[4,48,2688]{2,1,0:T(8,128)(2,1)S(1)}, bf16[4,48,2688]{2,1,0:T(8,128)(2,1)}, u32[]{:S(2)}, u32[]{:S(2)}) collective-permute-start(bf16[4,48,2688]{2,1,0:T(8,128)(2,1)S(1)} %pad_maximum_fusion.5.refs_0_), channel_id=1, source_target_pairs={{0,1},{1,0},{2,3},{3,2},{4,5},{5,4},{6,7},{7,6},{8,9},{9,8},{10,11... | collective-permute-start | bytes 3096584 | tf_op jit(solution)/shard_map/ppermute | solution.py:818
  60.3 21.2 %collective-permute-start.4 = (bf16[4,48,2688]{2,1,0:T(8,128)(2,1)S(1)}, bf16[4,48,2688]{2,1,0:T(8,128)(2,1)}, u32[]{:S(2)}, u32[]{:S(2)}) collective-permute-start(bf16[4,48,2688]{2,1,0:T(8,128)(2,1)S(1)} %pad_maximum_fusion.5.refs_0_), channel_id=1, source_target_pairs={{0,2},{1,3},{2,0},{3,1},{4,6},{5,7},{6,4},{7,5},{8,10},{9,11},{10,... | collective-permute-start | bytes 3096584 | tf_op jit(solution)/shard_map/ppermute | solution.py:818
  81.5 386.3 %reduce-scatter.2.cloned.1.call-start = ((), (), s32[]{:S(2)}) async-start(), calls=%async_computation.1 | async-start | bytes 15925248 | tf_op jit(solution)/shard_map/reduce_scatter | solution.py:928
  131.0 28.5 %collective-permute-start.23 = (bf16[4,48,1536]{2,1,0:T(8,128)(2,1)S(1)}, bf16[4,48,1536]{2,1,0:T(8,128)(2,1)S(1)}, u32[]{:S(2)}, u32[]{:S(2)}) collective-permute-start(bf16[4,48,1536]{2,1,0:T(8,128)(2,1)S(1)} %pad_maximum_fusion.8.refs_0_), channel_id=1, source_target_pairs={{0,4},{4,0},{8,12},{12,8},{16,20},{20,16},{24,28},{28,24},{1,5},{5... | collective-permute-start | bytes 1769480 | tf_op jit(solution)/shard_map/ppermute | solution.py:932
  131.0 28.5 %collective-permute-start.24 = (bf16[4,48,1536]{2,1,0:T(8,128)(2,1)}, bf16[4,48,1536]{2,1,0:T(8,128)(2,1)}, u32[]{:S(2)}, u32[]{:S(2)}) collective-permute-start(bf16[4,48,1536]{2,1,0:T(8,128)(2,1)} %collective-permute-done.11.refs_1_), channel_id=1, source_target_pairs={{0,4},{4,0},{8,12},{12,8},{16,20},{20,16},{24,28},{28,24},{1,5},{5... | collective-permute-start | bytes 1769480 | tf_op jit(solution)/shard_map/ppermute | solution.py:932
  131.5 28.0 %collective-permute-start.25 = (bf16[4,48,1536]{2,1,0:T(8,128)(2,1)}, bf16[4,48,1536]{2,1,0:T(8,128)(2,1)}, u32[]{:S(2)}, u32[]{:S(2)}) collective-permute-start(bf16[4,48,1536]{2,1,0:T(8,128)(2,1)} %collective-permute-done.12.refs_2_), channel_id=1, source_target_pairs={{0,4},{4,0},{8,12},{12,8},{16,20},{20,16},{24,28},{28,24},{1,5},{5... | collective-permute-start | bytes 1769480 | tf_op jit(solution)/shard_map/ppermute | solution.py:932
  168.2 21.6 %collective-permute-start.27 = (bf16[256,1664]{1,0:T(8,128)(2,1)}, bf16[256,1664]{1,0:T(8,128)(2,1)S(1)}, u32[]{:S(2)}, u32[]{:S(2)}) collective-permute-start(bf16[256,1664]{1,0:T(8,128)(2,1)} %get-tuple-element.106.refs_0_.normed), channel_id=1, source_target_pairs={{0,1},{1,0},{2,3},{3,2},{4,5},{5,4},{6,7},{7,6},{8,9},{9,8},{10,11... | collective-permute-start | bytes 2555912 | tf_op jit(solution)/shard_map/ppermute | solution.py:818
  169.3 21.2 %collective-permute-start.28 = (bf16[256,1664]{1,0:T(8,128)(2,1)}, bf16[256,1664]{1,0:T(8,128)(2,1)S(1)}, u32[]{:S(2)}, u32[]{:S(2)}) collective-permute-start(bf16[256,1664]{1,0:T(8,128)(2,1)} %get-tuple-element.106.refs_0_.normed), channel_id=1, source_target_pairs={{0,2},{1,3},{2,0},{3,1},{4,6},{5,7},{6,4},{7,5},{8,10},{9,11},{10,... | collective-permute-start | bytes 2555912 | tf_op jit(solution)/shard_map/ppermute | solution.py:818
  361.9 66.5 %collective-permute-start.49 = (bf16[2,3,2,64,1536]{4,3,2,1,0:T(8,128)(2,1)}, bf16[2,3,2,64,1536]{4,3,2,1,0:T(8,128)(2,1)}, u32[]{:S(2)}, u32[]{:S(2)}) collective-permute-start(bf16[2,3,2,64,1536]{4,3,2,1,0:T(8,128)(2,1)} %get-tuple-element.136), channel_id=1, source_target_pairs={{0,4},{4,0},{8,12},{12,8},{16,20},{20,16},{24,28},{28,24},{1,5},{5... | collective-permute-start | bytes 7077896 | tf_op jit(solution)/shard_map/ppermute | solution.py:932
  361.9 55.9 %collective-permute-start.41 = (bf16[3,2,64,1536]{3,2,1,0:T(8,128)(2,1)S(1)}, bf16[3,2,64,1536]{3,2,1,0:T(8,128)(2,1)}, u32[]{:S(2)}, u32[]{:S(2)}) collective-permute-start(bf16[3,2,64,1536]{3,2,1,0:T(8,128)(2,1)S(1)} %get-tuple-element.213), channel_id=1, source_target_pairs={{0,8},{4,12},{8,16},{12,20},{16,24},{20,28},{24,0},{28,4},{1,9},{5... | collective-permute-start | bytes 3538952 | tf_op jit(solution)/shard_map/ppermute | solution.py:936
  378.1 39.8 %collective-permute-start.40 = (bf16[256,1536]{1,0:T(8,128)(2,1)S(1)}, bf16[256,1536]{1,0:T(8,128)(2,1)}, u32[]{:S(2)}, u32[]{:S(2)}) collective-permute-start(bf16[256,1536]{1,0:T(8,128)(2,1)S(1)} %get-tuple-element.125), channel_id=1, source_target_pairs={{0,3},{1,2},{2,1},{3,0},{4,7},{5,6},{6,5},{7,4},{8,11},{9,10},{10,... | collective-permute-start | bytes 2359304 | tf_op jit(solution)/shard_map/ppermute | solution.py:884
  379.4 60.8 %collective-permute-start.48 = (bf16[4,4,48,1664]{3,2,1,0:T(8,128)(2,1)}, bf16[4,4,48,1664]{3,2,1,0:T(8,128)(2,1)}, u32[]{:S(2)}, u32[]{:S(2)}) collective-permute-start(bf16[4,4,48,1664]{3,2,1,0:T(8,128)(2,1)} %get-tuple-element.135), channel_id=1, source_target_pairs={{0,4},{4,0},{8,12},{12,8},{16,20},{20,16},{24,28},{28,24},{1,5},{5... | collective-permute-start | bytes 7667720 | tf_op jit(solution)/shard_map/ppermute | solution.py:932
  433.4 34.4 %collective-permute-start.54 = (bf16[3,2,64,1536]{3,2,1,0:T(8,128)(2,1)}, bf16[3,2,64,1536]{3,2,1,0:T(8,128)(2,1)}, u32[]{:S(2)}, u32[]{:S(2)}) collective-permute-start(bf16[3,2,64,1536]{3,2,1,0:T(8,128)(2,1)} %get-tuple-element.144), channel_id=1, source_target_pairs={{0,24},{4,28},{8,0},{12,4},{16,8},{20,12},{24,16},{28,20},{1,25},{... | collective-permute-start | bytes 3538952 | tf_op jit(solution)/shard_map/ppermute | solution.py:940
  443.3 20.7 %collective-permute-start.53 = (bf16[2,48,1664]{2,1,0:T(8,128)(2,1)}, bf16[2,48,1664]{2,1,0:T(8,128)(2,1)}, u32[]{:S(2)}, u32[]{:S(2)}) collective-permute-start(bf16[2,48,1664]{2,1,0:T(8,128)(2,1)} %get-tuple-element.245), channel_id=1, source_target_pairs={{0,1},{1,0},{2,3},{3,2},{4,5},{5,4},{6,7},{7,6},{8,9},{9,8},{10,11... | collective-permute-start | bytes 958472 | tf_op jit(solution)/shard_map/ppermute | solution.py:844
  443.8 22.2 %collective-permute-start.52 = (bf16[2,48,1664]{2,1,0:T(8,128)(2,1)S(1)}, bf16[2,48,1664]{2,1,0:T(8,128)(2,1)}, u32[]{:S(2)}, u32[]{:S(2)}) collective-permute-start(bf16[2,48,1664]{2,1,0:T(8,128)(2,1)S(1)} %get-tuple-element.246), channel_id=1, source_target_pairs={{0,2},{1,3},{2,0},{3,1},{4,6},{5,7},{6,4},{7,5},{8,10},{9,11},{10,... | collective-permute-start | bytes 958472 | tf_op jit(solution)/shard_map/ppermute | solution.py:845
  445.3 22.5 %collective-permute-start.50 = (bf16[2,48,1664]{2,1,0:T(8,128)(2,1)}, bf16[2,48,1664]{2,1,0:T(8,128)(2,1)}, u32[]{:S(2)}, u32[]{:S(2)}) collective-permute-start(bf16[2,48,1664]{2,1,0:T(8,128)(2,1)} %slice_bitcast_fusion.13), channel_id=1, source_target_pairs={{0,1},{1,0},{2,3},{3,2},{4,5},{5,4},{6,7},{7,6},{8,9},{9,8},{10,11... | collective-permute-start | bytes 958472 | tf_op jit(solution)/shard_map/ppermute | solution.py:846
  467.8 32.0 %collective-permute-start.55 = (bf16[4,4,48,2688]{3,2,1,0:T(8,128)(2,1)}, bf16[4,4,48,2688]{3,2,1,0:T(8,128)(2,1)}, u32[]{:S(2)}, u32[]{:S(2)}) collective-permute-start(bf16[4,4,48,2688]{3,2,1,0:T(8,128)(2,1)} %get-tuple-element.145), channel_id=1, source_target_pairs={{0,4},{4,0},{8,12},{12,8},{16,20},{20,16},{24,28},{28,24},{1,5},{5... | collective-permute-start | bytes 12386312 | tf_op jit(solution)/shard_map/ppermute | solution.py:932
  467.9 30.5 %collective-permute-start.62 = (bf16[3,2,64,1536]{3,2,1,0:T(8,128)(2,1)}, bf16[3,2,64,1536]{3,2,1,0:T(8,128)(2,1)}, u32[]{:S(2)}, u32[]{:S(2)}) collective-permute-start(bf16[3,2,64,1536]{3,2,1,0:T(8,128)(2,1)} %fusion), channel_id=1, source_target_pairs={{0,8},{4,12},{8,16},{12,20},{16,24},{20,28},{24,0},{28,4},{1,9},{5... | collective-permute-start | bytes 3538952 | tf_op jit(solution)/shard_map/ppermute | solution.py:936
  498.4 34.5 %collective-permute-start.56 = (bf16[2,48,1664]{2,1,0:T(8,128)(2,1)S(1)}, bf16[2,48,1664]{2,1,0:T(8,128)(2,1)S(1)}, u32[]{:S(2)}, u32[]{:S(2)}) collective-permute-start(bf16[2,48,1664]{2,1,0:T(8,128)(2,1)S(1)} %copy-done.27), channel_id=1, source_target_pairs={{0,2},{1,3},{2,0},{3,1},{4,6},{5,7},{6,4},{7,5},{8,10},{9,11},{10,... | collective-permute-start | bytes 958472 | tf_op jit(solution)/shard_map/ppermute | solution.py:858
  499.0 33.9 %collective-permute-start.57 = (bf16[2,48,1664]{2,1,0:T(8,128)(2,1)S(1)}, bf16[2,48,1664]{2,1,0:T(8,128)(2,1)S(1)}, u32[]{:S(2)}, u32[]{:S(2)}) collective-permute-start(bf16[2,48,1664]{2,1,0:T(8,128)(2,1)S(1)} %copy-done.28), channel_id=1, source_target_pairs={{0,1},{1,0},{2,3},{3,2},{4,5},{5,4},{6,7},{7,6},{8,9},{9,8},{10,11... | collective-permute-start | bytes 958472 | tf_op jit(solution)/shard_map/ppermute | solution.py:859
  505.8 24.1 %collective-permute-start.58 = (bf16[2,48,2688]{2,1,0:T(8,128)(2,1)S(1)}, bf16[2,48,2688]{2,1,0:T(8,128)(2,1)S(1)}, u32[]{:S(2)}, u32[]{:S(2)}) collective-permute-start(bf16[2,48,2688]{2,1,0:T(8,128)(2,1)S(1)} %slice_bitcast_fusion.5), channel_id=1, source_target_pairs={{0,1},{1,0},{2,3},{3,2},{4,5},{5,4},{6,7},{7,6},{8,9},{9,8},{10,11... | collective-permute-start | bytes 1548296 | tf_op jit(solution)/shard_map/ppermute | solution.py:846
  535.1 22.0 %collective-permute-start.68 = (bf16[48,1664]{1,0:T(8,128)(2,1)}, bf16[48,1664]{1,0:T(8,128)(2,1)}, u32[]{:S(2)}, u32[]{:S(2)}) collective-permute-start(bf16[48,1664]{1,0:T(8,128)(2,1)} %get-tuple-element.235), channel_id=1, source_target_pairs={{0,24},{4,28},{8,0},{12,4},{16,8},{20,12},{24,16},{28,20},{1,25},{... | collective-permute-start | bytes 479240 | tf_op jit(solution)/shard_map/ppermute | solution.py:940
  (89 other events, 1227.6 us)
Sparse Core Ops, SparseCore 0:
  55.6 126.8 all-gather.6
  184.7 88.9 all-gather.4
  276.0 176.0 reduce-scatter.1

commit v4 on v3

--- a/solution.py
+++ b/solution.py
@@ -1202,13 +1202,12 @@
         key_parts = blocks_of(key_grads)
     if cut:
         out_found = out_found[1], exchange_cores(out_found[0])
-        key_parts = after(key_parts, (mixture_parts[3], up_part))
+        key_parts = after(key_parts, mixture_parts[3])
     keyval_sum = scatter_blocks(key_parts)
     if cut:
         out_state = scatter_start(join_cores(*out_found))
     if cut:
-        up_sum = add_low(rest[0], near[0], up_part)
-        keyval_sum = after(keyval_sum, (out_found, up_sum))
+        keyval_sum = after(keyval_sum, out_found)
     left = leave(
         place,
         qkv_spots,
@@ -1229,10 +1228,10 @@
     qkv_found, input_grad = left[:-1], left[-1]
     result = (residual + total_of(mixture_parts)).astype(low)
     if cut:
-        down_term = step_down(after(down_sum, key_parts))
-        received = exchange_cores(after(qkv_found[0], (totals[0], out_state[1:], down_term)))
+        received = exchange_cores(after(qkv_found[0], (totals[0], out_state[1:], up_part)))
         out_plane = scatter_finish(out_state)
-        up_term = step_up(up_sum)
+        up_term = step_up(add_low(rest[0], near[0], after(up_part, received)))
+        down_term = step_down(after(down_sum, up_term))
         qkv_parts = join_cores(qkv_found[1], after(received, out_plane))
         qkv_state = after(scatter_start(qkv_parts), up_term)
         qkv_plane = scatter_finish(qkv_state)
@@ -1241,7 +1240,7 @@
         near, down_term, up_term = after((near, down_term, up_term), qkv_plane)
         terms = [[(totals[0], 0)], [(own, None), (near, 1), (down_term, None), (up_term, None)]]
         expert_totals = unpack(terms, gate_weight.shape, down_weight.shape)
-        qkv_sum = line_finish(qkv_state, expert_totals)
+        qkv_sum = line_finish(qkv_state, down_term)
     else:
         out_sum = scatter_whole(out_found)
         qkv_sum = scatter_whole(qkv_found)

time: 584 us -> 568 us (0.973)
  waiting for transfers between devices: 224 us -> 210 us
  other arithmetic: 41.8 us -> 35.9 us
    ppermute x8, waiting for transfers between devices: 59.4 us -> 45.1 us  [step_up(): return lax.ppermute(values, 'batch', shift_moves(1))]
  transfers between devices with their start and end apart: 74 -> 74, of which waited for: 42 -> 40; matrix products, arithmetic and copies ran while one was open for 12% -> 11% of each run, Pallas kernels for 33% -> 34%
where the time goes in v4:
time: 568 us; the launch traced here: 560 us
  waiting for transfers between devices  210 us (37%)
  Pallas kernels  195 us (34%)
  starting transfers between devices  68.1 us (12%)
  other arithmetic  35.9 us (6%)
  local copies, waits for them, and re-layouts  34.1 us (6%)
  between operations  15.1 us (3%)
    pallas_call x2, Pallas kernels, expert_pass(): pl.pallas_call(partial(expert_kernel, cut, carried, last, len(rows), len(...  108 us
    ppermute x10, waiting for transfers between devices, gather_start(): lax.ppermute(rows, 'expert', pair_moves(4, r))  59 us
    ppermute x8, waiting for transfers between devices, step_up(): return lax.ppermute(values, 'batch', shift_moves(1))  45.1 us
    pallas_call x1, Pallas kernels, attend_back(): pl.pallas_call(attend_back_kernel, in_specs=[INSIDE] * 7, out_specs=[INSI...  21.3 us
    ppermute x4, waiting for transfers between devices, scatter_start(): first_top = lax.ppermute(parts[1][:half].astype(low), 'expert', across)  18.6 us
    pallas_call x1, Pallas kernels, leave(): pl.pallas_call(partial(leave_kernel, len(pieces), cut, gain_at), in_specs...  15.1 us
    convert_element_type x15, other arithmetic, add_low(): return total.astype(jnp.bfloat16)  14.7 us
    ppermute x5, waiting for transfers between devices, gather_finish(): top = lax.ppermute(second[:half], 'expert', pair_moves(4, 1))  14.5 us
  transfers between devices with their start and end apart: 74, of which 40 were waited for; matrix products, arithmetic and copies ran while one was open for 11% of the time, Pallas kernels for 34%

profile of v4, /device:TPU:0, one launch (start us, length us, event | category | flops | bytes accessed | tf_op | source)
XLA Modules:
  0.0 560.3 jit_solution(18267939465067300898)
XLA Ops:
  29.8 7.3 %collective-permute-done.1 = bf16[48,4224]{1,0:T(8,128)(2,1)} collective-permute-done((bf16[48,4224]{1,0:T(8,128)(2,1)}, bf16[48,4224]{1,0:T(8,128)(2,1)}, u32[]{:S(2)}, u32[]{:S(2)}) %collective-permute-start.1) | collective-permute-done | bytes 405536 | tf_op jit(solution)/shard_map/ppermute | solution.py:940
  37.0 4.0 collective-permute-done.17.refs_6_
  44.6 10.9 %collective-permute-done.2 = bf16[48,4224]{1,0:T(8,128)(2,1)S(1)} collective-permute-done((bf16[48,4224]{1,0:T(8,128)(2,1)}, bf16[48,4224]{1,0:T(8,128)(2,1)S(1)}, u32[]{:S(2)}, u32[]{:S(2)}) %collective-permute-start.2) | collective-permute-done | bytes 405536 | tf_op jit(solution)/shard_map/ppermute | solution.py:936
  60.8 19.5 %collective-permute-done.3.refs_1_ = bf16[4,48,2688]{2,1,0:T(8,128)(2,1)} collective-permute-done((bf16[4,48,2688]{2,1,0:T(8,128)(2,1)S(1)}, bf16[4,48,2688]{2,1,0:T(8,128)(2,1)}, u32[]{:S(2)}, u32[]{:S(2)}) %collective-permute-start.3) | collective-permute-done | bytes 1032224 | tf_op jit(solution)/shard_map/ppermute | solution.py:818
  101.3 8.1 %enter.1 = (bf16[256,1536]{1,0:T(8,128)(2,1)}, bf16[256,1536]{1,0:T(8,128)(2,1)}, bf16[256,1024]{1,0:T(8,128)(2,1)}, f32[128,1536]{1,0:T(8,128)}) custom-call(s32[8,4]{1,0:T(8,128)} %concatenate.91.spots, bf16[256,1536]{1,0:T(8,128)(2,1)} %bitcast.173, f32[256,128]{1,0:T(8,128)} %copy.56.cosine, f32[256,128]{1,0:T(8,128)} %copy.57.sine, ...), custom_call_target="tpu_custom_call" | custom-call | flops 1 | bytes 1 | tf_op jit(solution)/shard_map/enter/pallas_call | solution.py:137
  118.1 8.8 %collective-permute-done.13 = bf16[256,1024]{1,0:T(8,128)(2,1)S(1)} collective-permute-done((bf16[256,1024]{1,0:T(8,128)(2,1)}, bf16[256,1024]{1,0:T(8,128)(2,1)S(1)}, u32[]{:S(2)}, u32[]{:S(2)}) %collective-permute-start.13) | collective-permute-done | bytes 524320 | tf_op jit(solution)/shard_map/ppermute | solution.py:818
  141.6 13.7 %attend.1 = (bf16[256,1536]{1,0:T(8,128)(2,1)}, f32[256,128]{1,0:T(8,128)}) custom-call(bf16[256,1536]{1,0:T(8,128)(2,1)} %get-tuple-element.91.query, bf16[768,1024]{1,0:T(8,128)(2,1)} %pad_maximum_fusion.3.keyval, f32[256,768]{1,0:T(8,128)} %and_select_fusion.1.bias), custom_call_target="tpu_custom_call" | custom-call | flops 1 | bytes 1 | tf_op jit(solution)/shard_map/attend/pallas_call | solution.py:203
  160.5 7.7 %project.1 = (f32[256,1536]{1,0:T(8,128)}, bf16[256,1664]{1,0:T(8,128)(2,1)}, f32[256,128]{1,0:T(8,128)}) custom-call(s32[8,4]{1,0:T(8,128)} %concatenate.91.spots, bf16[256,1536]{1,0:T(8,128)(2,1)} %get-tuple-element.97.attended, bf16[256,1536]{1,0:T(8,128)(2,1)} %bitcast.174, f32[128,1536]{1,0:T(8,128)} %get-tuple-element.98.small, ...), custom_call_target="tpu_custom_call" | custom-call | flops 1 | bytes 1 | tf_op jit(solution)/shard_map/project/pallas_call | solution.py:245
  170.8 18.9 %collective-permute-done.27.refs_1_ = bf16[256,1664]{1,0:T(8,128)(2,1)S(1)} collective-permute-done((bf16[256,1664]{1,0:T(8,128)(2,1)}, bf16[256,1664]{1,0:T(8,128)(2,1)S(1)}, u32[]{:S(2)}, u32[]{:S(2)}) %collective-permute-start.27) | collective-permute-done | bytes 852000 | tf_op jit(solution)/shard_map/ppermute | solution.py:818
  193.5 8.4 %collective-permute-done.29.refs_3_ = bf16[128,1664]{1,0:T(8,128)(2,1)} collective-permute-done((bf16[128,1664]{1,0:T(8,128)(2,1)S(1)}, bf16[128,1664]{1,0:T(8,128)(2,1)}, u32[]{:S(2)}, u32[]{:S(2)}) %collective-permute-start.29) | collective-permute-done | bytes 426016 | tf_op jit(solution)/shard_map/ppermute | solution.py:826
  202.5 62.7 %experts.2 = (bf16[8,3,3,64,1536]{4,3,2,1,0:T(8,128)(2,1)}, f32[1024,1536]{1,0:T(8,128)}, f32[1024,1664]{1,0:T(8,128)}) custom-call(s32[3]{0:T(128)} %pad_add_fusion.1.place, s32[1]{0:T(128)} %bitcast.61.first, bf16[8,3,3,64,1536]{4,3,2,1,0:T(8,128)(2,1)} %bitcast.171, bf16[256,1664]{1,0:T(8,128)(2,1)} %get-tuple-element.107.refs_0_.normed, ...), custom_call_target="tpu_custom_call" | custom-call | flops 1 | bytes 1 | tf_op jit(solution)/shard_map/experts/pallas_call | solution.py:727
  265.2 8.6 %all-gather.5.cloned.1.call-done = bf16[24,2,64,1536]{3,2,1,0:T(8,128)(2,1)} async-done(((bf16[3,2,64,1536]{3,2,1,0:T(8,128)(2,1)}), bf16[24,2,64,1536]{3,2,1,0:T(8,128)(2,1)}) %all-gather.5.cloned.1.call-update) | async-done | bytes 9437200 | tf_op jit(solution)/shard_map/all_gather | solution.py:1101
  273.7 45.6 %experts.3 = (bf16[3,2,64,1536]{3,2,1,0:T(8,128)(2,1)}, bf16[3,3,2,64,1536]{4,3,2,1,0:T(8,128)(2,1)}, bf16[2,3,2,64,1536]{4,3,2,1,0:T(8,128)(2,1)}, bf16[2,3,2,6...) custom-call(s32[3]{0:T(128)} %pad_add_fusion.1.place, s32[1]{0:T(128)} %bitcast.59.first, ...), custom_call_target="tpu_custom_call" | custom-call | flops 1 | bytes 1 | tf_op jit(solution)/shard_map/experts/pallas_call | solution.py:727
  325.6 8.5 %collective-permute-done.33 = bf16[128,1664]{1,0:T(8,128)(2,1)S(1)} collective-permute-done((bf16[128,1664]{1,0:T(8,128)(2,1)S(1)}, bf16[128,1664]{1,0:T(8,128)(2,1)S(1)}, u32[]{:S(2)}, u32[]{:S(2)}) %collective-permute-start.33) | collective-permute-done | bytes 426016 | tf_op jit(solution)/shard_map/ppermute | solution.py:845
  338.1 5.7 %collective-permute-done.31 = bf16[128,1664]{1,0:T(8,128)(2,1)S(1)} collective-permute-done((bf16[128,1664]{1,0:T(8,128)(2,1)S(1)}, bf16[128,1664]{1,0:T(8,128)(2,1)S(1)}, u32[]{:S(2)}, u32[]{:S(2)}) %collective-permute-start.31) | collective-permute-done | bytes 426016 | tf_op jit(solution)/shard_map/ppermute | solution.py:846
  345.8 8.9 %collective-permute-done.36 = bf16[128,1664]{1,0:T(8,128)(2,1)S(1)} collective-permute-done((bf16[128,1664]{1,0:T(8,128)(2,1)S(1)}, bf16[128,1664]{1,0:T(8,128)(2,1)S(1)}, u32[]{:S(2)}, u32[]{:S(2)}) %collective-permute-start.36) | collective-permute-done | bytes 426016 | tf_op jit(solution)/shard_map/ppermute | solution.py:858
  361.7 11.4 %turn.1 = (bf16[4,4,48,1664]{3,2,1,0:T(8,128)(2,1)}, bf16[4,4,48,1664]{3,2,1,0:T(8,128)(2,1)}, f32[256,1536]{1,0:T(8,128)}, bf16[256,1536]{1,0:T(8,128)(2,1)}) custom-call(s32[3]{0:T(128)} %pad_add_fusion.1.place, s32[8,4]{1,0:T(8,128)} %concatenate.91.spots, f32[256,1664]{1,0:T(8,128)} %pad_maximum_fusion.2.normed_grad, ...), custom_call_target="tpu_custom_call" | custom-call | flops 1 | bytes 1 | tf_op jit(solution)/shard_map/turn/pallas_call | solution.py:370
  379.0 21.3 %attend_back.1 = (bf16[256,1536]{1,0:T(8,128)(2,1)}, bf16[768,1024]{1,0:T(8,128)(2,1)}) custom-call(bf16[256,1536]{1,0:T(8,128)(2,1)} %get-tuple-element.128.head_grad, bf16[256,1536]{1,0:T(8,128)(2,1)} %get-tuple-element.91.query, bf16[768,1024]{1,0:T(8,128)(2,1)} %pad_maximum_fusion.3.keyval, f32[768,256]{1,0:T(8,128)} %and_select_fusion.bias, ...), custom_call_target="tpu_custom_call" | custom-call | flops 1 | bytes 1 | tf_op jit(solution)/shard_map/attend_back/pallas_call | solution.py:445
  406.3 5.0 collective-permute-done.44
  429.4 15.1 %leave.1 = (bf16[4,4,48,2688]{3,2,1,0:T(8,128)(2,1)}, bf16[4,4,48,2688]{3,2,1,0:T(8,128)(2,1)}, f32[256,1536]{1,0:T(8,128)}) custom-call(s32[3]{0:T(128)} %pad_add_fusion.1.place, s32[8,4]{1,0:T(8,128)} %concatenate.91.spots, f32[256,1024]{1,0:T(8,128)} %pad_maximum_fusion.4.keyval_sum, bf16[256,1536]{1,0:T(8,128)(2,1)} %get-tuple-element.138.query_grad, ...), custom_call_target="tpu_custom_call" | custom-call | flops 1 | bytes 1 | tf_op jit(solution)/shard_map/leave/pallas_call | solution.py:530
  466.3 11.7 %collective-permute-done.59 = bf16[2,48,2688]{2,1,0:T(8,128)(2,1)S(1)} collective-permute-done((bf16[2,48,2688]{2,1,0:T(8,128)(2,1)S(1)}, bf16[2,48,2688]{2,1,0:T(8,128)(2,1)S(1)}, u32[]{:S(2)}, u32[]{:S(2)}) %collective-permute-start.59) | collective-permute-done | bytes 516128 | tf_op jit(solution)/shard_map/ppermute | solution.py:844
  480.4 10.6 %collective-permute-done.56 = bf16[2,48,2688]{2,1,0:T(8,128)(2,1)S(1)} collective-permute-done((bf16[2,48,2688]{2,1,0:T(8,128)(2,1)S(1)}, bf16[2,48,2688]{2,1,0:T(8,128)(2,1)S(1)}, u32[]{:S(2)}, u32[]{:S(2)}) %collective-permute-start.56) | collective-permute-done | bytes 516128 | tf_op jit(solution)/shard_map/ppermute | solution.py:846
  509.9 28.4 %collective-permute-done.65 = bf16[48,2688]{1,0:T(8,128)(2,1)S(1)} collective-permute-done((bf16[48,2688]{1,0:T(8,128)(2,1)S(1)}, bf16[48,2688]{1,0:T(8,128)(2,1)S(1)}, u32[]{:S(2)}, u32[]{:S(2)}) %collective-permute-start.65) | collective-permute-done | bytes 258080 | tf_op jit(solution)/shard_map/ppermute | solution.py:936
  544.0 6.0 %unpack.1 = (f32[5,192,512]{2,1,0:T(8,128)}, f32[5,192,512]{2,1,0:T(8,128)}, f32[5,64,1536]{2,1,0:T(8,128)}) custom-call(bf16[1,3,3,64,1536]{4,3,2,1,0:T(8,128)(2,1)} %reduce-scatter.2.cloned.1.call-done.refs_0_, bf16[3,2,64,1536]{3,2,1,0:T(8,128)(2,1)} %get-tuple-element.156.refs_1_, bf16[2,3,2,64,1536]{4,3,2,1,0:T(8,128)(2,1)} %collective-permute-done.60.refs_2_, ...), custom_call_target="tpu_custom_call" | custom-call | flops 1 | bytes 1 | tf_op jit(solution)/shard_map/unpack/pallas_call | solution.py:783
  (323 shorter events, 188.7 us)
Async XLA Ops:
  7.2 195.3 %all-gather.7.cloned.1.call-start = ((), (), s32[]{:S(2)}) async-start(), calls=%async_computation.3 | async-start | bytes 15925248 | tf_op jit(solution)/shard_map/all_gather | solution.py:1101
  55.5 218.2 %all-gather.5.cloned.1.call-start = ((), (), s32[]{:S(2)}) async-start(), calls=%async_computation.2 | async-start | bytes 10616832 | tf_op jit(solution)/shard_map/all_gather | solution.py:1101
  58.8 21.6 %collective-permute-start.3 = (bf16[4,48,2688]{2,1,0:T(8,128)(2,1)S(1)}, bf16[4,48,2688]{2,1,0:T(8,128)(2,1)}, u32[]{:S(2)}, u32[]{:S(2)}) collective-permute-start(bf16[4,48,2688]{2,1,0:T(8,128)(2,1)S(1)} %pad_maximum_fusion.5.refs_0_), channel_id=1, source_target_pairs={{0,1},{1,0},{2,3},{3,2},{4,5},{5,4},{6,7},{7,6},{8,9},{9,8},{10,11... | collective-permute-start | bytes 3096584 | tf_op jit(solution)/shard_map/ppermute | solution.py:818
  60.3 21.2 %collective-permute-start.4 = (bf16[4,48,2688]{2,1,0:T(8,128)(2,1)S(1)}, bf16[4,48,2688]{2,1,0:T(8,128)(2,1)}, u32[]{:S(2)}, u32[]{:S(2)}) collective-permute-start(bf16[4,48,2688]{2,1,0:T(8,128)(2,1)S(1)} %pad_maximum_fusion.5.refs_0_), channel_id=1, source_target_pairs={{0,2},{1,3},{2,0},{3,1},{4,6},{5,7},{6,4},{7,5},{8,10},{9,11},{10,... | collective-permute-start | bytes 3096584 | tf_op jit(solution)/shard_map/ppermute | solution.py:818
  81.5 366.0 %reduce-scatter.2.cloned.1.call-start = ((), (), s32[]{:S(2)}) async-start(), calls=%async_computation.1 | async-start | bytes 15925248 | tf_op jit(solution)/shard_map/reduce_scatter | solution.py:928
  131.0 28.5 %collective-permute-start.23 = (bf16[4,48,1536]{2,1,0:T(8,128)(2,1)S(1)}, bf16[4,48,1536]{2,1,0:T(8,128)(2,1)S(1)}, u32[]{:S(2)}, u32[]{:S(2)}) collective-permute-start(bf16[4,48,1536]{2,1,0:T(8,128)(2,1)S(1)} %pad_maximum_fusion.8.refs_0_), channel_id=1, source_target_pairs={{0,4},{4,0},{8,12},{12,8},{16,20},{20,16},{24,28},{28,24},{1,5},{5... | collective-permute-start | bytes 1769480 | tf_op jit(solution)/shard_map/ppermute | solution.py:932
  131.0 28.5 %collective-permute-start.24 = (bf16[4,48,1536]{2,1,0:T(8,128)(2,1)}, bf16[4,48,1536]{2,1,0:T(8,128)(2,1)}, u32[]{:S(2)}, u32[]{:S(2)}) collective-permute-start(bf16[4,48,1536]{2,1,0:T(8,128)(2,1)} %collective-permute-done.11.refs_1_), channel_id=1, source_target_pairs={{0,4},{4,0},{8,12},{12,8},{16,20},{20,16},{24,28},{28,24},{1,5},{5... | collective-permute-start | bytes 1769480 | tf_op jit(solution)/shard_map/ppermute | solution.py:932
  131.5 28.0 %collective-permute-start.25 = (bf16[4,48,1536]{2,1,0:T(8,128)(2,1)}, bf16[4,48,1536]{2,1,0:T(8,128)(2,1)}, u32[]{:S(2)}, u32[]{:S(2)}) collective-permute-start(bf16[4,48,1536]{2,1,0:T(8,128)(2,1)} %collective-permute-done.12.refs_2_), channel_id=1, source_target_pairs={{0,4},{4,0},{8,12},{12,8},{16,20},{20,16},{24,28},{28,24},{1,5},{5... | collective-permute-start | bytes 1769480 | tf_op jit(solution)/shard_map/ppermute | solution.py:932
  168.2 21.5 %collective-permute-start.27 = (bf16[256,1664]{1,0:T(8,128)(2,1)}, bf16[256,1664]{1,0:T(8,128)(2,1)S(1)}, u32[]{:S(2)}, u32[]{:S(2)}) collective-permute-start(bf16[256,1664]{1,0:T(8,128)(2,1)} %get-tuple-element.107.refs_0_.normed), channel_id=1, source_target_pairs={{0,1},{1,0},{2,3},{3,2},{4,5},{5,4},{6,7},{7,6},{8,9},{9,8},{10,11... | collective-permute-start | bytes 2555912 | tf_op jit(solution)/shard_map/ppermute | solution.py:818
  169.4 21.2 %collective-permute-start.28 = (bf16[256,1664]{1,0:T(8,128)(2,1)}, bf16[256,1664]{1,0:T(8,128)(2,1)S(1)}, u32[]{:S(2)}, u32[]{:S(2)}) collective-permute-start(bf16[256,1664]{1,0:T(8,128)(2,1)} %get-tuple-element.107.refs_0_.normed), channel_id=1, source_target_pairs={{0,2},{1,3},{2,0},{3,1},{4,6},{5,7},{6,4},{7,5},{8,10},{9,11},{10,... | collective-permute-start | bytes 2555912 | tf_op jit(solution)/shard_map/ppermute | solution.py:818
  373.1 47.5 %collective-permute-start.47 = (bf16[4,4,48,1664]{3,2,1,0:T(8,128)(2,1)}, bf16[4,4,48,1664]{3,2,1,0:T(8,128)(2,1)}, u32[]{:S(2)}, u32[]{:S(2)}) collective-permute-start(bf16[4,4,48,1664]{3,2,1,0:T(8,128)(2,1)} %get-tuple-element.136), channel_id=1, source_target_pairs={{0,4},{4,0},{8,12},{12,8},{16,20},{20,16},{24,28},{28,24},{1,5},{5... | collective-permute-start | bytes 7667720 | tf_op jit(solution)/shard_map/ppermute | solution.py:932
  377.6 24.3 %collective-permute-start.40 = (bf16[256,1536]{1,0:T(8,128)(2,1)S(1)}, bf16[256,1536]{1,0:T(8,128)(2,1)S(1)}, u32[]{:S(2)}, u32[]{:S(2)}) collective-permute-start(bf16[256,1536]{1,0:T(8,128)(2,1)S(1)} %get-tuple-element.126), channel_id=1, source_target_pairs={{0,3},{1,2},{2,1},{3,0},{4,7},{5,6},{6,5},{7,4},{8,11},{9,10},{10,... | collective-permute-start | bytes 2359304 | tf_op jit(solution)/shard_map/ppermute | solution.py:884
  415.9 31.5 %collective-permute-start.52 = (bf16[3,2,64,1536]{3,2,1,0:T(8,128)(2,1)}, bf16[3,2,64,1536]{3,2,1,0:T(8,128)(2,1)}, u32[]{:S(2)}, u32[]{:S(2)}) collective-permute-start(bf16[3,2,64,1536]{3,2,1,0:T(8,128)(2,1)} %get-tuple-element.215), channel_id=1, source_target_pairs={{0,8},{4,12},{8,16},{12,20},{16,24},{20,28},{24,0},{28,4},{1,9},{5... | collective-permute-start | bytes 3538952 | tf_op jit(solution)/shard_map/ppermute | solution.py:936
  423.8 20.7 %collective-permute-start.51 = (bf16[2,48,1664]{2,1,0:T(8,128)(2,1)}, bf16[2,48,1664]{2,1,0:T(8,128)(2,1)}, u32[]{:S(2)}, u32[]{:S(2)}) collective-permute-start(bf16[2,48,1664]{2,1,0:T(8,128)(2,1)} %get-tuple-element.247), channel_id=1, source_target_pairs={{0,1},{1,0},{2,3},{3,2},{4,5},{5,4},{6,7},{7,6},{8,9},{9,8},{10,11... | collective-permute-start | bytes 958472 | tf_op jit(solution)/shard_map/ppermute | solution.py:844
  424.5 21.9 %collective-permute-start.50 = (bf16[2,48,1664]{2,1,0:T(8,128)(2,1)}, bf16[2,48,1664]{2,1,0:T(8,128)(2,1)}, u32[]{:S(2)}, u32[]{:S(2)}) collective-permute-start(bf16[2,48,1664]{2,1,0:T(8,128)(2,1)} %get-tuple-element.248), channel_id=1, source_target_pairs={{0,2},{1,3},{2,0},{3,1},{4,6},{5,7},{6,4},{7,5},{8,10},{9,11},{10,... | collective-permute-start | bytes 958472 | tf_op jit(solution)/shard_map/ppermute | solution.py:845
  426.6 20.9 %collective-permute-start.48 = (bf16[2,48,1664]{2,1,0:T(8,128)(2,1)}, bf16[2,48,1664]{2,1,0:T(8,128)(2,1)}, u32[]{:S(2)}, u32[]{:S(2)}) collective-permute-start(bf16[2,48,1664]{2,1,0:T(8,128)(2,1)} %slice_bitcast_fusion.13), channel_id=1, source_target_pairs={{0,1},{1,0},{2,3},{3,2},{4,5},{5,4},{6,7},{7,6},{8,9},{9,8},{10,11... | collective-permute-start | bytes 958472 | tf_op jit(solution)/shard_map/ppermute | solution.py:846
  451.4 42.2 %collective-permute-start.54 = (bf16[2,48,1664]{2,1,0:T(8,128)(2,1)S(1)}, bf16[2,48,1664]{2,1,0:T(8,128)(2,1)S(1)}, u32[]{:S(2)}, u32[]{:S(2)}) collective-permute-start(bf16[2,48,1664]{2,1,0:T(8,128)(2,1)S(1)} %copy-done.27), channel_id=1, source_target_pairs={{0,2},{1,3},{2,0},{3,1},{4,6},{5,7},{6,4},{7,5},{8,10},{9,11},{10,... | collective-permute-start | bytes 958472 | tf_op jit(solution)/shard_map/ppermute | solution.py:858
  452.1 41.5 %collective-permute-start.55 = (bf16[2,48,1664]{2,1,0:T(8,128)(2,1)S(1)}, bf16[2,48,1664]{2,1,0:T(8,128)(2,1)S(1)}, u32[]{:S(2)}, u32[]{:S(2)}) collective-permute-start(bf16[2,48,1664]{2,1,0:T(8,128)(2,1)S(1)} %fusion.13), channel_id=1, source_target_pairs={{0,1},{1,0},{2,3},{3,2},{4,5},{5,4},{6,7},{7,6},{8,9},{9,8},{10,11... | collective-permute-start | bytes 958472 | tf_op jit(solution)/shard_map/ppermute | solution.py:859
  460.8 30.7 %collective-permute-start.61 = (bf16[3,2,64,1536]{3,2,1,0:T(8,128)(2,1)S(1)}, bf16[3,2,64,1536]{3,2,1,0:T(8,128)(2,1)S(1)}, u32[]{:S(2)}, u32[]{:S(2)}) collective-permute-start(bf16[3,2,64,1536]{3,2,1,0:T(8,128)(2,1)S(1)} %fusion), channel_id=1, source_target_pairs={{0,8},{4,12},{8,16},{12,20},{16,24},{20,28},{24,0},{28,4},{1,9},{5... | collective-permute-start | bytes 3538952 | tf_op jit(solution)/shard_map/ppermute | solution.py:936
  496.5 42.6 %collective-permute-start.68 = (bf16[48,1664]{1,0:T(8,128)(2,1)S(1)}, bf16[48,1664]{1,0:T(8,128)(2,1)S(1)}, u32[]{:S(2)}, u32[]{:S(2)}) collective-permute-start(bf16[48,1664]{1,0:T(8,128)(2,1)S(1)} %get-tuple-element.237), channel_id=1, source_target_pairs={{0,24},{4,28},{8,0},{12,4},{16,8},{20,12},{24,16},{28,20},{1,25},{... | collective-permute-start | bytes 479240 | tf_op jit(solution)/shard_map/ppermute | solution.py:940
  499.0 40.1 %collective-permute-start.66 = (bf16[3,2,64,1536]{3,2,1,0:T(8,128)(2,1)S(1)}, bf16[3,2,64,1536]{3,2,1,0:T(8,128)(2,1)S(1)}, u32[]{:S(2)}, u32[]{:S(2)}) collective-permute-start(bf16[3,2,64,1536]{3,2,1,0:T(8,128)(2,1)S(1)} %copy-done.21), channel_id=1, source_target_pairs={{0,24},{4,28},{8,0},{12,4},{16,8},{20,12},{24,16},{28,20},{1,25},{... | collective-permute-start | bytes 3538952 | tf_op jit(solution)/shard_map/ppermute | solution.py:940
  505.0 33.4 %collective-permute-start.65 = (bf16[48,2688]{1,0:T(8,128)(2,1)S(1)}, bf16[48,2688]{1,0:T(8,128)(2,1)S(1)}, u32[]{:S(2)}, u32[]{:S(2)}) collective-permute-start(bf16[48,2688]{1,0:T(8,128)(2,1)S(1)} %get-tuple-element.232), channel_id=1, source_target_pairs={{0,8},{4,12},{8,16},{12,20},{16,24},{20,28},{24,0},{28,4},{1,9},{5... | collective-permute-start | bytes 774152 | tf_op jit(solution)/shard_map/ppermute | solution.py:936
  506.0 35.8 %collective-permute-start.70 = (bf16[48,1664]{1,0:T(8,128)(2,1)S(1)}, bf16[48,1664]{1,0:T(8,128)(2,1)S(1)}, u32[]{:S(2)}, u32[]{:S(2)}) collective-permute-start(bf16[48,1664]{1,0:T(8,128)(2,1)S(1)} %fusion.37), channel_id=1, source_target_pairs={{0,8},{4,12},{8,16},{12,20},{16,24},{20,28},{24,0},{28,4},{1,9},{5... | collective-permute-start | bytes 479240 | tf_op jit(solution)/shard_map/ppermute | solution.py:936
  506.5 43.5 %collective-permute-start.64 = (bf16[48,2688]{1,0:T(8,128)(2,1)S(1)}, bf16[48,2688]{1,0:T(8,128)(2,1)S(1)}, u32[]{:S(2)}, u32[]{:S(2)}) collective-permute-start(bf16[48,2688]{1,0:T(8,128)(2,1)S(1)} %get-tuple-element.231), channel_id=1, source_target_pairs={{0,24},{4,28},{8,0},{12,4},{16,8},{20,12},{24,16},{28,20},{1,25},{... | collective-permute-start | bytes 774152 | tf_op jit(solution)/shard_map/ppermute | solution.py:940
  (88 other events, 1166.7 us)
Sparse Core Ops, SparseCore 0:
  55.6 126.8 all-gather.6
  184.7 88.9 all-gather.4
  276.0 143.9 reduce-scatter.1

commit v5 on v4

--- a/solution.py
+++ b/solution.py
@@ -1230,17 +1230,20 @@
     if cut:
         received = exchange_cores(after(qkv_found[0], (totals[0], out_state[1:], up_part)))
         out_plane = scatter_finish(out_state)
-        up_term = step_up(add_low(rest[0], near[0], after(up_part, received)))
-        down_term = step_down(after(down_sum, up_term))
+        down_term = step_down(after(down_sum, up_part))
         qkv_parts = join_cores(qkv_found[1], after(received, out_plane))
-        qkv_state = after(scatter_start(qkv_parts), up_term)
+        qkv_parts[1:3] = after(qkv_parts[1:3], down_term)
+        qkv_state = scatter_start(qkv_parts)
+        up_sum = add_low(rest[0], near[0], up_part)
+        up_term = step_up(after(up_sum, qkv_state[1:3]))
+        out_line = line_start(out_plane)
         qkv_plane = scatter_finish(qkv_state)
-        out_sum = line_finish(line_start(out_plane))
+        out_sum = line_finish(out_line)
         qkv_state = line_start(qkv_plane)
         near, down_term, up_term = after((near, down_term, up_term), qkv_plane)
         terms = [[(totals[0], 0)], [(own, None), (near, 1), (down_term, None), (up_term, None)]]
         expert_totals = unpack(terms, gate_weight.shape, down_weight.shape)
-        qkv_sum = line_finish(qkv_state, down_term)
+        qkv_sum = line_finish(qkv_state, up_term)
     else:
         out_sum = scatter_whole(out_found)
         qkv_sum = scatter_whole(qkv_found)

time: 568 us -> 577 us (1.016)
  waiting for transfers between devices: 210 us -> 220 us
    ppermute x4, waiting for transfers between devices: 13.5 us -> 34.7 us  [scatter_start(): bottom = lax.ppermute(parts[3][half:].astype(low), 'expert', along)]
    ppermute x4, waiting for transfers between devices: 13.3 us -> 1.91 us  [scatter_start(): top = lax.ppermute(parts[3][:half].astype(low), 'expert', across)]
    ppermute x4, waiting for transfers between devices: 18.6 us -> 8.02 us  [scatter_start(): first_top = lax.ppermute(parts[1][:half].astype(low), 'expert', across)]
  transfers between devices with their start and end apart: 74 -> 74, of which waited for: 40 -> 39; matrix products, arithmetic and copies ran while one was open for 11% -> 11% of each run, Pallas kernels for 34% -> 34%
where the time goes in v5:
time: 577 us; the launch traced here: 570 us
  waiting for transfers between devices  220 us (38%)
  Pallas kernels  195 us (34%)
  starting transfers between devices  67 us (12%)
  other arithmetic  36 us (6%)
  local copies, waits for them, and re-layouts  34.7 us (6%)
  between operations  15.1 us (3%)
    pallas_call x2, Pallas kernels, expert_pass(): pl.pallas_call(partial(expert_kernel, cut, carried, last, len(rows), len(...  108 us
    ppermute x10, waiting for transfers between devices, gather_start(): lax.ppermute(rows, 'expert', pair_moves(4, r))  59 us
    ppermute x8, waiting for transfers between devices, step_up(): return lax.ppermute(values, 'batch', shift_moves(1))  45.1 us
    ppermute x4, waiting for transfers between devices, scatter_start(): bottom = lax.ppermute(parts[3][half:].astype(low), 'expert', along)  34.7 us
    pallas_call x1, Pallas kernels, attend_back(): pl.pallas_call(attend_back_kernel, in_specs=[INSIDE] * 7, out_specs=[INSI...  21.3 us
    convert_element_type x15, other arithmetic, add_low(): return total.astype(jnp.bfloat16)  15.3 us
    pallas_call x1, Pallas kernels, leave(): pl.pallas_call(partial(leave_kernel, len(pieces), cut, gain_at), in_specs...  15 us
    ppermute x5, waiting for transfers between devices, gather_finish(): top = lax.ppermute(second[:half], 'expert', pair_moves(4, 1))  14.5 us
  transfers between devices with their start and end apart: 74, of which 39 were waited for; matrix products, arithmetic and copies ran while one was open for 11% of the time, Pallas kernels for 34%

profile of v5, /device:TPU:0, one launch (start us, length us, event | category | flops | bytes accessed | tf_op | source)
XLA Modules:
  0.0 569.5 jit_solution(5630881252074651226)
XLA Ops:
  29.8 7.3 %collective-permute-done.1 = bf16[48,4224]{1,0:T(8,128)(2,1)} collective-permute-done((bf16[48,4224]{1,0:T(8,128)(2,1)}, bf16[48,4224]{1,0:T(8,128)(2,1)}, u32[]{:S(2)}, u32[]{:S(2)}) %collective-permute-start.1) | collective-permute-done | bytes 405536 | tf_op jit(solution)/shard_map/ppermute | solution.py:940
  44.6 10.9 %collective-permute-done.2 = bf16[48,4224]{1,0:T(8,128)(2,1)S(1)} collective-permute-done((bf16[48,4224]{1,0:T(8,128)(2,1)}, bf16[48,4224]{1,0:T(8,128)(2,1)S(1)}, u32[]{:S(2)}, u32[]{:S(2)}) %collective-permute-start.2) | collective-permute-done | bytes 405536 | tf_op jit(solution)/shard_map/ppermute | solution.py:936
  60.8 19.5 %collective-permute-done.3.refs_1_ = bf16[4,48,2688]{2,1,0:T(8,128)(2,1)} collective-permute-done((bf16[4,48,2688]{2,1,0:T(8,128)(2,1)S(1)}, bf16[4,48,2688]{2,1,0:T(8,128)(2,1)}, u32[]{:S(2)}, u32[]{:S(2)}) %collective-permute-start.3) | collective-permute-done | bytes 1032224 | tf_op jit(solution)/shard_map/ppermute | solution.py:818
  101.3 8.1 %enter.1 = (bf16[256,1536]{1,0:T(8,128)(2,1)}, bf16[256,1536]{1,0:T(8,128)(2,1)}, bf16[256,1024]{1,0:T(8,128)(2,1)}, f32[128,1536]{1,0:T(8,128)}) custom-call(s32[8,4]{1,0:T(8,128)} %concatenate.91.spots, bf16[256,1536]{1,0:T(8,128)(2,1)} %bitcast.171, f32[256,128]{1,0:T(8,128)} %copy.56.cosine, f32[256,128]{1,0:T(8,128)} %copy.57.sine, ...), custom_call_target="tpu_custom_call" | custom-call | flops 1 | bytes 1 | tf_op jit(solution)/shard_map/enter/pallas_call | solution.py:137
  118.1 8.8 %collective-permute-done.13 = bf16[256,1024]{1,0:T(8,128)(2,1)S(1)} collective-permute-done((bf16[256,1024]{1,0:T(8,128)(2,1)}, bf16[256,1024]{1,0:T(8,128)(2,1)S(1)}, u32[]{:S(2)}, u32[]{:S(2)}) %collective-permute-start.13) | collective-permute-done | bytes 524320 | tf_op jit(solution)/shard_map/ppermute | solution.py:818
  141.5 13.7 %attend.1 = (bf16[256,1536]{1,0:T(8,128)(2,1)}, f32[256,128]{1,0:T(8,128)}) custom-call(bf16[256,1536]{1,0:T(8,128)(2,1)} %get-tuple-element.88.query, bf16[768,1024]{1,0:T(8,128)(2,1)} %pad_maximum_fusion.3.keyval, f32[256,768]{1,0:T(8,128)} %and_select_fusion.1.bias), custom_call_target="tpu_custom_call" | custom-call | flops 1 | bytes 1 | tf_op jit(solution)/shard_map/attend/pallas_call | solution.py:203
  160.6 7.7 %project.1 = (f32[256,1536]{1,0:T(8,128)}, bf16[256,1664]{1,0:T(8,128)(2,1)}, f32[256,128]{1,0:T(8,128)}) custom-call(s32[8,4]{1,0:T(8,128)} %concatenate.91.spots, bf16[256,1536]{1,0:T(8,128)(2,1)} %get-tuple-element.94.attended, bf16[256,1536]{1,0:T(8,128)(2,1)} %bitcast.172, f32[128,1536]{1,0:T(8,128)} %get-tuple-element.95.small, ...), custom_call_target="tpu_custom_call" | custom-call | flops 1 | bytes 1 | tf_op jit(solution)/shard_map/project/pallas_call | solution.py:245
  170.9 18.9 %collective-permute-done.27.refs_1_ = bf16[256,1664]{1,0:T(8,128)(2,1)S(1)} collective-permute-done((bf16[256,1664]{1,0:T(8,128)(2,1)}, bf16[256,1664]{1,0:T(8,128)(2,1)S(1)}, u32[]{:S(2)}, u32[]{:S(2)}) %collective-permute-start.27) | collective-permute-done | bytes 852000 | tf_op jit(solution)/shard_map/ppermute | solution.py:818
  193.5 8.4 %collective-permute-done.29.refs_3_ = bf16[128,1664]{1,0:T(8,128)(2,1)} collective-permute-done((bf16[128,1664]{1,0:T(8,128)(2,1)S(1)}, bf16[128,1664]{1,0:T(8,128)(2,1)}, u32[]{:S(2)}, u32[]{:S(2)}) %collective-permute-start.29) | collective-permute-done | bytes 426016 | tf_op jit(solution)/shard_map/ppermute | solution.py:826
  202.5 62.7 %experts.2 = (bf16[8,3,3,64,1536]{4,3,2,1,0:T(8,128)(2,1)}, f32[1024,1536]{1,0:T(8,128)}, f32[1024,1664]{1,0:T(8,128)}) custom-call(s32[3]{0:T(128)} %pad_add_fusion.1.place, s32[1]{0:T(128)} %bitcast.61.first, bf16[8,3,3,64,1536]{4,3,2,1,0:T(8,128)(2,1)} %bitcast.169, bf16[256,1664]{1,0:T(8,128)(2,1)} %get-tuple-element.104.refs_0_.normed, ...), custom_call_target="tpu_custom_call" | custom-call | flops 1 | bytes 1 | tf_op jit(solution)/shard_map/experts/pallas_call | solution.py:727
  265.2 8.5 %all-gather.5.cloned.1.call-done = bf16[24,2,64,1536]{3,2,1,0:T(8,128)(2,1)} async-done(((bf16[3,2,64,1536]{3,2,1,0:T(8,128)(2,1)}), bf16[24,2,64,1536]{3,2,1,0:T(8,128)(2,1)}) %all-gather.5.cloned.1.call-update) | async-done | bytes 9437200 | tf_op jit(solution)/shard_map/all_gather | solution.py:1101
  273.7 45.5 %experts.3 = (bf16[3,2,64,1536]{3,2,1,0:T(8,128)(2,1)}, bf16[3,3,2,64,1536]{4,3,2,1,0:T(8,128)(2,1)}, bf16[2,3,2,64,1536]{4,3,2,1,0:T(8,128)(2,1)}, bf16[2,3,2,6...) custom-call(s32[3]{0:T(128)} %pad_add_fusion.1.place, s32[1]{0:T(128)} %bitcast.59.first, ...), custom_call_target="tpu_custom_call" | custom-call | flops 1 | bytes 1 | tf_op jit(solution)/shard_map/experts/pallas_call | solution.py:727
  325.5 8.5 %collective-permute-done.33 = bf16[128,1664]{1,0:T(8,128)(2,1)S(1)} collective-permute-done((bf16[128,1664]{1,0:T(8,128)(2,1)S(1)}, bf16[128,1664]{1,0:T(8,128)(2,1)S(1)}, u32[]{:S(2)}, u32[]{:S(2)}) %collective-permute-start.33) | collective-permute-done | bytes 426016 | tf_op jit(solution)/shard_map/ppermute | solution.py:845
  338.0 5.7 collective-permute-done.31
  345.7 8.9 %collective-permute-done.36 = bf16[128,1664]{1,0:T(8,128)(2,1)S(1)} collective-permute-done((bf16[128,1664]{1,0:T(8,128)(2,1)S(1)}, bf16[128,1664]{1,0:T(8,128)(2,1)S(1)}, u32[]{:S(2)}, u32[]{:S(2)}) %collective-permute-start.36) | collective-permute-done | bytes 426016 | tf_op jit(solution)/shard_map/ppermute | solution.py:858
  361.7 11.5 %turn.1 = (bf16[4,4,48,1664]{3,2,1,0:T(8,128)(2,1)}, bf16[4,4,48,1664]{3,2,1,0:T(8,128)(2,1)}, f32[256,1536]{1,0:T(8,128)}, bf16[256,1536]{1,0:T(8,128)(2,1)}) custom-call(s32[3]{0:T(128)} %pad_add_fusion.1.place, s32[8,4]{1,0:T(8,128)} %concatenate.91.spots, f32[256,1664]{1,0:T(8,128)} %pad_maximum_fusion.2.normed_grad, ...), custom_call_target="tpu_custom_call" | custom-call | flops 1 | bytes 1 | tf_op jit(solution)/shard_map/turn/pallas_call | solution.py:370
  379.0 21.3 %attend_back.1 = (bf16[256,1536]{1,0:T(8,128)(2,1)}, bf16[768,1024]{1,0:T(8,128)(2,1)}) custom-call(bf16[256,1536]{1,0:T(8,128)(2,1)} %get-tuple-element.125.head_grad, bf16[256,1536]{1,0:T(8,128)(2,1)} %get-tuple-element.88.query, bf16[768,1024]{1,0:T(8,128)(2,1)} %pad_maximum_fusion.3.keyval, f32[768,256]{1,0:T(8,128)} %and_select_fusion.bias, ...), custom_call_target="tpu_custom_call" | custom-call | flops 1 | bytes 1 | tf_op jit(solution)/shard_map/attend_back/pallas_call | solution.py:445
  406.2 5.0 collective-permute-done.44
  429.4 15.0 %leave.1 = (bf16[4,4,48,2688]{3,2,1,0:T(8,128)(2,1)}, bf16[4,4,48,2688]{3,2,1,0:T(8,128)(2,1)}, f32[256,1536]{1,0:T(8,128)}) custom-call(s32[3]{0:T(128)} %pad_add_fusion.1.place, s32[8,4]{1,0:T(8,128)} %concatenate.91.spots, f32[256,1024]{1,0:T(8,128)} %pad_maximum_fusion.4.keyval_sum, bf16[256,1536]{1,0:T(8,128)(2,1)} %get-tuple-element.135.query_grad, ...), custom_call_target="tpu_custom_call" | custom-call | flops 1 | bytes 1 | tf_op jit(solution)/shard_map/leave/pallas_call | solution.py:530
  448.9 8.9 %collective-permute-done.65.refs_2_ = bf16[2,3,2,64,1536]{4,3,2,1,0:T(8,128)(2,1)S(1)} collective-permute-done((bf16[2,3,2,64,1536]{4,3,2,1,0:T(8,128)(2,1)}, bf16[2,3,2,64,1536]{4,3,2,1,0:T(8,128)(2,1)S(1)}, u32[]{:S(2)}, u32[]{:S(2)}) %collective-permute-start.65) | collective-permute-done | bytes 2359328 | tf_op jit(solution)/shard_map/ppermute | solution.py:932
  470.4 5.7 collective-permute-done.56.refs_3_
  479.5 21.2 %collective-permute-done.60 = bf16[2,48,2688]{2,1,0:T(8,128)(2,1)S(1)} collective-permute-done((bf16[2,48,2688]{2,1,0:T(8,128)(2,1)S(1)}, bf16[2,48,2688]{2,1,0:T(8,128)(2,1)S(1)}, u32[]{:S(2)}, u32[]{:S(2)}) %collective-permute-start.60) | collective-permute-done | bytes 516128 | tf_op jit(solution)/shard_map/ppermute | solution.py:845
  519.1 28.5 %collective-permute-done.64 = bf16[48,2688]{1,0:T(8,128)(2,1)S(1)} collective-permute-done((bf16[48,2688]{1,0:T(8,128)(2,1)S(1)}, bf16[48,2688]{1,0:T(8,128)(2,1)S(1)}, u32[]{:S(2)}, u32[]{:S(2)}) %collective-permute-start.64) | collective-permute-done | bytes 258080 | tf_op jit(solution)/shard_map/ppermute | solution.py:936
  553.3 6.0 %unpack.1 = (f32[5,192,512]{2,1,0:T(8,128)}, f32[5,192,512]{2,1,0:T(8,128)}, f32[5,64,1536]{2,1,0:T(8,128)}) custom-call(bf16[1,3,3,64,1536]{4,3,2,1,0:T(8,128)(2,1)} %reduce-scatter.2.cloned.1.call-done.refs_0_, bf16[3,2,64,1536]{3,2,1,0:T(8,128)(2,1)} %get-tuple-element.150.refs_1_, bf16[2,3,2,64,1536]{4,3,2,1,0:T(8,128)(2,1)} %copy-done.11, ...), custom_call_target="tpu_custom_call" | custom-call | flops 1 | bytes 1 | tf_op jit(solution)/shard_map/unpack/pallas_call | solution.py:783
  (327 shorter events, 188.5 us)
Async XLA Ops:
  7.2 195.3 %all-gather.7.cloned.1.call-start = ((), (), s32[]{:S(2)}) async-start(), calls=%async_computation.3 | async-start | bytes 15925248 | tf_op jit(solution)/shard_map/all_gather | solution.py:1101
  55.5 218.2 %all-gather.5.cloned.1.call-start = ((), (), s32[]{:S(2)}) async-start(), calls=%async_computation.2 | async-start | bytes 10616832 | tf_op jit(solution)/shard_map/all_gather | solution.py:1101
  58.8 21.6 %collective-permute-start.3 = (bf16[4,48,2688]{2,1,0:T(8,128)(2,1)S(1)}, bf16[4,48,2688]{2,1,0:T(8,128)(2,1)}, u32[]{:S(2)}, u32[]{:S(2)}) collective-permute-start(bf16[4,48,2688]{2,1,0:T(8,128)(2,1)S(1)} %pad_maximum_fusion.5.refs_0_), channel_id=1, source_target_pairs={{0,1},{1,0},{2,3},{3,2},{4,5},{5,4},{6,7},{7,6},{8,9},{9,8},{10,11... | collective-permute-start | bytes 3096584 | tf_op jit(solution)/shard_map/ppermute | solution.py:818
  81.5 365.9 %reduce-scatter.2.cloned.1.call-start = ((), (), s32[]{:S(2)}) async-start(), calls=%async_computation.1 | async-start | bytes 15925248 | tf_op jit(solution)/shard_map/reduce_scatter | solution.py:928
  131.0 28.5 %collective-permute-start.23 = (bf16[4,48,1536]{2,1,0:T(8,128)(2,1)S(1)}, bf16[4,48,1536]{2,1,0:T(8,128)(2,1)S(1)}, u32[]{:S(2)}, u32[]{:S(2)}) collective-permute-start(bf16[4,48,1536]{2,1,0:T(8,128)(2,1)S(1)} %pad_maximum_fusion.8.refs_0_), channel_id=1, source_target_pairs={{0,4},{4,0},{8,12},{12,8},{16,20},{20,16},{24,28},{28,24},{1,5},{5... | collective-permute-start | bytes 1769480 | tf_op jit(solution)/shard_map/ppermute | solution.py:932
  131.0 28.5 %collective-permute-start.24 = (bf16[4,48,1536]{2,1,0:T(8,128)(2,1)}, bf16[4,48,1536]{2,1,0:T(8,128)(2,1)}, u32[]{:S(2)}, u32[]{:S(2)}) collective-permute-start(bf16[4,48,1536]{2,1,0:T(8,128)(2,1)} %collective-permute-done.11.refs_1_), channel_id=1, source_target_pairs={{0,4},{4,0},{8,12},{12,8},{16,20},{20,16},{24,28},{28,24},{1,5},{5... | collective-permute-start | bytes 1769480 | tf_op jit(solution)/shard_map/ppermute | solution.py:932
  131.5 28.0 %collective-permute-start.25 = (bf16[4,48,1536]{2,1,0:T(8,128)(2,1)}, bf16[4,48,1536]{2,1,0:T(8,128)(2,1)}, u32[]{:S(2)}, u32[]{:S(2)}) collective-permute-start(bf16[4,48,1536]{2,1,0:T(8,128)(2,1)} %collective-permute-done.12.refs_2_), channel_id=1, source_target_pairs={{0,4},{4,0},{8,12},{12,8},{16,20},{20,16},{24,28},{28,24},{1,5},{5... | collective-permute-start | bytes 1769480 | tf_op jit(solution)/shard_map/ppermute | solution.py:932
  168.3 21.5 %collective-permute-start.27 = (bf16[256,1664]{1,0:T(8,128)(2,1)}, bf16[256,1664]{1,0:T(8,128)(2,1)S(1)}, u32[]{:S(2)}, u32[]{:S(2)}) collective-permute-start(bf16[256,1664]{1,0:T(8,128)(2,1)} %get-tuple-element.104.refs_0_.normed), channel_id=1, source_target_pairs={{0,1},{1,0},{2,3},{3,2},{4,5},{5,4},{6,7},{7,6},{8,9},{9,8},{10,11... | collective-permute-start | bytes 2555912 | tf_op jit(solution)/shard_map/ppermute | solution.py:818
  169.4 21.2 %collective-permute-start.28 = (bf16[256,1664]{1,0:T(8,128)(2,1)}, bf16[256,1664]{1,0:T(8,128)(2,1)S(1)}, u32[]{:S(2)}, u32[]{:S(2)}) collective-permute-start(bf16[256,1664]{1,0:T(8,128)(2,1)} %get-tuple-element.104.refs_0_.normed), channel_id=1, source_target_pairs={{0,2},{1,3},{2,0},{3,1},{4,6},{5,7},{6,4},{7,5},{8,10},{9,11},{10,... | collective-permute-start | bytes 2555912 | tf_op jit(solution)/shard_map/ppermute | solution.py:818
  373.1 47.5 %collective-permute-start.47 = (bf16[4,4,48,1664]{3,2,1,0:T(8,128)(2,1)}, bf16[4,4,48,1664]{3,2,1,0:T(8,128)(2,1)}, u32[]{:S(2)}, u32[]{:S(2)}) collective-permute-start(bf16[4,4,48,1664]{3,2,1,0:T(8,128)(2,1)} %get-tuple-element.133), channel_id=1, source_target_pairs={{0,4},{4,0},{8,12},{12,8},{16,20},{20,16},{24,28},{28,24},{1,5},{5... | collective-permute-start | bytes 7667720 | tf_op jit(solution)/shard_map/ppermute | solution.py:932
  377.6 24.3 %collective-permute-start.40 = (bf16[256,1536]{1,0:T(8,128)(2,1)S(1)}, bf16[256,1536]{1,0:T(8,128)(2,1)S(1)}, u32[]{:S(2)}, u32[]{:S(2)}) collective-permute-start(bf16[256,1536]{1,0:T(8,128)(2,1)S(1)} %get-tuple-element.123), channel_id=1, source_target_pairs={{0,3},{1,2},{2,1},{3,0},{4,7},{5,6},{6,5},{7,4},{8,11},{9,10},{10,... | collective-permute-start | bytes 2359304 | tf_op jit(solution)/shard_map/ppermute | solution.py:884
  415.9 31.4 %collective-permute-start.52 = (bf16[3,2,64,1536]{3,2,1,0:T(8,128)(2,1)}, bf16[3,2,64,1536]{3,2,1,0:T(8,128)(2,1)}, u32[]{:S(2)}, u32[]{:S(2)}) collective-permute-start(bf16[3,2,64,1536]{3,2,1,0:T(8,128)(2,1)} %get-tuple-element.209), channel_id=1, source_target_pairs={{0,8},{4,12},{8,16},{12,20},{16,24},{20,28},{24,0},{28,4},{1,9},{5... | collective-permute-start | bytes 3538952 | tf_op jit(solution)/shard_map/ppermute | solution.py:936
  424.5 21.8 %collective-permute-start.50 = (bf16[2,48,1664]{2,1,0:T(8,128)(2,1)S(1)}, bf16[2,48,1664]{2,1,0:T(8,128)(2,1)}, u32[]{:S(2)}, u32[]{:S(2)}) collective-permute-start(bf16[2,48,1664]{2,1,0:T(8,128)(2,1)S(1)} %get-tuple-element.242), channel_id=1, source_target_pairs={{0,2},{1,3},{2,0},{3,1},{4,6},{5,7},{6,4},{7,5},{8,10},{9,11},{10,... | collective-permute-start | bytes 958472 | tf_op jit(solution)/shard_map/ppermute | solution.py:845
  448.0 28.2 %collective-permute-start.56 = (bf16[3,2,64,1536]{3,2,1,0:T(8,128)(2,1)}, bf16[3,2,64,1536]{3,2,1,0:T(8,128)(2,1)S(1)}, u32[]{:S(2)}, u32[]{:S(2)}) collective-permute-start(bf16[3,2,64,1536]{3,2,1,0:T(8,128)(2,1)} %get-tuple-element.143), channel_id=1, source_target_pairs={{0,24},{4,28},{8,0},{12,4},{16,8},{20,12},{24,16},{28,20},{1,25},{... | collective-permute-start | bytes 3538952 | tf_op jit(solution)/shard_map/ppermute | solution.py:940
  468.4 33.9 %collective-permute-start.54 = (bf16[2,48,1664]{2,1,0:T(8,128)(2,1)S(1)}, bf16[2,48,1664]{2,1,0:T(8,128)(2,1)S(1)}, u32[]{:S(2)}, u32[]{:S(2)}) collective-permute-start(bf16[2,48,1664]{2,1,0:T(8,128)(2,1)S(1)} %copy-done.29), channel_id=1, source_target_pairs={{0,2},{1,3},{2,0},{3,1},{4,6},{5,7},{6,4},{7,5},{8,10},{9,11},{10,... | collective-permute-start | bytes 958472 | tf_op jit(solution)/shard_map/ppermute | solution.py:858
  469.2 33.8 %collective-permute-start.55 = (bf16[2,48,1664]{2,1,0:T(8,128)(2,1)S(1)}, bf16[2,48,1664]{2,1,0:T(8,128)(2,1)S(1)}, u32[]{:S(2)}, u32[]{:S(2)}) collective-permute-start(bf16[2,48,1664]{2,1,0:T(8,128)(2,1)S(1)} %fusion.14), channel_id=1, source_target_pairs={{0,1},{1,0},{2,3},{3,2},{4,5},{5,4},{6,7},{7,6},{8,9},{9,8},{10,11... | collective-permute-start | bytes 958472 | tf_op jit(solution)/shard_map/ppermute | solution.py:859
  476.2 28.9 %collective-permute-start.57 = (bf16[2,48,2688]{2,1,0:T(8,128)(2,1)S(1)}, bf16[2,48,2688]{2,1,0:T(8,128)(2,1)S(1)}, u32[]{:S(2)}, u32[]{:S(2)}) collective-permute-start(bf16[2,48,2688]{2,1,0:T(8,128)(2,1)S(1)} %slice.391), channel_id=1, source_target_pairs={{0,1},{1,0},{2,3},{3,2},{4,5},{5,4},{6,7},{7,6},{8,9},{9,8},{10,11... | collective-permute-start | bytes 1548296 | tf_op jit(solution)/shard_map/ppermute | solution.py:846
  477.0 31.3 %collective-permute-start.62 = (bf16[2,48,2688]{2,1,0:T(8,128)(2,1)S(1)}, bf16[2,48,2688]{2,1,0:T(8,128)(2,1)S(1)}, u32[]{:S(2)}, u32[]{:S(2)}) collective-permute-start(bf16[2,48,2688]{2,1,0:T(8,128)(2,1)S(1)} %slice.401), channel_id=1, source_target_pairs={{0,2},{1,3},{2,0},{3,1},{4,6},{5,7},{6,4},{7,5},{8,10},{9,11},{10,... | collective-permute-start | bytes 1548296 | tf_op jit(solution)/shard_map/ppermute | solution.py:847
  478.7 22.0 %collective-permute-start.60 = (bf16[2,48,2688]{2,1,0:T(8,128)(2,1)S(1)}, bf16[2,48,2688]{2,1,0:T(8,128)(2,1)S(1)}, u32[]{:S(2)}, u32[]{:S(2)}) collective-permute-start(bf16[2,48,2688]{2,1,0:T(8,128)(2,1)S(1)} %get-tuple-element.235), channel_id=1, source_target_pairs={{0,2},{1,3},{2,0},{3,1},{4,6},{5,7},{6,4},{7,5},{8,10},{9,11},{10,... | collective-permute-start | bytes 1548296 | tf_op jit(solution)/shard_map/ppermute | solution.py:845
  505.1 43.3 %collective-permute-start.68 = (bf16[48,1664]{1,0:T(8,128)(2,1)S(1)}, bf16[48,1664]{1,0:T(8,128)(2,1)S(1)}, u32[]{:S(2)}, u32[]{:S(2)}) collective-permute-start(bf16[48,1664]{1,0:T(8,128)(2,1)S(1)} %get-tuple-element.231), channel_id=1, source_target_pairs={{0,24},{4,28},{8,0},{12,4},{16,8},{20,12},{24,16},{28,20},{1,25},{... | collective-permute-start | bytes 479240 | tf_op jit(solution)/shard_map/ppermute | solution.py:940
  508.3 40.1 %collective-permute-start.66 = (bf16[3,2,64,1536]{3,2,1,0:T(8,128)(2,1)S(1)}, bf16[3,2,64,1536]{3,2,1,0:T(8,128)(2,1)S(1)}, u32[]{:S(2)}, u32[]{:S(2)}) collective-permute-start(bf16[3,2,64,1536]{3,2,1,0:T(8,128)(2,1)S(1)} %fusion), channel_id=1, source_target_pairs={{0,8},{4,12},{8,16},{12,20},{16,24},{20,28},{24,0},{28,4},{1,9},{5... | collective-permute-start | bytes 3538952 | tf_op jit(solution)/shard_map/ppermute | solution.py:936
  514.2 33.3 %collective-permute-start.64 = (bf16[48,2688]{1,0:T(8,128)(2,1)S(1)}, bf16[48,2688]{1,0:T(8,128)(2,1)S(1)}, u32[]{:S(2)}, u32[]{:S(2)}) collective-permute-start(bf16[48,2688]{1,0:T(8,128)(2,1)S(1)} %get-tuple-element.226), channel_id=1, source_target_pairs={{0,8},{4,12},{8,16},{12,20},{16,24},{20,28},{24,0},{28,4},{1,9},{5... | collective-permute-start | bytes 774152 | tf_op jit(solution)/shard_map/ppermute | solution.py:936
  515.2 35.9 %collective-permute-start.70 = (bf16[48,1664]{1,0:T(8,128)(2,1)S(1)}, bf16[48,1664]{1,0:T(8,128)(2,1)S(1)}, u32[]{:S(2)}, u32[]{:S(2)}) collective-permute-start(bf16[48,1664]{1,0:T(8,128)(2,1)S(1)} %fusion.38), channel_id=1, source_target_pairs={{0,8},{4,12},{8,16},{12,20},{16,24},{20,28},{24,0},{28,4},{1,9},{5... | collective-permute-start | bytes 479240 | tf_op jit(solution)/shard_map/ppermute | solution.py:936
  516.4 42.9 %collective-permute-start.63 = (bf16[48,2688]{1,0:T(8,128)(2,1)S(1)}, bf16[48,2688]{1,0:T(8,128)(2,1)S(1)}, u32[]{:S(2)}, u32[]{:S(2)}) collective-permute-start(bf16[48,2688]{1,0:T(8,128)(2,1)S(1)} %get-tuple-element.225), channel_id=1, source_target_pairs={{0,24},{4,28},{8,0},{12,4},{16,8},{20,12},{24,16},{28,20},{1,25},{... | collective-permute-start | bytes 774152 | tf_op jit(solution)/shard_map/ppermute | solution.py:940
  (90 other events, 1225.0 us)
Sparse Core Ops, SparseCore 0:
  55.6 126.8 all-gather.6
  184.7 88.9 all-gather.4
  276.0 143.9 reduce-scatter.1

commit v6 on v3

--- a/solution.py
+++ b/solution.py
@@ -874,15 +874,9 @@
     return lax.optimization_barrier((values, events))[0]
 
 
-def send_parts(parts, events):
-    if lax.axis_size("expert") != 4:
-        return [scatter_blocks(parts)]
-    low = jnp.bfloat16
-    first, second = (
-        lax.ppermute(parts[r].astype(low), "expert", pair_moves(4, r)) for r in (1, 2)
-    )
-    far = lax.ppermute(after(parts[3].astype(low), (first, second, events)), "expert", pair_moves(4, 3))
-    return [parts[0], first, second, far]
+def send_part(parts, r, events=()):
+    part = after(parts[r].astype(jnp.bfloat16), events)
+    return lax.ppermute(part, "expert", pair_moves(4, r))
 
 
 def total_of(parts):
@@ -1183,9 +1177,10 @@
     )
     out_found = turned[:-2]
     resid_grad, head_grad = turned[-2:]
-    mixture_parts = send_parts(blocks_of(after(mixture_all, normed_grad)), resid_grad)
+    mixture_blocks = blocks_of(after(mixture_all, normed_grad))
     if cut:
-        head_grad = after(head_grad, mixture_parts[1:3])
+        mixture_parts = [mixture_blocks[0]] + [send_part(mixture_blocks, r) for r in (1, 2)]
+        head_grad = after(head_grad, mixture_parts[1:])
         up_part = step_up(far_sum)
     query_grad, key_grads = attend_back(
         head_grad, query, keys, bias_turned, log_totals, cosine, sine_part
@@ -1202,7 +1197,7 @@
         key_parts = blocks_of(key_grads)
     if cut:
         out_found = out_found[1], exchange_cores(out_found[0])
-        key_parts = after(key_parts, (mixture_parts[3], up_part))
+        key_parts = after(key_parts, up_part)
     keyval_sum = scatter_blocks(key_parts)
     if cut:
         out_state = scatter_start(join_cores(*out_found))
@@ -1227,28 +1222,30 @@
         first_gain,
     )
     qkv_found, input_grad = left[:-1], left[-1]
-    result = (residual + total_of(mixture_parts)).astype(low)
     if cut:
         down_term = step_down(after(down_sum, key_parts))
         received = exchange_cores(after(qkv_found[0], (totals[0], out_state[1:], down_term)))
         out_plane = scatter_finish(out_state)
         up_term = step_up(up_sum)
         qkv_parts = join_cores(qkv_found[1], after(received, out_plane))
-        qkv_state = after(scatter_start(qkv_parts), up_term)
-        qkv_plane = scatter_finish(qkv_state)
+        qkv_plane = after(scatter_blocks(qkv_parts), up_term)
+        mixture_parts.append(send_part(mixture_blocks, 3, qkv_plane))
         out_sum = line_finish(line_start(out_plane))
         qkv_state = line_start(qkv_plane)
         near, down_term, up_term = after((near, down_term, up_term), qkv_plane)
         terms = [[(totals[0], 0)], [(own, None), (near, 1), (down_term, None), (up_term, None)]]
         expert_totals = unpack(terms, gate_weight.shape, down_weight.shape)
-        qkv_sum = line_finish(qkv_state, expert_totals)
+        qkv_sum = line_finish(qkv_state, (expert_totals, mixture_parts[3]))
+        mixture = total_of(mixture_parts)
     else:
+        mixture = scatter_blocks(mixture_blocks)
         out_sum = scatter_whole(out_found)
         qkv_sum = scatter_whole(qkv_found)
         totals += [sum_chunk(found[0]) for found in chunk_grads[1:]]
         terms = [[(total, 0)] for total in totals]
         expert_totals = unpack(terms, gate_weight.shape, down_weight.shape)
     gate_total, up_total, down_total = expert_totals
+    result = (residual + mixture).astype(low)
     return (
         result[None],
         input_grad[None],

time: 584 us -> 587 us (level)
    ppermute x8, waiting for transfers between devices: 59.4 us -> 33.1 us  [step_up(): return lax.ppermute(values, 'batch', shift_moves(1))]
    ppermute x4, waiting for transfers between devices: 10 us -> 25.7 us  [step_down(): return lax.ppermute(values, 'batch', shift_moves(3))]
    ppermute x4, waiting for transfers between devices: 16.9 us -> 2.74 us  [scatter_start(): top = lax.ppermute(parts[3][:half].astype(low), 'expert', across)]
    ppermute x4, waiting for transfers between devices: 13.8 us -> 21.9 us  [scatter_start(): bottom = lax.ppermute(parts[3][half:].astype(low), 'expert', along)]
    ppermute x3, waiting for transfers between devices: 4.73 us -> 12.6 us  [send_part(): return lax.ppermute(part, 'expert', pair_moves(4, r))]
    ppermute x4, waiting for transfers between devices: 3.78 us -> 10.7 us  [scatter_finish(): first_bottom = lax.ppermute(for_first, 'expert', pair_moves(4, 1))]
    convert_element_type x15 -> x14, other arithmetic: 19.6 us -> 17.9 us  [add_low(): return total.astype(jnp.bfloat16)]
  transfers between devices with their start and end apart: 74 -> 74, of which waited for: 42 -> 46; matrix products, arithmetic and copies ran while one was open for 12% -> 13% of each run, Pallas kernels for 33% -> 33%
where the time goes in v6:
time: 587 us; the launch traced here: 579 us
  waiting for transfers between devices  221 us (38%)
  Pallas kernels  196 us (33%)
  starting transfers between devices  65 us (11%)
  other arithmetic  41.9 us (7%)
  local copies, waits for them, and re-layouts  39.4 us (7%)
  between operations  14.9 us (3%)
    pallas_call x2, Pallas kernels, expert_pass(): pl.pallas_call(partial(expert_kernel, cut, carried, last, len(rows), len(...  108 us
    ppermute x10, waiting for transfers between devices, gather_start(): lax.ppermute(rows, 'expert', pair_moves(4, r))  58.4 us
    ppermute x8, waiting for transfers between devices, step_up(): return lax.ppermute(values, 'batch', shift_moves(1))  33.1 us
    ppermute x4, waiting for transfers between devices, step_down(): return lax.ppermute(values, 'batch', shift_moves(3))  25.7 us
    ppermute x4, waiting for transfers between devices, scatter_start(): bottom = lax.ppermute(parts[3][half:].astype(low), 'expert', along)  21.9 us
    pallas_call x1, Pallas kernels, attend_back(): pl.pallas_call(attend_back_kernel, in_specs=[INSIDE] * 7, out_specs=[INSI...  21.2 us
    convert_element_type x14, other arithmetic, add_low(): return total.astype(jnp.bfloat16)  17.9 us
    ppermute x4, waiting for transfers between devices, scatter_finish(): second_top = lax.ppermute(for_second, 'expert', pair_moves(4, 2))  16 us
  transfers between devices with their start and end apart: 74, of which 46 were waited for; matrix products, arithmetic and copies ran while one was open for 13% of the time, Pallas kernels for 33%

profile of v6, /device:TPU:0, one launch (start us, length us, event | category | flops | bytes accessed | tf_op | source)
XLA Modules:
  0.0 579.4 jit_solution(15024851306948317296)
XLA Ops:
  29.7 7.4 %collective-permute-done.1 = bf16[48,4224]{1,0:T(8,128)(2,1)} collective-permute-done((bf16[48,4224]{1,0:T(8,128)(2,1)}, bf16[48,4224]{1,0:T(8,128)(2,1)}, u32[]{:S(2)}, u32[]{:S(2)}) %collective-permute-start.1) | collective-permute-done | bytes 405536 | tf_op jit(solution)/shard_map/ppermute | solution.py:934
  45.4 10.9 %collective-permute-done.2 = bf16[48,4224]{1,0:T(8,128)(2,1)S(1)} collective-permute-done((bf16[48,4224]{1,0:T(8,128)(2,1)}, bf16[48,4224]{1,0:T(8,128)(2,1)S(1)}, u32[]{:S(2)}, u32[]{:S(2)}) %collective-permute-start.2) | collective-permute-done | bytes 405536 | tf_op jit(solution)/shard_map/ppermute | solution.py:930
  63.2 19.6 %collective-permute-done.3.refs_1_ = bf16[4,48,2688]{2,1,0:T(8,128)(2,1)} collective-permute-done((bf16[4,48,2688]{2,1,0:T(8,128)(2,1)S(1)}, bf16[4,48,2688]{2,1,0:T(8,128)(2,1)}, u32[]{:S(2)}, u32[]{:S(2)}) %collective-permute-start.3) | collective-permute-done | bytes 1032224 | tf_op jit(solution)/shard_map/ppermute | solution.py:818
  106.3 8.2 %enter.1 = (bf16[256,1536]{1,0:T(8,128)(2,1)}, bf16[256,1536]{1,0:T(8,128)(2,1)}, bf16[256,1024]{1,0:T(8,128)(2,1)}, f32[128,1536]{1,0:T(8,128)}) custom-call(s32[8,4]{1,0:T(8,128)} %concatenate.91.spots, bf16[256,1536]{1,0:T(8,128)(2,1)} %bitcast.177, f32[256,128]{1,0:T(8,128)} %copy.56.cosine, f32[256,128]{1,0:T(8,128)} %copy.57.sine, ...), custom_call_target="tpu_custom_call" | custom-call | flops 1 | bytes 1 | tf_op jit(solution)/shard_map/enter/pallas_call | solution.py:137
  119.9 10.5 %collective-permute-done.13 = bf16[256,1024]{1,0:T(8,128)(2,1)S(1)} collective-permute-done((bf16[256,1024]{1,0:T(8,128)(2,1)}, bf16[256,1024]{1,0:T(8,128)(2,1)S(1)}, u32[]{:S(2)}, u32[]{:S(2)}) %collective-permute-start.13) | collective-permute-done | bytes 524320 | tf_op jit(solution)/shard_map/ppermute | solution.py:818
  145.0 13.8 %attend.1 = (bf16[256,1536]{1,0:T(8,128)(2,1)}, f32[256,128]{1,0:T(8,128)}) custom-call(bf16[256,1536]{1,0:T(8,128)(2,1)} %get-tuple-element.86.query, bf16[768,1024]{1,0:T(8,128)(2,1)} %pad_maximum_fusion.3.keyval, f32[256,768]{1,0:T(8,128)} %and_select_fusion.1.bias), custom_call_target="tpu_custom_call" | custom-call | flops 1 | bytes 1 | tf_op jit(solution)/shard_map/attend/pallas_call | solution.py:203
  164.1 7.7 %project.1 = (f32[256,1536]{1,0:T(8,128)}, bf16[256,1664]{1,0:T(8,128)(2,1)}, f32[256,128]{1,0:T(8,128)}) custom-call(s32[8,4]{1,0:T(8,128)} %concatenate.91.spots, bf16[256,1536]{1,0:T(8,128)(2,1)} %get-tuple-element.92.attended, bf16[256,1536]{1,0:T(8,128)(2,1)} %bitcast.178, f32[128,1536]{1,0:T(8,128)} %get-tuple-element.93.small, ...), custom_call_target="tpu_custom_call" | custom-call | flops 1 | bytes 1 | tf_op jit(solution)/shard_map/project/pallas_call | solution.py:245
  174.6 18.7 %collective-permute-done.27.refs_1_ = bf16[256,1664]{1,0:T(8,128)(2,1)S(1)} collective-permute-done((bf16[256,1664]{1,0:T(8,128)(2,1)}, bf16[256,1664]{1,0:T(8,128)(2,1)S(1)}, u32[]{:S(2)}, u32[]{:S(2)}) %collective-permute-start.27) | collective-permute-done | bytes 852000 | tf_op jit(solution)/shard_map/ppermute | solution.py:818
  197.1 8.3 %collective-permute-done.29.refs_3_ = bf16[128,1664]{1,0:T(8,128)(2,1)} collective-permute-done((bf16[128,1664]{1,0:T(8,128)(2,1)S(1)}, bf16[128,1664]{1,0:T(8,128)(2,1)}, u32[]{:S(2)}, u32[]{:S(2)}) %collective-permute-start.29) | collective-permute-done | bytes 426016 | tf_op jit(solution)/shard_map/ppermute | solution.py:826
  206.0 62.5 %experts.2 = (bf16[8,3,3,64,1536]{4,3,2,1,0:T(8,128)(2,1)}, f32[1024,1536]{1,0:T(8,128)}, f32[1024,1664]{1,0:T(8,128)}) custom-call(s32[3]{0:T(128)} %pad_add_fusion.1.place, s32[1]{0:T(128)} %bitcast.61.first, bf16[8,3,3,64,1536]{4,3,2,1,0:T(8,128)(2,1)} %bitcast.175, bf16[256,1664]{1,0:T(8,128)(2,1)} %get-tuple-element.102.refs_0_.normed, ...), custom_call_target="tpu_custom_call" | custom-call | flops 1 | bytes 1 | tf_op jit(solution)/shard_map/experts/pallas_call | solution.py:727
  268.6 6.6 %all-gather.5.cloned.1.call-done = bf16[24,2,64,1536]{3,2,1,0:T(8,128)(2,1)} async-done(((bf16[3,2,64,1536]{3,2,1,0:T(8,128)(2,1)}), bf16[24,2,64,1536]{3,2,1,0:T(8,128)(2,1)}) %all-gather.5.cloned.1.call-update) | async-done | bytes 9437200 | tf_op jit(solution)/shard_map/all_gather | solution.py:1095
  275.2 45.6 %experts.3 = (bf16[3,2,64,1536]{3,2,1,0:T(8,128)(2,1)}, bf16[3,3,2,64,1536]{4,3,2,1,0:T(8,128)(2,1)}, bf16[2,3,2,64,1536]{4,3,2,1,0:T(8,128)(2,1)}, bf16[2,3,2,6...) custom-call(s32[3]{0:T(128)} %pad_add_fusion.1.place, s32[1]{0:T(128)} %bitcast.59.first, ...), custom_call_target="tpu_custom_call" | custom-call | flops 1 | bytes 1 | tf_op jit(solution)/shard_map/experts/pallas_call | solution.py:727
  327.1 8.5 %collective-permute-done.33 = bf16[128,1664]{1,0:T(8,128)(2,1)S(1)} collective-permute-done((bf16[128,1664]{1,0:T(8,128)(2,1)S(1)}, bf16[128,1664]{1,0:T(8,128)(2,1)S(1)}, u32[]{:S(2)}, u32[]{:S(2)}) %collective-permute-start.33) | collective-permute-done | bytes 426016 | tf_op jit(solution)/shard_map/ppermute | solution.py:845
  339.2 6.1 %collective-permute-done.31 = bf16[128,1664]{1,0:T(8,128)(2,1)S(1)} collective-permute-done((bf16[128,1664]{1,0:T(8,128)(2,1)S(1)}, bf16[128,1664]{1,0:T(8,128)(2,1)S(1)}, u32[]{:S(2)}, u32[]{:S(2)}) %collective-permute-start.31) | collective-permute-done | bytes 426016 | tf_op jit(solution)/shard_map/ppermute | solution.py:846
  347.3 8.9 %collective-permute-done.36 = bf16[128,1664]{1,0:T(8,128)(2,1)S(1)} collective-permute-done((bf16[128,1664]{1,0:T(8,128)(2,1)S(1)}, bf16[128,1664]{1,0:T(8,128)(2,1)S(1)}, u32[]{:S(2)}, u32[]{:S(2)}) %collective-permute-start.36) | collective-permute-done | bytes 426016 | tf_op jit(solution)/shard_map/ppermute | solution.py:858
  363.5 11.4 %turn.1 = (bf16[4,4,48,1664]{3,2,1,0:T(8,128)(2,1)}, bf16[4,4,48,1664]{3,2,1,0:T(8,128)(2,1)}, f32[256,1536]{1,0:T(8,128)}, bf16[256,1536]{1,0:T(8,128)(2,1)}) custom-call(s32[3]{0:T(128)} %pad_add_fusion.1.place, s32[8,4]{1,0:T(8,128)} %concatenate.91.spots, f32[256,1664]{1,0:T(8,128)} %pad_maximum_fusion.2.normed_grad, ...), custom_call_target="tpu_custom_call" | custom-call | flops 1 | bytes 1 | tf_op jit(solution)/shard_map/turn/pallas_call | solution.py:370
  379.4 21.2 %attend_back.1 = (bf16[256,1536]{1,0:T(8,128)(2,1)}, bf16[768,1024]{1,0:T(8,128)(2,1)}) custom-call(bf16[256,1536]{1,0:T(8,128)(2,1)} %get-tuple-element.121.head_grad, bf16[256,1536]{1,0:T(8,128)(2,1)} %get-tuple-element.86.query, bf16[768,1024]{1,0:T(8,128)(2,1)} %pad_maximum_fusion.3.keyval, f32[768,256]{1,0:T(8,128)} %and_select_fusion.bias, ...), custom_call_target="tpu_custom_call" | custom-call | flops 1 | bytes 1 | tf_op jit(solution)/shard_map/attend_back/pallas_call | solution.py:445
  434.3 15.3 %leave.1 = (bf16[4,4,48,2688]{3,2,1,0:T(8,128)(2,1)}, bf16[4,4,48,2688]{3,2,1,0:T(8,128)(2,1)}, f32[256,1536]{1,0:T(8,128)}) custom-call(s32[3]{0:T(128)} %pad_add_fusion.1.place, s32[8,4]{1,0:T(8,128)} %concatenate.91.spots, f32[256,1024]{1,0:T(8,128)} %pad_maximum_fusion.4.keyval_sum, bf16[256,1536]{1,0:T(8,128)(2,1)} %get-tuple-element.132.query_grad, ...), custom_call_target="tpu_custom_call" | custom-call | flops 1 | bytes 1 | tf_op jit(solution)/shard_map/leave/pallas_call | solution.py:530
  451.7 16.1 %collective-permute-done.53.refs_3_ = bf16[3,2,64,1536]{3,2,1,0:T(8,128)(2,1)} collective-permute-done((bf16[3,2,64,1536]{3,2,1,0:T(8,128)(2,1)}, bf16[3,2,64,1536]{3,2,1,0:T(8,128)(2,1)}, u32[]{:S(2)}, u32[]{:S(2)}) %collective-permute-start.53) | collective-permute-done | bytes 1179680 | tf_op jit(solution)/shard_map/ppermute | solution.py:934
  472.5 6.7 %collective-permute-done.55 = bf16[2,48,1664]{2,1,0:T(8,128)(2,1)S(1)} collective-permute-done((bf16[2,48,1664]{2,1,0:T(8,128)(2,1)S(1)}, bf16[2,48,1664]{2,1,0:T(8,128)(2,1)S(1)}, u32[]{:S(2)}, u32[]{:S(2)}) %collective-permute-start.55) | collective-permute-done | bytes 319520 | tf_op jit(solution)/shard_map/ppermute | solution.py:858
  492.1 9.0 %collective-permute-done.60 = bf16[2,48,2688]{2,1,0:T(8,128)(2,1)S(1)} collective-permute-done((bf16[2,48,2688]{2,1,0:T(8,128)(2,1)S(1)}, bf16[2,48,2688]{2,1,0:T(8,128)(2,1)S(1)}, u32[]{:S(2)}, u32[]{:S(2)}) %collective-permute-start.60) | collective-permute-done | bytes 516128 | tf_op jit(solution)/shard_map/ppermute | solution.py:845
  524.0 11.8 %collective-permute-done.63.refs_4_ = bf16[3,2,64,1536]{3,2,1,0:T(8,128)(2,1)S(1)} collective-permute-done((bf16[3,2,64,1536]{3,2,1,0:T(8,128)(2,1)S(1)}, bf16[3,2,64,1536]{3,2,1,0:T(8,128)(2,1)S(1)}, u32[]{:S(2)}, u32[]{:S(2)}) %collective-permute-start.63) | collective-permute-done | bytes 1179680 | tf_op jit(solution)/shard_map/ppermute | solution.py:930
  545.6 6.1 %unpack.1 = (f32[5,192,512]{2,1,0:T(8,128)}, f32[5,192,512]{2,1,0:T(8,128)}, f32[5,64,1536]{2,1,0:T(8,128)}) custom-call(bf16[1,3,3,64,1536]{4,3,2,1,0:T(8,128)(2,1)} %reduce-scatter.2.cloned.1.call-done.refs_0_, bf16[3,2,64,1536]{3,2,1,0:T(8,128)(2,1)} %get-tuple-element.144.refs_1_, bf16[2,3,2,64,1536]{4,3,2,1,0:T(8,128)(2,1)} %collective-permute-done.48.refs_2_, ...), custom_call_target="tpu_custom_call" | custom-call | flops 1 | bytes 1 | tf_op jit(solution)/shard_map/unpack/pallas_call | solution.py:783
  552.8 8.2 %collective-permute-done.64 = bf16[256,1536]{1,0:T(8,128)(2,1)} collective-permute-done((bf16[256,1536]{1,0:T(8,128)(2,1)}, bf16[256,1536]{1,0:T(8,128)(2,1)}, u32[]{:S(2)}, u32[]{:S(2)}) %collective-permute-start.64) | collective-permute-done | bytes 786464 | tf_op jit(solution)/shard_map/ppermute | solution.py:879
  (316 shorter events, 215.4 us)
Async XLA Ops:
  7.2 198.8 %all-gather.7.cloned.1.call-start = ((), (), s32[]{:S(2)}) async-start(), calls=%async_computation.3 | async-start | bytes 15925248 | tf_op jit(solution)/shard_map/all_gather | solution.py:1095
  57.1 218.2 %all-gather.5.cloned.1.call-start = ((), (), s32[]{:S(2)}) async-start(), calls=%async_computation.2 | async-start | bytes 10616832 | tf_op jit(solution)/shard_map/all_gather | solution.py:1095
  61.2 21.5 %collective-permute-start.3 = (bf16[4,48,2688]{2,1,0:T(8,128)(2,1)S(1)}, bf16[4,48,2688]{2,1,0:T(8,128)(2,1)}, u32[]{:S(2)}, u32[]{:S(2)}) collective-permute-start(bf16[4,48,2688]{2,1,0:T(8,128)(2,1)S(1)} %pad_maximum_fusion.5.refs_0_), channel_id=1, source_target_pairs={{0,1},{1,0},{2,3},{3,2},{4,5},{5,4},{6,7},{7,6},{8,9},{9,8},{10,11... | collective-permute-start | bytes 3096584 | tf_op jit(solution)/shard_map/ppermute | solution.py:818
  62.7 21.2 %collective-permute-start.4 = (bf16[4,48,2688]{2,1,0:T(8,128)(2,1)S(1)}, bf16[4,48,2688]{2,1,0:T(8,128)(2,1)}, u32[]{:S(2)}, u32[]{:S(2)}) collective-permute-start(bf16[4,48,2688]{2,1,0:T(8,128)(2,1)S(1)} %pad_maximum_fusion.5.refs_0_), channel_id=1, source_target_pairs={{0,2},{1,3},{2,0},{3,1},{4,6},{5,7},{6,4},{7,5},{8,10},{9,11},{10,... | collective-permute-start | bytes 3096584 | tf_op jit(solution)/shard_map/ppermute | solution.py:818
  83.9 385.2 %reduce-scatter.2.cloned.1.call-start = ((), (), s32[]{:S(2)}) async-start(), calls=%async_computation.1 | async-start | bytes 15925248 | tf_op jit(solution)/shard_map/reduce_scatter | solution.py:922
  134.4 28.7 %collective-permute-start.23 = (bf16[4,48,1536]{2,1,0:T(8,128)(2,1)}, bf16[4,48,1536]{2,1,0:T(8,128)(2,1)S(1)}, u32[]{:S(2)}, u32[]{:S(2)}) collective-permute-start(bf16[4,48,1536]{2,1,0:T(8,128)(2,1)} %pad_maximum_fusion.8.refs_0_), channel_id=1, source_target_pairs={{0,4},{4,0},{8,12},{12,8},{16,20},{20,16},{24,28},{28,24},{1,5},{5... | collective-permute-start | bytes 1769480 | tf_op jit(solution)/shard_map/ppermute | solution.py:926
  134.5 28.6 %collective-permute-start.24 = (bf16[4,48,1536]{2,1,0:T(8,128)(2,1)}, bf16[4,48,1536]{2,1,0:T(8,128)(2,1)}, u32[]{:S(2)}, u32[]{:S(2)}) collective-permute-start(bf16[4,48,1536]{2,1,0:T(8,128)(2,1)} %collective-permute-done.11.refs_1_), channel_id=1, source_target_pairs={{0,4},{4,0},{8,12},{12,8},{16,20},{20,16},{24,28},{28,24},{1,5},{5... | collective-permute-start | bytes 1769480 | tf_op jit(solution)/shard_map/ppermute | solution.py:926
  135.0 28.1 %collective-permute-start.25 = (bf16[4,48,1536]{2,1,0:T(8,128)(2,1)S(1)}, bf16[4,48,1536]{2,1,0:T(8,128)(2,1)}, u32[]{:S(2)}, u32[]{:S(2)}) collective-permute-start(bf16[4,48,1536]{2,1,0:T(8,128)(2,1)S(1)} %collective-permute-done.12.refs_2_), channel_id=1, source_target_pairs={{0,4},{4,0},{8,12},{12,8},{16,20},{20,16},{24,28},{28,24},{1,5},{5... | collective-permute-start | bytes 1769480 | tf_op jit(solution)/shard_map/ppermute | solution.py:926
  171.8 21.5 %collective-permute-start.27 = (bf16[256,1664]{1,0:T(8,128)(2,1)}, bf16[256,1664]{1,0:T(8,128)(2,1)S(1)}, u32[]{:S(2)}, u32[]{:S(2)}) collective-permute-start(bf16[256,1664]{1,0:T(8,128)(2,1)} %get-tuple-element.102.refs_0_.normed), channel_id=1, source_target_pairs={{0,1},{1,0},{2,3},{3,2},{4,5},{5,4},{6,7},{7,6},{8,9},{9,8},{10,11... | collective-permute-start | bytes 2555912 | tf_op jit(solution)/shard_map/ppermute | solution.py:818
  173.0 21.2 %collective-permute-start.28 = (bf16[256,1664]{1,0:T(8,128)(2,1)}, bf16[256,1664]{1,0:T(8,128)(2,1)S(1)}, u32[]{:S(2)}, u32[]{:S(2)}) collective-permute-start(bf16[256,1664]{1,0:T(8,128)(2,1)} %get-tuple-element.102.refs_0_.normed), channel_id=1, source_target_pairs={{0,2},{1,3},{2,0},{3,1},{4,6},{5,7},{6,4},{7,5},{8,10},{9,11},{10,... | collective-permute-start | bytes 2555912 | tf_op jit(solution)/shard_map/ppermute | solution.py:818
  347.3 67.4 %collective-permute-start.48 = (bf16[2,3,2,64,1536]{4,3,2,1,0:T(8,128)(2,1)}, bf16[2,3,2,64,1536]{4,3,2,1,0:T(8,128)(2,1)}, u32[]{:S(2)}, u32[]{:S(2)}) collective-permute-start(bf16[2,3,2,64,1536]{4,3,2,1,0:T(8,128)(2,1)} %get-tuple-element.130), channel_id=1, source_target_pairs={{0,4},{4,0},{8,12},{12,8},{16,20},{20,16},{24,28},{28,24},{1,5},{5... | collective-permute-start | bytes 7077896 | tf_op jit(solution)/shard_map/ppermute | solution.py:926
  347.3 55.9 %collective-permute-start.40 = (bf16[3,2,64,1536]{3,2,1,0:T(8,128)(2,1)S(1)}, bf16[3,2,64,1536]{3,2,1,0:T(8,128)(2,1)}, u32[]{:S(2)}, u32[]{:S(2)}) collective-permute-start(bf16[3,2,64,1536]{3,2,1,0:T(8,128)(2,1)S(1)} %get-tuple-element.205), channel_id=1, source_target_pairs={{0,8},{4,12},{8,16},{12,20},{16,24},{20,28},{24,0},{28,4},{1,9},{5... | collective-permute-start | bytes 3538952 | tf_op jit(solution)/shard_map/ppermute | solution.py:930
  374.9 50.7 %collective-permute-start.47 = (bf16[4,4,48,1664]{3,2,1,0:T(8,128)(2,1)}, bf16[4,4,48,1664]{3,2,1,0:T(8,128)(2,1)}, u32[]{:S(2)}, u32[]{:S(2)}) collective-permute-start(bf16[4,4,48,1664]{3,2,1,0:T(8,128)(2,1)} %get-tuple-element.129), channel_id=1, source_target_pairs={{0,4},{4,0},{8,12},{12,8},{16,20},{20,16},{24,28},{28,24},{1,5},{5... | collective-permute-start | bytes 7667720 | tf_op jit(solution)/shard_map/ppermute | solution.py:926
  419.7 48.1 %collective-permute-start.53 = (bf16[3,2,64,1536]{3,2,1,0:T(8,128)(2,1)}, bf16[3,2,64,1536]{3,2,1,0:T(8,128)(2,1)}, u32[]{:S(2)}, u32[]{:S(2)}) collective-permute-start(bf16[3,2,64,1536]{3,2,1,0:T(8,128)(2,1)} %get-tuple-element.138), channel_id=1, source_target_pairs={{0,24},{4,28},{8,0},{12,4},{16,8},{20,12},{24,16},{28,20},{1,25},{... | collective-permute-start | bytes 3538952 | tf_op jit(solution)/shard_map/ppermute | solution.py:934
  428.7 20.8 %collective-permute-start.52 = (bf16[2,48,1664]{2,1,0:T(8,128)(2,1)}, bf16[2,48,1664]{2,1,0:T(8,128)(2,1)}, u32[]{:S(2)}, u32[]{:S(2)}) collective-permute-start(bf16[2,48,1664]{2,1,0:T(8,128)(2,1)} %get-tuple-element.237), channel_id=1, source_target_pairs={{0,1},{1,0},{2,3},{3,2},{4,5},{5,4},{6,7},{7,6},{8,9},{9,8},{10,11... | collective-permute-start | bytes 958472 | tf_op jit(solution)/shard_map/ppermute | solution.py:844
  429.4 21.3 %collective-permute-start.51 = (bf16[2,48,1664]{2,1,0:T(8,128)(2,1)}, bf16[2,48,1664]{2,1,0:T(8,128)(2,1)}, u32[]{:S(2)}, u32[]{:S(2)}) collective-permute-start(bf16[2,48,1664]{2,1,0:T(8,128)(2,1)} %get-tuple-element.238), channel_id=1, source_target_pairs={{0,2},{1,3},{2,0},{3,1},{4,6},{5,7},{6,4},{7,5},{8,10},{9,11},{10,... | collective-permute-start | bytes 958472 | tf_op jit(solution)/shard_map/ppermute | solution.py:845
  431.6 36.2 %collective-permute-start.49 = (bf16[2,48,1664]{2,1,0:T(8,128)(2,1)}, bf16[2,48,1664]{2,1,0:T(8,128)(2,1)}, u32[]{:S(2)}, u32[]{:S(2)}) collective-permute-start(bf16[2,48,1664]{2,1,0:T(8,128)(2,1)} %slice_bitcast_fusion.15), channel_id=1, source_target_pairs={{0,1},{1,0},{2,3},{3,2},{4,5},{5,4},{6,7},{7,6},{8,9},{9,8},{10,11... | collective-permute-start | bytes 958472 | tf_op jit(solution)/shard_map/ppermute | solution.py:846
  433.7 34.1 %collective-permute-start.50 = (bf16[2,48,1664]{2,1,0:T(8,128)(2,1)}, bf16[2,48,1664]{2,1,0:T(8,128)(2,1)}, u32[]{:S(2)}, u32[]{:S(2)}) collective-permute-start(bf16[2,48,1664]{2,1,0:T(8,128)(2,1)} %slice_bitcast_fusion.14), channel_id=1, source_target_pairs={{0,2},{1,3},{2,0},{3,1},{4,6},{5,7},{6,4},{7,5},{8,10},{9,11},{10,... | collective-permute-start | bytes 958472 | tf_op jit(solution)/shard_map/ppermute | solution.py:847
  482.9 22.0 %collective-permute-start.69 = (bf16[48,1664]{1,0:T(8,128)(2,1)}, bf16[48,1664]{1,0:T(8,128)(2,1)}, u32[]{:S(2)}, u32[]{:S(2)}) collective-permute-start(bf16[48,1664]{1,0:T(8,128)(2,1)} %get-tuple-element.228), channel_id=1, source_target_pairs={{0,8},{4,12},{8,16},{12,20},{16,24},{20,28},{24,0},{28,4},{1,9},{5... | collective-permute-start | bytes 479240 | tf_op jit(solution)/shard_map/ppermute | solution.py:930
  489.2 23.4 %collective-permute-start.57 = (bf16[2,48,2688]{2,1,0:T(8,128)(2,1)}, bf16[2,48,2688]{2,1,0:T(8,128)(2,1)}, u32[]{:S(2)}, u32[]{:S(2)}) collective-permute-start(bf16[2,48,2688]{2,1,0:T(8,128)(2,1)} %slice_bitcast_fusion.6), channel_id=1, source_target_pairs={{0,1},{1,0},{2,3},{3,2},{4,5},{5,4},{6,7},{7,6},{8,9},{9,8},{10,11... | collective-permute-start | bytes 1548296 | tf_op jit(solution)/shard_map/ppermute | solution.py:846
  490.4 25.9 %collective-permute-start.62 = (bf16[2,48,2688]{2,1,0:T(8,128)(2,1)}, bf16[2,48,2688]{2,1,0:T(8,128)(2,1)}, u32[]{:S(2)}, u32[]{:S(2)}) collective-permute-start(bf16[2,48,2688]{2,1,0:T(8,128)(2,1)} %slice_bitcast_fusion), channel_id=1, source_target_pairs={{0,2},{1,3},{2,0},{3,1},{4,6},{5,7},{6,4},{7,5},{8,10},{9,11},{10,... | collective-permute-start | bytes 1548296 | tf_op jit(solution)/shard_map/ppermute | solution.py:847
  504.9 30.9 %collective-permute-start.63 = (bf16[3,2,64,1536]{3,2,1,0:T(8,128)(2,1)S(1)}, bf16[3,2,64,1536]{3,2,1,0:T(8,128)(2,1)S(1)}, u32[]{:S(2)}, u32[]{:S(2)}) collective-permute-start(bf16[3,2,64,1536]{3,2,1,0:T(8,128)(2,1)S(1)} %copy-done.27), channel_id=1, source_target_pairs={{0,8},{4,12},{8,16},{12,20},{16,24},{20,28},{24,0},{28,4},{1,9},{5... | collective-permute-start | bytes 3538952 | tf_op jit(solution)/shard_map/ppermute | solution.py:930
  512.6 26.4 %collective-permute-start.68 = (bf16[48,1664]{1,0:T(8,128)(2,1)}, bf16[48,1664]{1,0:T(8,128)(2,1)S(1)}, u32[]{:S(2)}, u32[]{:S(2)}) collective-permute-start(bf16[48,1664]{1,0:T(8,128)(2,1)} %get-tuple-element.227), channel_id=1, source_target_pairs={{0,24},{4,28},{8,0},{12,4},{16,8},{20,12},{24,16},{28,20},{1,25},{... | collective-permute-start | bytes 479240 | tf_op jit(solution)/shard_map/ppermute | solution.py:934
  516.2 24.5 %collective-permute-start.70 = (bf16[48,1664]{1,0:T(8,128)(2,1)S(1)}, bf16[48,1664]{1,0:T(8,128)(2,1)S(1)}, u32[]{:S(2)}, u32[]{:S(2)}) collective-permute-start(bf16[48,1664]{1,0:T(8,128)(2,1)S(1)} %fusion.28), channel_id=1, source_target_pairs={{0,8},{4,12},{8,16},{12,20},{16,24},{20,28},{24,0},{28,4},{1,9},{5... | collective-permute-start | bytes 479240 | tf_op jit(solution)/shard_map/ppermute | solution.py:930
  (84 other events, 1215.1 us)
Sparse Core Ops, SparseCore 0:
  57.2 126.8 all-gather.6
  186.3 88.9 all-gather.4
  277.6 191.4 reduce-scatter.1

commit v7 on v2

--- a/solution.py
+++ b/solution.py
@@ -1159,7 +1159,7 @@
         far_sum, down_sum = add_low(rest[1], far[0]), add_low(rest[2], far[1])
     turn_state = scatter_start(blocks_of(row_grad))
     if cut:
-        turn_state = after(turn_state, (far_sum, down_sum))
+        turn_state = after(turn_state, (far_sum, down_sum, near))
     normed_grad = scatter_finish(turn_state)
     turned = turn(
         place,
@@ -1183,8 +1183,7 @@
     resid_grad, head_grad = turned[-2:]
     mixture_parts = send_parts(blocks_of(after(mixture_all, normed_grad)))
     if cut:
-        head_grad = after(head_grad, mixture_parts[1:3])
-        up_part = step_up(far_sum)
+        up_sum = add_low(rest[0], near[0], step_up(far_sum))
     query_grad, key_grads = attend_back(
         head_grad, query, keys, bias_turned, log_totals, cosine, sine_part
     )
@@ -1200,14 +1199,12 @@
         key_parts = blocks_of(key_grads)
     if cut:
         out_found = out_found[1], exchange_cores(out_found[0])
-        key_parts = after(key_parts, (mixture_parts[3], up_part))
+        key_parts = after(key_parts, (mixture_parts[1:], up_sum))
     keyval_sum = scatter_blocks(key_parts)
     if cut:
         out_state = scatter_start(join_cores(*out_found))
     if cut:
-        up_sum = add_low(rest[0], near[0], up_part)
-        down_term = step_down(after(down_sum, key_parts))
-        keyval_sum = after(keyval_sum, (out_found, up_sum, down_term))
+        keyval_sum = after(keyval_sum, out_found)
     left = leave(
         place,
         qkv_spots,
@@ -1228,7 +1225,8 @@
     qkv_found, input_grad = left[:-1], left[-1]
     result = (residual + total_of(mixture_parts)).astype(low)
     if cut:
-        received = exchange_cores(after(qkv_found[0], (totals[0], out_state[1:])))
+        down_term = step_down(after(down_sum, key_parts))
+        received = exchange_cores(after(qkv_found[0], (totals[0], out_state[1:], down_term)))
         out_plane = scatter_finish(out_state)
         up_term = step_up(up_sum)
         qkv_parts = join_cores(qkv_found[1], after(received, out_plane))

time: 581 us -> 563 us (0.969)
  waiting for transfers between devices: 211 us -> 189 us
    ppermute x3, waiting for transfers between devices: 20.9 us -> 5.4 us  [send_parts(): lax.ppermute(parts[r].astype(low), 'expert', pair_moves(4, r))]
    ppermute x4, waiting for transfers between devices: 29.1 us -> 15.6 us  [step_down(): return lax.ppermute(values, 'batch', shift_moves(3))]
  transfers between devices with their start and end apart: 74 -> 74, of which waited for: 38 -> 40; matrix products, arithmetic and copies ran while one was open for 12% -> 13% of each run, Pallas kernels for 33% -> 35%
where the time goes in v7:
time: 563 us; the launch traced here: 555 us
  Pallas kernels  196 us (35%)
  waiting for transfers between devices  189 us (34%)
  starting transfers between devices  72 us (13%)
  other arithmetic  42 us (7%)
  local copies, waits for them, and re-layouts  39.6 us (7%)
  between operations  15 us (3%)
    pallas_call x2, Pallas kernels, expert_pass(): pl.pallas_call(partial(expert_kernel, cut, carried, last, len(rows), len(...  108 us
    ppermute x10, waiting for transfers between devices, gather_start(): lax.ppermute(rows, 'expert', pair_moves(4, r))  58.4 us
    ppermute x4, waiting for transfers between devices, scatter_start(): bottom = lax.ppermute(parts[3][half:].astype(low), 'expert', along)  25 us
    ppermute x8, waiting for transfers between devices, step_up(): return lax.ppermute(values, 'batch', shift_moves(1))  22.1 us
    pallas_call x1, Pallas kernels, attend_back(): pl.pallas_call(attend_back_kernel, in_specs=[INSIDE] * 7, out_specs=[INSI...  21.3 us
    convert_element_type x14, other arithmetic, add_low(): return total.astype(jnp.bfloat16)  17.6 us
    ppermute x4, waiting for transfers between devices, scatter_start(): first_top = lax.ppermute(parts[1][:half].astype(low), 'expert', across)  17.1 us
    ppermute x4, waiting for transfers between devices, step_down(): return lax.ppermute(values, 'batch', shift_moves(3))  15.6 us
  transfers between devices with their start and end apart: 74, of which 40 were waited for; matrix products, arithmetic and copies ran while one was open for 13% of the time, Pallas kernels for 35%

profile of v7, /device:TPU:0, one launch (start us, length us, event | category | flops | bytes accessed | tf_op | source)
XLA Modules:
  0.0 555.0 jit_solution(2965355265326154567)
XLA Ops:
  29.7 7.4 %collective-permute-done.1 = bf16[48,4224]{1,0:T(8,128)(2,1)} collective-permute-done((bf16[48,4224]{1,0:T(8,128)(2,1)}, bf16[48,4224]{1,0:T(8,128)(2,1)}, u32[]{:S(2)}, u32[]{:S(2)}) %collective-permute-start.1) | collective-permute-done | bytes 405536 | tf_op jit(solution)/shard_map/ppermute | solution.py:938
  45.4 10.9 %collective-permute-done.2 = bf16[48,4224]{1,0:T(8,128)(2,1)S(1)} collective-permute-done((bf16[48,4224]{1,0:T(8,128)(2,1)}, bf16[48,4224]{1,0:T(8,128)(2,1)S(1)}, u32[]{:S(2)}, u32[]{:S(2)}) %collective-permute-start.2) | collective-permute-done | bytes 405536 | tf_op jit(solution)/shard_map/ppermute | solution.py:934
  63.2 19.6 %collective-permute-done.3.refs_1_ = bf16[4,48,2688]{2,1,0:T(8,128)(2,1)} collective-permute-done((bf16[4,48,2688]{2,1,0:T(8,128)(2,1)S(1)}, bf16[4,48,2688]{2,1,0:T(8,128)(2,1)}, u32[]{:S(2)}, u32[]{:S(2)}) %collective-permute-start.3) | collective-permute-done | bytes 1032224 | tf_op jit(solution)/shard_map/ppermute | solution.py:818
  106.3 8.2 %enter.1 = (bf16[256,1536]{1,0:T(8,128)(2,1)}, bf16[256,1536]{1,0:T(8,128)(2,1)}, bf16[256,1024]{1,0:T(8,128)(2,1)}, f32[128,1536]{1,0:T(8,128)}) custom-call(s32[8,4]{1,0:T(8,128)} %concatenate.91.spots, bf16[256,1536]{1,0:T(8,128)(2,1)} %bitcast.177, f32[256,128]{1,0:T(8,128)} %copy.56.cosine, f32[256,128]{1,0:T(8,128)} %copy.57.sine, ...), custom_call_target="tpu_custom_call" | custom-call | flops 1 | bytes 1 | tf_op jit(solution)/shard_map/enter/pallas_call | solution.py:137
  119.9 10.5 %collective-permute-done.13 = bf16[256,1024]{1,0:T(8,128)(2,1)S(1)} collective-permute-done((bf16[256,1024]{1,0:T(8,128)(2,1)}, bf16[256,1024]{1,0:T(8,128)(2,1)S(1)}, u32[]{:S(2)}, u32[]{:S(2)}) %collective-permute-start.13) | collective-permute-done | bytes 524320 | tf_op jit(solution)/shard_map/ppermute | solution.py:818
  145.1 13.8 %attend.1 = (bf16[256,1536]{1,0:T(8,128)(2,1)}, f32[256,128]{1,0:T(8,128)}) custom-call(bf16[256,1536]{1,0:T(8,128)(2,1)} %get-tuple-element.84.query, bf16[768,1024]{1,0:T(8,128)(2,1)} %pad_maximum_fusion.3.keyval, f32[256,768]{1,0:T(8,128)} %and_select_fusion.1.bias), custom_call_target="tpu_custom_call" | custom-call | flops 1 | bytes 1 | tf_op jit(solution)/shard_map/attend/pallas_call | solution.py:203
  164.1 7.7 %project.1 = (f32[256,1536]{1,0:T(8,128)}, bf16[256,1664]{1,0:T(8,128)(2,1)}, f32[256,128]{1,0:T(8,128)}) custom-call(s32[8,4]{1,0:T(8,128)} %concatenate.91.spots, bf16[256,1536]{1,0:T(8,128)(2,1)} %get-tuple-element.90.attended, bf16[256,1536]{1,0:T(8,128)(2,1)} %bitcast.178, f32[128,1536]{1,0:T(8,128)} %get-tuple-element.91.small, ...), custom_call_target="tpu_custom_call" | custom-call | flops 1 | bytes 1 | tf_op jit(solution)/shard_map/project/pallas_call | solution.py:245
  174.6 18.7 %collective-permute-done.27.refs_1_ = bf16[256,1664]{1,0:T(8,128)(2,1)S(1)} collective-permute-done((bf16[256,1664]{1,0:T(8,128)(2,1)}, bf16[256,1664]{1,0:T(8,128)(2,1)S(1)}, u32[]{:S(2)}, u32[]{:S(2)}) %collective-permute-start.27) | collective-permute-done | bytes 852000 | tf_op jit(solution)/shard_map/ppermute | solution.py:818
  197.2 8.3 %collective-permute-done.29.refs_3_ = bf16[128,1664]{1,0:T(8,128)(2,1)} collective-permute-done((bf16[128,1664]{1,0:T(8,128)(2,1)S(1)}, bf16[128,1664]{1,0:T(8,128)(2,1)}, u32[]{:S(2)}, u32[]{:S(2)}) %collective-permute-start.29) | collective-permute-done | bytes 426016 | tf_op jit(solution)/shard_map/ppermute | solution.py:826
  206.1 62.5 %experts.2 = (bf16[8,3,3,64,1536]{4,3,2,1,0:T(8,128)(2,1)}, f32[1024,1536]{1,0:T(8,128)}, f32[1024,1664]{1,0:T(8,128)}) custom-call(s32[3]{0:T(128)} %pad_add_fusion.1.place, s32[1]{0:T(128)} %bitcast.61.first, bf16[8,3,3,64,1536]{4,3,2,1,0:T(8,128)(2,1)} %bitcast.175, bf16[256,1664]{1,0:T(8,128)(2,1)} %get-tuple-element.100.refs_0_.normed, ...), custom_call_target="tpu_custom_call" | custom-call | flops 1 | bytes 1 | tf_op jit(solution)/shard_map/experts/pallas_call | solution.py:727
  268.6 6.7 %all-gather.5.cloned.1.call-done = bf16[24,2,64,1536]{3,2,1,0:T(8,128)(2,1)} async-done(((bf16[3,2,64,1536]{3,2,1,0:T(8,128)(2,1)}), bf16[24,2,64,1536]{3,2,1,0:T(8,128)(2,1)}) %all-gather.5.cloned.1.call-update) | async-done | bytes 9437200 | tf_op jit(solution)/shard_map/all_gather | solution.py:1099
  275.3 45.5 %experts.3 = (bf16[3,2,64,1536]{3,2,1,0:T(8,128)(2,1)}, bf16[3,3,2,64,1536]{4,3,2,1,0:T(8,128)(2,1)}, bf16[2,3,2,64,1536]{4,3,2,1,0:T(8,128)(2,1)}, bf16[2,3,2,6...) custom-call(s32[3]{0:T(128)} %pad_add_fusion.1.place, s32[1]{0:T(128)} %bitcast.59.first, ...), custom_call_target="tpu_custom_call" | custom-call | flops 1 | bytes 1 | tf_op jit(solution)/shard_map/experts/pallas_call | solution.py:727
  327.0 8.2 %collective-permute-done.33 = bf16[128,1664]{1,0:T(8,128)(2,1)S(1)} collective-permute-done((bf16[128,1664]{1,0:T(8,128)(2,1)S(1)}, bf16[128,1664]{1,0:T(8,128)(2,1)S(1)}, u32[]{:S(2)}, u32[]{:S(2)}) %collective-permute-start.33) | collective-permute-done | bytes 426016 | tf_op jit(solution)/shard_map/ppermute | solution.py:845
  340.3 5.3 collective-permute-done.31
  349.4 7.8 %collective-permute-done.37 = bf16[128,1664]{1,0:T(8,128)(2,1)} collective-permute-done((bf16[128,1664]{1,0:T(8,128)(2,1)}, bf16[128,1664]{1,0:T(8,128)(2,1)}, u32[]{:S(2)}, u32[]{:S(2)}) %collective-permute-start.37) | collective-permute-done | bytes 426016 | tf_op jit(solution)/shard_map/ppermute | solution.py:858
  360.9 11.4 %turn.1 = (bf16[4,4,48,1664]{3,2,1,0:T(8,128)(2,1)}, bf16[4,4,48,1664]{3,2,1,0:T(8,128)(2,1)}, f32[256,1536]{1,0:T(8,128)}, bf16[256,1536]{1,0:T(8,128)(2,1)}) custom-call(s32[3]{0:T(128)} %pad_add_fusion.1.place, s32[8,4]{1,0:T(8,128)} %concatenate.91.spots, f32[256,1664]{1,0:T(8,128)} %pad_maximum_fusion.2.normed_grad, ...), custom_call_target="tpu_custom_call" | custom-call | flops 1 | bytes 1 | tf_op jit(solution)/shard_map/turn/pallas_call | solution.py:370
  378.8 21.3 %attend_back.1 = (bf16[256,1536]{1,0:T(8,128)(2,1)}, bf16[768,1024]{1,0:T(8,128)(2,1)}) custom-call(bf16[256,1536]{1,0:T(8,128)(2,1)} %get-tuple-element.119.head_grad, bf16[256,1536]{1,0:T(8,128)(2,1)} %get-tuple-element.84.query, bf16[768,1024]{1,0:T(8,128)(2,1)} %pad_maximum_fusion.3.keyval, f32[768,256]{1,0:T(8,128)} %and_select_fusion.bias, ...), custom_call_target="tpu_custom_call" | custom-call | flops 1 | bytes 1 | tf_op jit(solution)/shard_map/attend_back/pallas_call | solution.py:445
  408.2 5.4 collective-permute-done.40
  442.9 15.4 %leave.1 = (bf16[4,4,48,2688]{3,2,1,0:T(8,128)(2,1)}, bf16[4,4,48,2688]{3,2,1,0:T(8,128)(2,1)}, f32[256,1536]{1,0:T(8,128)}) custom-call(s32[3]{0:T(128)} %pad_add_fusion.1.place, s32[8,4]{1,0:T(8,128)} %concatenate.91.spots, f32[256,1024]{1,0:T(8,128)} %pad_maximum_fusion.4.keyval_sum, bf16[256,1536]{1,0:T(8,128)(2,1)} %get-tuple-element.129.query_grad, ...), custom_call_target="tpu_custom_call" | custom-call | flops 1 | bytes 1 | tf_op jit(solution)/shard_map/leave/pallas_call | solution.py:530
  461.4 6.5 %collective-permute-done.54.refs_3_ = bf16[3,2,64,1536]{3,2,1,0:T(8,128)(2,1)} collective-permute-done((bf16[3,2,64,1536]{3,2,1,0:T(8,128)(2,1)}, bf16[3,2,64,1536]{3,2,1,0:T(8,128)(2,1)}, u32[]{:S(2)}, u32[]{:S(2)}) %collective-permute-start.54) | collective-permute-done | bytes 1179680 | tf_op jit(solution)/shard_map/ppermute | solution.py:938
  481.7 11.8 %collective-permute-done.61 = bf16[2,48,2688]{2,1,0:T(8,128)(2,1)S(1)} collective-permute-done((bf16[2,48,2688]{2,1,0:T(8,128)(2,1)S(1)}, bf16[2,48,2688]{2,1,0:T(8,128)(2,1)S(1)}, u32[]{:S(2)}, u32[]{:S(2)}) %collective-permute-start.61) | collective-permute-done | bytes 516128 | tf_op jit(solution)/shard_map/ppermute | solution.py:845
  500.5 7.7 %collective-permute-done.58 = bf16[2,48,2688]{2,1,0:T(8,128)(2,1)S(1)} collective-permute-done((bf16[2,48,2688]{2,1,0:T(8,128)(2,1)S(1)}, bf16[2,48,2688]{2,1,0:T(8,128)(2,1)S(1)}, u32[]{:S(2)}, u32[]{:S(2)}) %collective-permute-start.58) | collective-permute-done | bytes 516128 | tf_op jit(solution)/shard_map/ppermute | solution.py:846
  512.0 5.5 collective-permute-done.62
  527.9 6.0 %unpack.1 = (f32[5,192,512]{2,1,0:T(8,128)}, f32[5,192,512]{2,1,0:T(8,128)}, f32[5,64,1536]{2,1,0:T(8,128)}) custom-call(bf16[1,3,3,64,1536]{4,3,2,1,0:T(8,128)(2,1)} %reduce-scatter.2.cloned.1.call-done.refs_0_, bf16[3,2,64,1536]{3,2,1,0:T(8,128)(2,1)} %get-tuple-element.140.refs_1_, bf16[2,3,2,64,1536]{4,3,2,1,0:T(8,128)(2,1)} %collective-permute-done.36.refs_2_, ...), custom_call_target="tpu_custom_call" | custom-call | flops 1 | bytes 1 | tf_op jit(solution)/shard_map/unpack/pallas_call | solution.py:783
  (316 shorter events, 207.9 us)
Async XLA Ops:
  7.2 198.9 %all-gather.7.cloned.1.call-start = ((), (), s32[]{:S(2)}) async-start(), calls=%async_computation.3 | async-start | bytes 15925248 | tf_op jit(solution)/shard_map/all_gather | solution.py:1099
  57.1 218.2 %all-gather.5.cloned.1.call-start = ((), (), s32[]{:S(2)}) async-start(), calls=%async_computation.2 | async-start | bytes 10616832 | tf_op jit(solution)/shard_map/all_gather | solution.py:1099
  61.3 21.5 %collective-permute-start.3 = (bf16[4,48,2688]{2,1,0:T(8,128)(2,1)S(1)}, bf16[4,48,2688]{2,1,0:T(8,128)(2,1)}, u32[]{:S(2)}, u32[]{:S(2)}) collective-permute-start(bf16[4,48,2688]{2,1,0:T(8,128)(2,1)S(1)} %pad_maximum_fusion.5.refs_0_), channel_id=1, source_target_pairs={{0,1},{1,0},{2,3},{3,2},{4,5},{5,4},{6,7},{7,6},{8,9},{9,8},{10,11... | collective-permute-start | bytes 3096584 | tf_op jit(solution)/shard_map/ppermute | solution.py:818
  83.9 383.9 %reduce-scatter.2.cloned.1.call-start = ((), (), s32[]{:S(2)}) async-start(), calls=%async_computation.1 | async-start | bytes 15925248 | tf_op jit(solution)/shard_map/reduce_scatter | solution.py:926
  134.4 28.7 %collective-permute-start.23 = (bf16[4,48,1536]{2,1,0:T(8,128)(2,1)}, bf16[4,48,1536]{2,1,0:T(8,128)(2,1)S(1)}, u32[]{:S(2)}, u32[]{:S(2)}) collective-permute-start(bf16[4,48,1536]{2,1,0:T(8,128)(2,1)} %pad_maximum_fusion.8.refs_0_), channel_id=1, source_target_pairs={{0,4},{4,0},{8,12},{12,8},{16,20},{20,16},{24,28},{28,24},{1,5},{5... | collective-permute-start | bytes 1769480 | tf_op jit(solution)/shard_map/ppermute | solution.py:930
  134.5 28.6 %collective-permute-start.24 = (bf16[4,48,1536]{2,1,0:T(8,128)(2,1)}, bf16[4,48,1536]{2,1,0:T(8,128)(2,1)}, u32[]{:S(2)}, u32[]{:S(2)}) collective-permute-start(bf16[4,48,1536]{2,1,0:T(8,128)(2,1)} %collective-permute-done.11.refs_1_), channel_id=1, source_target_pairs={{0,4},{4,0},{8,12},{12,8},{16,20},{20,16},{24,28},{28,24},{1,5},{5... | collective-permute-start | bytes 1769480 | tf_op jit(solution)/shard_map/ppermute | solution.py:930
  135.0 28.1 %collective-permute-start.25 = (bf16[4,48,1536]{2,1,0:T(8,128)(2,1)S(1)}, bf16[4,48,1536]{2,1,0:T(8,128)(2,1)}, u32[]{:S(2)}, u32[]{:S(2)}) collective-permute-start(bf16[4,48,1536]{2,1,0:T(8,128)(2,1)S(1)} %collective-permute-done.12.refs_2_), channel_id=1, source_target_pairs={{0,4},{4,0},{8,12},{12,8},{16,20},{20,16},{24,28},{28,24},{1,5},{5... | collective-permute-start | bytes 1769480 | tf_op jit(solution)/shard_map/ppermute | solution.py:930
  171.8 21.5 %collective-permute-start.27 = (bf16[256,1664]{1,0:T(8,128)(2,1)}, bf16[256,1664]{1,0:T(8,128)(2,1)S(1)}, u32[]{:S(2)}, u32[]{:S(2)}) collective-permute-start(bf16[256,1664]{1,0:T(8,128)(2,1)} %get-tuple-element.100.refs_0_.normed), channel_id=1, source_target_pairs={{0,1},{1,0},{2,3},{3,2},{4,5},{5,4},{6,7},{7,6},{8,9},{9,8},{10,11... | collective-permute-start | bytes 2555912 | tf_op jit(solution)/shard_map/ppermute | solution.py:818
  173.0 21.2 %collective-permute-start.28 = (bf16[256,1664]{1,0:T(8,128)(2,1)}, bf16[256,1664]{1,0:T(8,128)(2,1)S(1)}, u32[]{:S(2)}, u32[]{:S(2)}) collective-permute-start(bf16[256,1664]{1,0:T(8,128)(2,1)} %get-tuple-element.100.refs_0_.normed), channel_id=1, source_target_pairs={{0,2},{1,3},{2,0},{3,1},{4,6},{5,7},{6,4},{7,5},{8,10},{9,11},{10,... | collective-permute-start | bytes 2555912 | tf_op jit(solution)/shard_map/ppermute | solution.py:818
  321.1 25.4 %collective-permute-start.36 = (bf16[2,3,2,64,1536]{4,3,2,1,0:T(8,128)(2,1)}, bf16[2,3,2,64,1536]{4,3,2,1,0:T(8,128)(2,1)}, u32[]{:S(2)}, u32[]{:S(2)}) collective-permute-start(bf16[2,3,2,64,1536]{4,3,2,1,0:T(8,128)(2,1)} %get-tuple-element.111), channel_id=1, source_target_pairs={{0,4},{4,0},{8,12},{12,8},{16,20},{20,16},{24,28},{28,24},{1,5},{5... | collective-permute-start | bytes 7077896 | tf_op jit(solution)/shard_map/ppermute | solution.py:930
  349.4 55.3 %collective-permute-start.42 = (bf16[3,2,64,1536]{3,2,1,0:T(8,128)(2,1)S(1)}, bf16[3,2,64,1536]{3,2,1,0:T(8,128)(2,1)}, u32[]{:S(2)}, u32[]{:S(2)}) collective-permute-start(bf16[3,2,64,1536]{3,2,1,0:T(8,128)(2,1)S(1)} %get-tuple-element.201), channel_id=1, source_target_pairs={{0,8},{4,12},{8,16},{12,20},{16,24},{20,28},{24,0},{28,4},{1,9},{5... | collective-permute-start | bytes 3538952 | tf_op jit(solution)/shard_map/ppermute | solution.py:934
  372.3 61.9 %collective-permute-start.49 = (bf16[4,4,48,1664]{3,2,1,0:T(8,128)(2,1)}, bf16[4,4,48,1664]{3,2,1,0:T(8,128)(2,1)}, u32[]{:S(2)}, u32[]{:S(2)}) collective-permute-start(bf16[4,4,48,1664]{3,2,1,0:T(8,128)(2,1)} %get-tuple-element.127), channel_id=1, source_target_pairs={{0,4},{4,0},{8,12},{12,8},{16,20},{20,16},{24,28},{28,24},{1,5},{5... | collective-permute-start | bytes 7667720 | tf_op jit(solution)/shard_map/ppermute | solution.py:930
  375.3 32.9 %collective-permute-start.39 = (bf16[256,1536]{1,0:T(8,128)(2,1)}, bf16[256,1536]{1,0:T(8,128)(2,1)}, u32[]{:S(2)}, u32[]{:S(2)}) collective-permute-start(bf16[256,1536]{1,0:T(8,128)(2,1)} %get-tuple-element.212), channel_id=1, source_target_pairs={{0,1},{1,0},{2,3},{3,2},{4,5},{5,4},{6,7},{7,6},{8,9},{9,8},{10,11... | collective-permute-start | bytes 2359304 | tf_op jit(solution)/shard_map/ppermute | solution.py:882
  376.7 36.8 %collective-permute-start.40 = (bf16[256,1536]{1,0:T(8,128)(2,1)}, bf16[256,1536]{1,0:T(8,128)(2,1)}, u32[]{:S(2)}, u32[]{:S(2)}) collective-permute-start(bf16[256,1536]{1,0:T(8,128)(2,1)} %get-tuple-element.214), channel_id=1, source_target_pairs={{0,2},{1,3},{2,0},{3,1},{4,6},{5,7},{6,4},{7,5},{8,10},{9,11},{10,... | collective-permute-start | bytes 2359304 | tf_op jit(solution)/shard_map/ppermute | solution.py:882
  377.4 36.2 %collective-permute-start.41 = (bf16[256,1536]{1,0:T(8,128)(2,1)S(1)}, bf16[256,1536]{1,0:T(8,128)(2,1)}, u32[]{:S(2)}, u32[]{:S(2)}) collective-permute-start(bf16[256,1536]{1,0:T(8,128)(2,1)S(1)} %get-tuple-element.213), channel_id=1, source_target_pairs={{0,3},{1,2},{2,1},{3,0},{4,7},{5,6},{6,5},{7,4},{8,11},{9,10},{10,... | collective-permute-start | bytes 2359304 | tf_op jit(solution)/shard_map/ppermute | solution.py:882
  429.2 38.6 %collective-permute-start.54 = (bf16[3,2,64,1536]{3,2,1,0:T(8,128)(2,1)}, bf16[3,2,64,1536]{3,2,1,0:T(8,128)(2,1)}, u32[]{:S(2)}, u32[]{:S(2)}) collective-permute-start(bf16[3,2,64,1536]{3,2,1,0:T(8,128)(2,1)} %get-tuple-element.136), channel_id=1, source_target_pairs={{0,24},{4,28},{8,0},{12,4},{16,8},{20,12},{24,16},{28,20},{1,25},{... | collective-permute-start | bytes 3538952 | tf_op jit(solution)/shard_map/ppermute | solution.py:938
  438.7 21.6 %collective-permute-start.52 = (bf16[2,48,1664]{2,1,0:T(8,128)(2,1)S(1)}, bf16[2,48,1664]{2,1,0:T(8,128)(2,1)}, u32[]{:S(2)}, u32[]{:S(2)}) collective-permute-start(bf16[2,48,1664]{2,1,0:T(8,128)(2,1)S(1)} %get-tuple-element.234), channel_id=1, source_target_pairs={{0,2},{1,3},{2,0},{3,1},{4,6},{5,7},{6,4},{7,5},{8,10},{9,11},{10,... | collective-permute-start | bytes 958472 | tf_op jit(solution)/shard_map/ppermute | solution.py:845
  440.2 27.6 %collective-permute-start.50 = (bf16[2,48,1664]{2,1,0:T(8,128)(2,1)}, bf16[2,48,1664]{2,1,0:T(8,128)(2,1)}, u32[]{:S(2)}, u32[]{:S(2)}) collective-permute-start(bf16[2,48,1664]{2,1,0:T(8,128)(2,1)} %slice_bitcast_fusion.15), channel_id=1, source_target_pairs={{0,1},{1,0},{2,3},{3,2},{4,5},{5,4},{6,7},{7,6},{8,9},{9,8},{10,11... | collective-permute-start | bytes 958472 | tf_op jit(solution)/shard_map/ppermute | solution.py:846
  442.2 25.6 %collective-permute-start.51 = (bf16[2,48,1664]{2,1,0:T(8,128)(2,1)}, bf16[2,48,1664]{2,1,0:T(8,128)(2,1)}, u32[]{:S(2)}, u32[]{:S(2)}) collective-permute-start(bf16[2,48,1664]{2,1,0:T(8,128)(2,1)} %slice_bitcast_fusion.14), channel_id=1, source_target_pairs={{0,2},{1,3},{2,0},{3,1},{4,6},{5,7},{6,4},{7,5},{8,10},{9,11},{10,... | collective-permute-start | bytes 958472 | tf_op jit(solution)/shard_map/ppermute | solution.py:847
  468.0 51.5 %collective-permute-start.64 = (bf16[3,2,64,1536]{3,2,1,0:T(8,128)(2,1)}, bf16[3,2,64,1536]{3,2,1,0:T(8,128)(2,1)S(1)}, u32[]{:S(2)}, u32[]{:S(2)}) collective-permute-start(bf16[3,2,64,1536]{3,2,1,0:T(8,128)(2,1)} %fusion), channel_id=1, source_target_pairs={{0,8},{4,12},{8,16},{12,20},{16,24},{20,28},{24,0},{28,4},{1,9},{5... | collective-permute-start | bytes 3538952 | tf_op jit(solution)/shard_map/ppermute | solution.py:934
  472.8 24.0 %collective-permute-start.56 = (bf16[2,48,1664]{2,1,0:T(8,128)(2,1)S(1)}, bf16[2,48,1664]{2,1,0:T(8,128)(2,1)S(1)}, u32[]{:S(2)}, u32[]{:S(2)}) collective-permute-start(bf16[2,48,1664]{2,1,0:T(8,128)(2,1)S(1)} %copy-done.31), channel_id=1, source_target_pairs={{0,2},{1,3},{2,0},{3,1},{4,6},{5,7},{6,4},{7,5},{8,10},{9,11},{10,... | collective-permute-start | bytes 958472 | tf_op jit(solution)/shard_map/ppermute | solution.py:858
  474.2 23.1 %collective-permute-start.57 = (bf16[2,48,1664]{2,1,0:T(8,128)(2,1)S(1)}, bf16[2,48,1664]{2,1,0:T(8,128)(2,1)S(1)}, u32[]{:S(2)}, u32[]{:S(2)}) collective-permute-start(bf16[2,48,1664]{2,1,0:T(8,128)(2,1)S(1)} %fusion.14), channel_id=1, source_target_pairs={{0,1},{1,0},{2,3},{3,2},{4,5},{5,4},{6,7},{7,6},{8,9},{9,8},{10,11... | collective-permute-start | bytes 958472 | tf_op jit(solution)/shard_map/ppermute | solution.py:859
  497.4 21.6 %collective-permute-start.60 = (bf16[2,48,2688]{2,1,0:T(8,128)(2,1)S(1)}, bf16[2,48,2688]{2,1,0:T(8,128)(2,1)S(1)}, u32[]{:S(2)}, u32[]{:S(2)}) collective-permute-start(bf16[2,48,2688]{2,1,0:T(8,128)(2,1)S(1)} %fusion.8), channel_id=1, source_target_pairs={{0,2},{1,3},{2,0},{3,1},{4,6},{5,7},{6,4},{7,5},{8,10},{9,11},{10,... | collective-permute-start | bytes 1548296 | tf_op jit(solution)/shard_map/ppermute | solution.py:858
  509.8 25.2 %collective-permute-start.68 = (bf16[48,1664]{1,0:T(8,128)(2,1)}, bf16[48,1664]{1,0:T(8,128)(2,1)S(1)}, u32[]{:S(2)}, u32[]{:S(2)}) collective-permute-start(bf16[48,1664]{1,0:T(8,128)(2,1)} %get-tuple-element.223), channel_id=1, source_target_pairs={{0,24},{4,28},{8,0},{12,4},{16,8},{20,12},{24,16},{28,20},{1,25},{... | collective-permute-start | bytes 479240 | tf_op jit(solution)/shard_map/ppermute | solution.py:938
  (84 other events, 1184.8 us)
Sparse Core Ops, SparseCore 0:
  57.2 126.8 all-gather.6
  186.3 88.9 all-gather.4
  277.6 180.5 reduce-scatter.1

commit v8 on v7

--- a/solution.py
+++ b/solution.py
@@ -1227,10 +1227,11 @@
     if cut:
         down_term = step_down(after(down_sum, key_parts))
         received = exchange_cores(after(qkv_found[0], (totals[0], out_state[1:], down_term)))
-        out_plane = scatter_finish(out_state)
         up_term = step_up(up_sum)
-        qkv_parts = join_cores(qkv_found[1], after(received, out_plane))
-        qkv_plane = after(scatter_blocks(qkv_parts), up_term)
+        qkv_parts = join_cores(qkv_found[1], received)
+        qkv_first = scatter_start(qkv_parts)
+        out_plane = scatter_finish(after(out_state, qkv_first[1:3]))
+        qkv_plane = after(scatter_finish(qkv_first), up_term)
         out_sum = line_finish(line_start(out_plane))
         qkv_state = line_start(qkv_plane)
         near, down_term, up_term = after((near, down_term, up_term), qkv_plane)

time: 563 us -> 568 us (level)
  waiting for transfers between devices: 189 us -> 197 us
    ppermute x4, waiting for transfers between devices: 15.6 us -> 24.7 us  [step_down(): return lax.ppermute(values, 'batch', shift_moves(3))]
    ppermute x12, waiting for transfers between devices: 0.03 us -> 5.84 us  [exchange_cores(): return lax.ppermute(values, 'batch', pair_moves(8, 1))]
  transfers between devices with their start and end apart: 74 -> 74, of which waited for: 40 -> 41; matrix products, arithmetic and copies ran while one was open for 13% -> 13% of each run, Pallas kernels for 35% -> 34%
where the time goes in v8:
time: 568 us; the launch traced here: 561 us
  waiting for transfers between devices  197 us (35%)
  Pallas kernels  196 us (35%)
  starting transfers between devices  70 us (12%)
  other arithmetic  42.4 us (7%)
  local copies, waits for them, and re-layouts  39.2 us (7%)
  between operations  14.9 us (3%)
    pallas_call x2, Pallas kernels, expert_pass(): pl.pallas_call(partial(expert_kernel, cut, carried, last, len(rows), len(...  108 us
    ppermute x10, waiting for transfers between devices, gather_start(): lax.ppermute(rows, 'expert', pair_moves(4, r))  58.4 us
    ppermute x4, waiting for transfers between devices, step_down(): return lax.ppermute(values, 'batch', shift_moves(3))  24.7 us
    ppermute x8, waiting for transfers between devices, step_up(): return lax.ppermute(values, 'batch', shift_moves(1))  22.6 us
    ppermute x4, waiting for transfers between devices, scatter_start(): bottom = lax.ppermute(parts[3][half:].astype(low), 'expert', along)  22.3 us
    pallas_call x1, Pallas kernels, attend_back(): pl.pallas_call(attend_back_kernel, in_specs=[INSIDE] * 7, out_specs=[INSI...  21.3 us
    convert_element_type x14, other arithmetic, add_low(): return total.astype(jnp.bfloat16)  17.9 us
    pallas_call x1, Pallas kernels, leave(): pl.pallas_call(partial(leave_kernel, len(pieces), cut, gain_at), in_specs...  15.4 us
  transfers between devices with their start and end apart: 74, of which 41 were waited for; matrix products, arithmetic and copies ran while one was open for 13% of the time, Pallas kernels for 34%

profile of v8, /device:TPU:0, one launch (start us, length us, event | category | flops | bytes accessed | tf_op | source)
XLA Modules:
  0.0 560.6 jit_solution(13986705124637799818)
XLA Ops:
  29.7 7.4 %collective-permute-done.1 = bf16[48,4224]{1,0:T(8,128)(2,1)} collective-permute-done((bf16[48,4224]{1,0:T(8,128)(2,1)}, bf16[48,4224]{1,0:T(8,128)(2,1)}, u32[]{:S(2)}, u32[]{:S(2)}) %collective-permute-start.1) | collective-permute-done | bytes 405536 | tf_op jit(solution)/shard_map/ppermute | solution.py:938
  45.4 10.9 %collective-permute-done.2 = bf16[48,4224]{1,0:T(8,128)(2,1)S(1)} collective-permute-done((bf16[48,4224]{1,0:T(8,128)(2,1)}, bf16[48,4224]{1,0:T(8,128)(2,1)S(1)}, u32[]{:S(2)}, u32[]{:S(2)}) %collective-permute-start.2) | collective-permute-done | bytes 405536 | tf_op jit(solution)/shard_map/ppermute | solution.py:934
  63.2 19.6 %collective-permute-done.3.refs_1_ = bf16[4,48,2688]{2,1,0:T(8,128)(2,1)} collective-permute-done((bf16[4,48,2688]{2,1,0:T(8,128)(2,1)S(1)}, bf16[4,48,2688]{2,1,0:T(8,128)(2,1)}, u32[]{:S(2)}, u32[]{:S(2)}) %collective-permute-start.3) | collective-permute-done | bytes 1032224 | tf_op jit(solution)/shard_map/ppermute | solution.py:818
  106.2 8.2 %enter.1 = (bf16[256,1536]{1,0:T(8,128)(2,1)}, bf16[256,1536]{1,0:T(8,128)(2,1)}, bf16[256,1024]{1,0:T(8,128)(2,1)}, f32[128,1536]{1,0:T(8,128)}) custom-call(s32[8,4]{1,0:T(8,128)} %concatenate.91.spots, bf16[256,1536]{1,0:T(8,128)(2,1)} %bitcast.169, f32[256,128]{1,0:T(8,128)} %copy.56.cosine, f32[256,128]{1,0:T(8,128)} %copy.57.sine, ...), custom_call_target="tpu_custom_call" | custom-call | flops 1 | bytes 1 | tf_op jit(solution)/shard_map/enter/pallas_call | solution.py:137
  119.8 10.5 %collective-permute-done.13 = bf16[256,1024]{1,0:T(8,128)(2,1)S(1)} collective-permute-done((bf16[256,1024]{1,0:T(8,128)(2,1)}, bf16[256,1024]{1,0:T(8,128)(2,1)S(1)}, u32[]{:S(2)}, u32[]{:S(2)}) %collective-permute-start.13) | collective-permute-done | bytes 524320 | tf_op jit(solution)/shard_map/ppermute | solution.py:818
  145.0 13.9 %attend.1 = (bf16[256,1536]{1,0:T(8,128)(2,1)}, f32[256,128]{1,0:T(8,128)}) custom-call(bf16[256,1536]{1,0:T(8,128)(2,1)} %get-tuple-element.88.query, bf16[768,1024]{1,0:T(8,128)(2,1)} %pad_maximum_fusion.2.keyval, f32[256,768]{1,0:T(8,128)} %and_select_fusion.1.bias), custom_call_target="tpu_custom_call" | custom-call | flops 1 | bytes 1 | tf_op jit(solution)/shard_map/attend/pallas_call | solution.py:203
  164.1 7.7 %project.1 = (f32[256,1536]{1,0:T(8,128)}, bf16[256,1664]{1,0:T(8,128)(2,1)}, f32[256,128]{1,0:T(8,128)}) custom-call(s32[8,4]{1,0:T(8,128)} %concatenate.91.spots, bf16[256,1536]{1,0:T(8,128)(2,1)} %get-tuple-element.94.attended, bf16[256,1536]{1,0:T(8,128)(2,1)} %bitcast.170, f32[128,1536]{1,0:T(8,128)} %get-tuple-element.95.small, ...), custom_call_target="tpu_custom_call" | custom-call | flops 1 | bytes 1 | tf_op jit(solution)/shard_map/project/pallas_call | solution.py:245
  174.6 18.7 %collective-permute-done.27.refs_1_ = bf16[256,1664]{1,0:T(8,128)(2,1)S(1)} collective-permute-done((bf16[256,1664]{1,0:T(8,128)(2,1)}, bf16[256,1664]{1,0:T(8,128)(2,1)S(1)}, u32[]{:S(2)}, u32[]{:S(2)}) %collective-permute-start.27) | collective-permute-done | bytes 852000 | tf_op jit(solution)/shard_map/ppermute | solution.py:818
  197.1 8.3 %collective-permute-done.29.refs_3_ = bf16[128,1664]{1,0:T(8,128)(2,1)} collective-permute-done((bf16[128,1664]{1,0:T(8,128)(2,1)S(1)}, bf16[128,1664]{1,0:T(8,128)(2,1)}, u32[]{:S(2)}, u32[]{:S(2)}) %collective-permute-start.29) | collective-permute-done | bytes 426016 | tf_op jit(solution)/shard_map/ppermute | solution.py:826
  206.1 62.5 %experts.2 = (bf16[8,3,3,64,1536]{4,3,2,1,0:T(8,128)(2,1)}, f32[1024,1536]{1,0:T(8,128)}, f32[1024,1664]{1,0:T(8,128)}) custom-call(s32[3]{0:T(128)} %pad_add_fusion.1.place, s32[1]{0:T(128)} %bitcast.61.first, bf16[8,3,3,64,1536]{4,3,2,1,0:T(8,128)(2,1)} %bitcast.167, bf16[256,1664]{1,0:T(8,128)(2,1)} %get-tuple-element.104.refs_0_.normed, ...), custom_call_target="tpu_custom_call" | custom-call | flops 1 | bytes 1 | tf_op jit(solution)/shard_map/experts/pallas_call | solution.py:727
  268.6 6.7 %all-gather.5.cloned.1.call-done = bf16[24,2,64,1536]{3,2,1,0:T(8,128)(2,1)} async-done(((bf16[3,2,64,1536]{3,2,1,0:T(8,128)(2,1)}), bf16[24,2,64,1536]{3,2,1,0:T(8,128)(2,1)}) %all-gather.5.cloned.1.call-update) | async-done | bytes 9437200 | tf_op jit(solution)/shard_map/all_gather | solution.py:1099
  275.3 45.6 %experts.3 = (bf16[3,2,64,1536]{3,2,1,0:T(8,128)(2,1)}, bf16[3,3,2,64,1536]{4,3,2,1,0:T(8,128)(2,1)}, bf16[2,3,2,64,1536]{4,3,2,1,0:T(8,128)(2,1)}, bf16[2,3,2,6...) custom-call(s32[3]{0:T(128)} %pad_add_fusion.1.place, s32[1]{0:T(128)} %bitcast.59.first, ...), custom_call_target="tpu_custom_call" | custom-call | flops 1 | bytes 1 | tf_op jit(solution)/shard_map/experts/pallas_call | solution.py:727
  327.0 8.2 %collective-permute-done.33 = bf16[128,1664]{1,0:T(8,128)(2,1)S(1)} collective-permute-done((bf16[128,1664]{1,0:T(8,128)(2,1)S(1)}, bf16[128,1664]{1,0:T(8,128)(2,1)S(1)}, u32[]{:S(2)}, u32[]{:S(2)}) %collective-permute-start.33) | collective-permute-done | bytes 426016 | tf_op jit(solution)/shard_map/ppermute | solution.py:845
  340.3 5.3 collective-permute-done.31
  349.5 7.8 %collective-permute-done.37 = bf16[128,1664]{1,0:T(8,128)(2,1)} collective-permute-done((bf16[128,1664]{1,0:T(8,128)(2,1)}, bf16[128,1664]{1,0:T(8,128)(2,1)}, u32[]{:S(2)}, u32[]{:S(2)}) %collective-permute-start.37) | collective-permute-done | bytes 426016 | tf_op jit(solution)/shard_map/ppermute | solution.py:858
  366.9 11.5 %turn.1 = (bf16[4,4,48,1664]{3,2,1,0:T(8,128)(2,1)}, bf16[4,4,48,1664]{3,2,1,0:T(8,128)(2,1)}, f32[256,1536]{1,0:T(8,128)}, bf16[256,1536]{1,0:T(8,128)(2,1)}) custom-call(s32[3]{0:T(128)} %pad_add_fusion.1.place, s32[8,4]{1,0:T(8,128)} %concatenate.91.spots, f32[256,1664]{1,0:T(8,128)} %pad_maximum_fusion.1.normed_grad, ...), custom_call_target="tpu_custom_call" | custom-call | flops 1 | bytes 1 | tf_op jit(solution)/shard_map/turn/pallas_call | solution.py:370
  378.4 21.3 %attend_back.1 = (bf16[256,1536]{1,0:T(8,128)(2,1)}, bf16[768,1024]{1,0:T(8,128)(2,1)}) custom-call(bf16[256,1536]{1,0:T(8,128)(2,1)} %get-tuple-element.123.head_grad, bf16[256,1536]{1,0:T(8,128)(2,1)} %get-tuple-element.88.query, bf16[768,1024]{1,0:T(8,128)(2,1)} %pad_maximum_fusion.2.keyval, f32[768,256]{1,0:T(8,128)} %and_select_fusion.bias, ...), custom_call_target="tpu_custom_call" | custom-call | flops 1 | bytes 1 | tf_op jit(solution)/shard_map/attend_back/pallas_call | solution.py:445
  412.5 5.0 collective-permute-done.46
  435.3 15.4 %leave.1 = (bf16[4,4,48,2688]{3,2,1,0:T(8,128)(2,1)}, bf16[4,4,48,2688]{3,2,1,0:T(8,128)(2,1)}, f32[256,1536]{1,0:T(8,128)}) custom-call(s32[3]{0:T(128)} %pad_add_fusion.1.place, s32[8,4]{1,0:T(8,128)} %concatenate.91.spots, f32[256,1024]{1,0:T(8,128)} %pad_maximum_fusion.3.keyval_sum, bf16[256,1536]{1,0:T(8,128)(2,1)} %get-tuple-element.133.query_grad, ...), custom_call_target="tpu_custom_call" | custom-call | flops 1 | bytes 1 | tf_op jit(solution)/shard_map/leave/pallas_call | solution.py:530
  452.8 15.1 %collective-permute-done.54.refs_3_ = bf16[3,2,64,1536]{3,2,1,0:T(8,128)(2,1)} collective-permute-done((bf16[3,2,64,1536]{3,2,1,0:T(8,128)(2,1)}, bf16[3,2,64,1536]{3,2,1,0:T(8,128)(2,1)}, u32[]{:S(2)}, u32[]{:S(2)}) %collective-permute-start.54) | collective-permute-done | bytes 1179680 | tf_op jit(solution)/shard_map/ppermute | solution.py:938
  469.5 5.8 %collective-permute-done.55 = bf16[4,4,48,2688]{3,2,1,0:T(8,128)(2,1)} collective-permute-done((bf16[4,4,48,2688]{3,2,1,0:T(8,128)(2,1)}, bf16[4,4,48,2688]{3,2,1,0:T(8,128)(2,1)}, u32[]{:S(2)}, u32[]{:S(2)}) %collective-permute-start.55) | collective-permute-done | bytes 4128800 | tf_op jit(solution)/shard_map/ppermute | solution.py:930
  487.3 7.1 %collective-permute-done.56 = bf16[2,48,2688]{2,1,0:T(8,128)(2,1)S(1)} collective-permute-done((bf16[2,48,2688]{2,1,0:T(8,128)(2,1)S(1)}, bf16[2,48,2688]{2,1,0:T(8,128)(2,1)S(1)}, u32[]{:S(2)}, u32[]{:S(2)}) %collective-permute-start.56) | collective-permute-done | bytes 516128 | tf_op jit(solution)/shard_map/ppermute | solution.py:846
  498.0 9.0 %collective-permute-done.59 = bf16[2,48,2688]{2,1,0:T(8,128)(2,1)S(1)} collective-permute-done((bf16[2,48,2688]{2,1,0:T(8,128)(2,1)S(1)}, bf16[2,48,2688]{2,1,0:T(8,128)(2,1)S(1)}, u32[]{:S(2)}, u32[]{:S(2)}) %collective-permute-start.59) | collective-permute-done | bytes 516128 | tf_op jit(solution)/shard_map/ppermute | solution.py:845
  532.8 6.0 %unpack.1 = (f32[5,192,512]{2,1,0:T(8,128)}, f32[5,192,512]{2,1,0:T(8,128)}, f32[5,64,1536]{2,1,0:T(8,128)}) custom-call(bf16[1,3,3,64,1536]{4,3,2,1,0:T(8,128)(2,1)} %reduce-scatter.2.cloned.1.call-done.refs_0_, bf16[3,2,64,1536]{3,2,1,0:T(8,128)(2,1)} %get-tuple-element.143.refs_1_, bf16[2,3,2,64,1536]{4,3,2,1,0:T(8,128)(2,1)} %collective-permute-done.36.refs_2_, ...), custom_call_target="tpu_custom_call" | custom-call | flops 1 | bytes 1 | tf_op jit(solution)/shard_map/unpack/pallas_call | solution.py:783
  (308 shorter events, 208.3 us)
Async XLA Ops:
  7.2 198.8 %all-gather.7.cloned.1.call-start = ((), (), s32[]{:S(2)}) async-start(), calls=%async_computation.3 | async-start | bytes 15925248 | tf_op jit(solution)/shard_map/all_gather | solution.py:1099
  57.1 218.2 %all-gather.5.cloned.1.call-start = ((), (), s32[]{:S(2)}) async-start(), calls=%async_computation.2 | async-start | bytes 10616832 | tf_op jit(solution)/shard_map/all_gather | solution.py:1099
  61.3 21.5 %collective-permute-start.3 = (bf16[4,48,2688]{2,1,0:T(8,128)(2,1)S(1)}, bf16[4,48,2688]{2,1,0:T(8,128)(2,1)}, u32[]{:S(2)}, u32[]{:S(2)}) collective-permute-start(bf16[4,48,2688]{2,1,0:T(8,128)(2,1)S(1)} %pad_maximum_fusion.4.refs_0_), channel_id=1, source_target_pairs={{0,1},{1,0},{2,3},{3,2},{4,5},{5,4},{6,7},{7,6},{8,9},{9,8},{10,11... | collective-permute-start | bytes 3096584 | tf_op jit(solution)/shard_map/ppermute | solution.py:818
  62.7 21.2 %collective-permute-start.4 = (bf16[4,48,2688]{2,1,0:T(8,128)(2,1)S(1)}, bf16[4,48,2688]{2,1,0:T(8,128)(2,1)}, u32[]{:S(2)}, u32[]{:S(2)}) collective-permute-start(bf16[4,48,2688]{2,1,0:T(8,128)(2,1)S(1)} %pad_maximum_fusion.4.refs_0_), channel_id=1, source_target_pairs={{0,2},{1,3},{2,0},{3,1},{4,6},{5,7},{6,4},{7,5},{8,10},{9,11},{10,... | collective-permute-start | bytes 3096584 | tf_op jit(solution)/shard_map/ppermute | solution.py:818
  83.9 383.9 %reduce-scatter.2.cloned.1.call-start = ((), (), s32[]{:S(2)}) async-start(), calls=%async_computation.1 | async-start | bytes 15925248 | tf_op jit(solution)/shard_map/reduce_scatter | solution.py:926
  134.3 28.7 %collective-permute-start.23 = (bf16[4,48,1536]{2,1,0:T(8,128)(2,1)}, bf16[4,48,1536]{2,1,0:T(8,128)(2,1)S(1)}, u32[]{:S(2)}, u32[]{:S(2)}) collective-permute-start(bf16[4,48,1536]{2,1,0:T(8,128)(2,1)} %pad_maximum_fusion.7.refs_0_), channel_id=1, source_target_pairs={{0,4},{4,0},{8,12},{12,8},{16,20},{20,16},{24,28},{28,24},{1,5},{5... | collective-permute-start | bytes 1769480 | tf_op jit(solution)/shard_map/ppermute | solution.py:930
  134.3 28.7 %collective-permute-start.24 = (bf16[4,48,1536]{2,1,0:T(8,128)(2,1)}, bf16[4,48,1536]{2,1,0:T(8,128)(2,1)}, u32[]{:S(2)}, u32[]{:S(2)}) collective-permute-start(bf16[4,48,1536]{2,1,0:T(8,128)(2,1)} %collective-permute-done.11.refs_1_), channel_id=1, source_target_pairs={{0,4},{4,0},{8,12},{12,8},{16,20},{20,16},{24,28},{28,24},{1,5},{5... | collective-permute-start | bytes 1769480 | tf_op jit(solution)/shard_map/ppermute | solution.py:930
  134.8 28.2 %collective-permute-start.25 = (bf16[4,48,1536]{2,1,0:T(8,128)(2,1)S(1)}, bf16[4,48,1536]{2,1,0:T(8,128)(2,1)}, u32[]{:S(2)}, u32[]{:S(2)}) collective-permute-start(bf16[4,48,1536]{2,1,0:T(8,128)(2,1)S(1)} %collective-permute-done.12.refs_2_), channel_id=1, source_target_pairs={{0,4},{4,0},{8,12},{12,8},{16,20},{20,16},{24,28},{28,24},{1,5},{5... | collective-permute-start | bytes 1769480 | tf_op jit(solution)/shard_map/ppermute | solution.py:930
  171.8 21.5 %collective-permute-start.27 = (bf16[256,1664]{1,0:T(8,128)(2,1)}, bf16[256,1664]{1,0:T(8,128)(2,1)S(1)}, u32[]{:S(2)}, u32[]{:S(2)}) collective-permute-start(bf16[256,1664]{1,0:T(8,128)(2,1)} %get-tuple-element.104.refs_0_.normed), channel_id=1, source_target_pairs={{0,1},{1,0},{2,3},{3,2},{4,5},{5,4},{6,7},{7,6},{8,9},{9,8},{10,11... | collective-permute-start | bytes 2555912 | tf_op jit(solution)/shard_map/ppermute | solution.py:818
  173.0 21.2 %collective-permute-start.28 = (bf16[256,1664]{1,0:T(8,128)(2,1)}, bf16[256,1664]{1,0:T(8,128)(2,1)S(1)}, u32[]{:S(2)}, u32[]{:S(2)}) collective-permute-start(bf16[256,1664]{1,0:T(8,128)(2,1)} %get-tuple-element.104.refs_0_.normed), channel_id=1, source_target_pairs={{0,2},{1,3},{2,0},{3,1},{4,6},{5,7},{6,4},{7,5},{8,10},{9,11},{10,... | collective-permute-start | bytes 2555912 | tf_op jit(solution)/shard_map/ppermute | solution.py:818
  321.2 25.4 %collective-permute-start.36 = (bf16[2,3,2,64,1536]{4,3,2,1,0:T(8,128)(2,1)}, bf16[2,3,2,64,1536]{4,3,2,1,0:T(8,128)(2,1)}, u32[]{:S(2)}, u32[]{:S(2)}) collective-permute-start(bf16[2,3,2,64,1536]{4,3,2,1,0:T(8,128)(2,1)} %get-tuple-element.115), channel_id=1, source_target_pairs={{0,4},{4,0},{8,12},{12,8},{16,20},{20,16},{24,28},{28,24},{1,5},{5... | collective-permute-start | bytes 7077896 | tf_op jit(solution)/shard_map/ppermute | solution.py:930
  349.5 55.2 %collective-permute-start.42 = (bf16[3,2,64,1536]{3,2,1,0:T(8,128)(2,1)S(1)}, bf16[3,2,64,1536]{3,2,1,0:T(8,128)(2,1)}, u32[]{:S(2)}, u32[]{:S(2)}) collective-permute-start(bf16[3,2,64,1536]{3,2,1,0:T(8,128)(2,1)S(1)} %get-tuple-element.209), channel_id=1, source_target_pairs={{0,8},{4,12},{8,16},{12,20},{16,24},{20,28},{24,0},{28,4},{1,9},{5... | collective-permute-start | bytes 3538952 | tf_op jit(solution)/shard_map/ppermute | solution.py:934
  363.4 44.8 %collective-permute-start.39 = (bf16[256,1536]{1,0:T(8,128)(2,1)}, bf16[256,1536]{1,0:T(8,128)(2,1)}, u32[]{:S(2)}, u32[]{:S(2)}) collective-permute-start(bf16[256,1536]{1,0:T(8,128)(2,1)} %get-tuple-element.220), channel_id=1, source_target_pairs={{0,1},{1,0},{2,3},{3,2},{4,5},{5,4},{6,7},{7,6},{8,9},{9,8},{10,11... | collective-permute-start | bytes 2359304 | tf_op jit(solution)/shard_map/ppermute | solution.py:882
  364.9 43.3 %collective-permute-start.40 = (bf16[256,1536]{1,0:T(8,128)(2,1)}, bf16[256,1536]{1,0:T(8,128)(2,1)}, u32[]{:S(2)}, u32[]{:S(2)}) collective-permute-start(bf16[256,1536]{1,0:T(8,128)(2,1)} %get-tuple-element.222), channel_id=1, source_target_pairs={{0,2},{1,3},{2,0},{3,1},{4,6},{5,7},{6,4},{7,5},{8,10},{9,11},{10,... | collective-permute-start | bytes 2359304 | tf_op jit(solution)/shard_map/ppermute | solution.py:882
  365.5 42.7 %collective-permute-start.41 = (bf16[256,1536]{1,0:T(8,128)(2,1)S(1)}, bf16[256,1536]{1,0:T(8,128)(2,1)}, u32[]{:S(2)}, u32[]{:S(2)}) collective-permute-start(bf16[256,1536]{1,0:T(8,128)(2,1)S(1)} %get-tuple-element.221), channel_id=1, source_target_pairs={{0,3},{1,2},{2,1},{3,0},{4,7},{5,6},{6,5},{7,4},{8,11},{9,10},{10,... | collective-permute-start | bytes 2359304 | tf_op jit(solution)/shard_map/ppermute | solution.py:882
  378.3 48.2 %collective-permute-start.49 = (bf16[4,4,48,1664]{3,2,1,0:T(8,128)(2,1)}, bf16[4,4,48,1664]{3,2,1,0:T(8,128)(2,1)}, u32[]{:S(2)}, u32[]{:S(2)}) collective-permute-start(bf16[4,4,48,1664]{3,2,1,0:T(8,128)(2,1)} %get-tuple-element.131), channel_id=1, source_target_pairs={{0,4},{4,0},{8,12},{12,8},{16,20},{20,16},{24,28},{28,24},{1,5},{5... | collective-permute-start | bytes 7667720 | tf_op jit(solution)/shard_map/ppermute | solution.py:930
  422.4 45.4 %collective-permute-start.54 = (bf16[3,2,64,1536]{3,2,1,0:T(8,128)(2,1)}, bf16[3,2,64,1536]{3,2,1,0:T(8,128)(2,1)}, u32[]{:S(2)}, u32[]{:S(2)}) collective-permute-start(bf16[3,2,64,1536]{3,2,1,0:T(8,128)(2,1)} %get-tuple-element.140), channel_id=1, source_target_pairs={{0,24},{4,28},{8,0},{12,4},{16,8},{20,12},{24,16},{28,20},{1,25},{... | collective-permute-start | bytes 3538952 | tf_op jit(solution)/shard_map/ppermute | solution.py:938
  429.7 20.9 %collective-permute-start.53 = (bf16[2,48,1664]{2,1,0:T(8,128)(2,1)}, bf16[2,48,1664]{2,1,0:T(8,128)(2,1)}, u32[]{:S(2)}, u32[]{:S(2)}) collective-permute-start(bf16[2,48,1664]{2,1,0:T(8,128)(2,1)} %get-tuple-element.241), channel_id=1, source_target_pairs={{0,1},{1,0},{2,3},{3,2},{4,5},{5,4},{6,7},{7,6},{8,9},{9,8},{10,11... | collective-permute-start | bytes 958472 | tf_op jit(solution)/shard_map/ppermute | solution.py:844
  433.5 34.4 %collective-permute-start.50 = (bf16[2,48,1664]{2,1,0:T(8,128)(2,1)}, bf16[2,48,1664]{2,1,0:T(8,128)(2,1)}, u32[]{:S(2)}, u32[]{:S(2)}) collective-permute-start(bf16[2,48,1664]{2,1,0:T(8,128)(2,1)} %slice_bitcast_fusion.13), channel_id=1, source_target_pairs={{0,1},{1,0},{2,3},{3,2},{4,5},{5,4},{6,7},{7,6},{8,9},{9,8},{10,11... | collective-permute-start | bytes 958472 | tf_op jit(solution)/shard_map/ppermute | solution.py:846
  434.9 32.9 %collective-permute-start.51 = (bf16[2,48,1664]{2,1,0:T(8,128)(2,1)}, bf16[2,48,1664]{2,1,0:T(8,128)(2,1)}, u32[]{:S(2)}, u32[]{:S(2)}) collective-permute-start(bf16[2,48,1664]{2,1,0:T(8,128)(2,1)} %slice_bitcast_fusion.12), channel_id=1, source_target_pairs={{0,2},{1,3},{2,0},{3,1},{4,6},{5,7},{6,4},{7,5},{8,10},{9,11},{10,... | collective-permute-start | bytes 958472 | tf_op jit(solution)/shard_map/ppermute | solution.py:847
  468.0 56.4 %collective-permute-start.62 = (bf16[3,2,64,1536]{3,2,1,0:T(8,128)(2,1)}, bf16[3,2,64,1536]{3,2,1,0:T(8,128)(2,1)S(1)}, u32[]{:S(2)}, u32[]{:S(2)}) collective-permute-start(bf16[3,2,64,1536]{3,2,1,0:T(8,128)(2,1)} %fusion), channel_id=1, source_target_pairs={{0,8},{4,12},{8,16},{12,20},{16,24},{20,28},{24,0},{28,4},{1,9},{5... | collective-permute-start | bytes 3538952 | tf_op jit(solution)/shard_map/ppermute | solution.py:934
  482.9 24.1 %collective-permute-start.59 = (bf16[2,48,2688]{2,1,0:T(8,128)(2,1)S(1)}, bf16[2,48,2688]{2,1,0:T(8,128)(2,1)S(1)}, u32[]{:S(2)}, u32[]{:S(2)}) collective-permute-start(bf16[2,48,2688]{2,1,0:T(8,128)(2,1)S(1)} %get-tuple-element.236), channel_id=1, source_target_pairs={{0,2},{1,3},{2,0},{3,1},{4,6},{5,7},{6,4},{7,5},{8,10},{9,11},{10,... | collective-permute-start | bytes 1548296 | tf_op jit(solution)/shard_map/ppermute | solution.py:845
  486.7 21.1 %collective-permute-start.57 = (bf16[2,48,2688]{2,1,0:T(8,128)(2,1)S(1)}, bf16[2,48,2688]{2,1,0:T(8,128)(2,1)S(1)}, u32[]{:S(2)}, u32[]{:S(2)}) collective-permute-start(bf16[2,48,2688]{2,1,0:T(8,128)(2,1)S(1)} %get-tuple-element.235), channel_id=1, source_target_pairs={{0,1},{1,0},{2,3},{3,2},{4,5},{5,4},{6,7},{7,6},{8,9},{9,8},{10,11... | collective-permute-start | bytes 1548296 | tf_op jit(solution)/shard_map/ppermute | solution.py:844
  517.5 22.5 %collective-permute-start.68 = (bf16[48,1664]{1,0:T(8,128)(2,1)}, bf16[48,1664]{1,0:T(8,128)(2,1)}, u32[]{:S(2)}, u32[]{:S(2)}) collective-permute-start(bf16[48,1664]{1,0:T(8,128)(2,1)} %get-tuple-element.231), channel_id=1, source_target_pairs={{0,24},{4,28},{8,0},{12,4},{16,8},{20,12},{24,16},{28,20},{1,25},{... | collective-permute-start | bytes 479240 | tf_op jit(solution)/shard_map/ppermute | solution.py:938
  (80 other events, 1132.6 us)
Sparse Core Ops, SparseCore 0:
  57.2 126.8 all-gather.6
  186.3 88.9 all-gather.4
  277.6 188.5 reduce-scatter.1
